TPU v7x, 32 devices: a whole 2x2x4 slice. The times are simulated.
32 devices in a mesh: parts: 2 (over y), view: 4 (over x, core), tile: 4 (over z).
Axes of the slice: x: 2, y: 2, z: 4, core: 2. Of those that a mesh axis runs over, the one named last changes fastest.
Arguments:
- data: float32 [8, 32, 48, 32], P(('parts', 'view'), 'tile'), parts along dimension 0, may hold values from 0.25 to 4
- labels: int32 [8, 32, 48, 32], P(('parts', 'view'), 'tile'), parts along dimension 0, may hold values from 0 to 3
- kernel: float32 [4, 32, 9], P('view'), may hold values from 0.1 to 1
- offsets: int32 [4, 32], P('view'), may hold values from -2 to 2
Outputs:
- estimate: float32 [8, 32, 48, 32], P(('parts', 'view'), 'tile'), parts along dimension 0
There are 2 independent parts, one for each index of `parts`. A program takes and returns all parts, laid end to end along the dimension named above; an argument that names none is the same for every part. Nothing has to cross between parts.
All inputs are finite; a program needn't handle non-finite values.
Results may differ from a plain program's by a relative error of at most 0.000088.
Values sent between devices are 32-bit elements; how exact they have to be, the bound alone decides.
No kernel may reach another device: no remote copies, remote signals or barrier semaphores. Data moves between devices by JAX's collectives and lax.ppermute only.
A program may use at most 64 MiB of HBM per device.

v0:
```python
import jax
import jax.numpy as jnp
from jax import lax
from jax.sharding import PartitionSpec as P

ITERS = 2
SWEEPS = 4


WEAK = 0.2
TAU = 0.15


def extended(cells, sides, width):
    for axis, dim in sides:
        count = lax.axis_size(axis)
        ends = count - 1
        head = lax.slice_in_dim(cells, 0, width, axis=dim)
        tail = lax.slice_in_dim(cells, cells.shape[dim] - width, cells.shape[dim], axis=dim)
        cells = jnp.concatenate(
            [
                lax.ppermute(tail, axis, [(i, (i + 1) % count) for i in range(ends)]),
                cells,
                lax.ppermute(head, axis, [((i + 1) % count, i) for i in range(ends)]),
            ],
            axis=dim,
        )
    return cells


def swapped(block, axis, stride):
    count = lax.axis_size(axis)
    route = []
    for low in range(count):
        high = low | 1 << stride
        if high != low and high < count:
            route += [(low, high), (high, low)]
    return lax.ppermute(block, axis, route)


def band(kernel, offsets):
    depth_cells = kernel.shape[0]
    taps = jnp.arange(kernel.shape[1], dtype=jnp.int32) - 4
    depth = jnp.arange(depth_cells, dtype=jnp.int32)
    index = jnp.clip(depth[:, None] + taps[None, :] + offsets[:, None], 0, depth_cells - 1)
    weight = kernel / jnp.sum(kernel, axis=1, keepdims=True)
    return (index, weight)


def axis_term(field, region, axis):
    count = field.shape[axis]
    upper = lax.slice_in_dim(field, 1, count, axis=axis)
    lower = lax.slice_in_dim(field, 0, count - 1, axis=axis)
    same = jnp.where(
        lax.slice_in_dim(region, 1, count, axis=axis)
        == lax.slice_in_dim(region, 0, count - 1, axis=axis),
        1.0,
        WEAK,
    )
    flux = same * (upper - lower)
    after = [(0, 0)] * 3
    before = [(0, 0)] * 3
    after[axis] = (0, 1)
    before[axis] = (1, 0)
    return jnp.pad(flux, after) - jnp.pad(flux, before)


def sweep_rows(field, region, first_row, total_rows):
    extent = field.shape[0]
    global_rows = first_row + jnp.arange(extent, dtype=jnp.int32)
    inside = ((global_rows >= 0) & (global_rows < total_rows)).astype(field.dtype)[:, None, None]
    same = jnp.where(region[1:] == region[:-1], 1.0, WEAK) * inside[1:] * inside[:-1]
    flux = same * (field[1:] - field[:-1])
    inner = field[1:-1]
    inner_labels = region[1:-1]
    total = (
        flux[1:] - flux[:-1] + axis_term(inner, inner_labels, 1) + axis_term(inner, inner_labels, 2)
    )
    return inner + TAU * total


def regroup(received, tiles):
    slab, rows, depth_cells = received.shape
    blocks = received.reshape(slab, rows, tiles, depth_cells // tiles)
    return blocks.transpose(3, 1, 2, 0).reshape(depth_cells // tiles, rows, depth_cells)


def on_device(data, labels, kernel, offsets):
    recorded = data[0]
    region = labels[0]
    index, weight = band(kernel[0], offsets[0])
    tiles = lax.axis_size("tile")
    slab, rows, depth_cells = recorded.shape
    total_rows = slab * tiles
    start = lax.axis_index("tile") * slab
    parity = lax.axis_index("view") % 2
    columns = jnp.arange(depth_cells, dtype=jnp.int32)
    matrix = jnp.sum(weight[:, :, None] * (index[:, :, None] == columns[None, None, :]), axis=1)
    label_ext = extended(region, (("tile", 0),), 4)
    current = recorded
    for step in range(ITERS):
        forward_flat = jnp.dot(
            current.reshape(-1, depth_cells), matrix.T, precision=lax.Precision.HIGHEST
        )
        field = recorded / forward_flat.reshape(current.shape)
        flat = jnp.dot(field.reshape(-1, depth_cells), matrix, precision=lax.Precision.HIGHEST)
        correction = flat.reshape(field.shape)
        turned = correction
        for repeat in range(2):
            turned = regroup(
                lax.all_to_all(
                    jnp.flip(turned, 2), "tile", split_axis=2, concat_axis=2, tiled=True
                ),
                tiles,
            )
        turned = swapped(turned, "view", 1)
        paired = jnp.sqrt(correction * turned)
        outgoing = jnp.where(parity == 0, jnp.flip(paired, 2), paired)
        rotated = regroup(
            lax.all_to_all(outgoing, "tile", split_axis=2, concat_axis=2, tiled=True), tiles
        )
        rotated = jnp.where(parity == 1, jnp.flip(rotated, 2), rotated)
        partner = swapped(rotated, "view", 0)
        current = current * jnp.sqrt(paired * partner)
        widened = extended(current, (("tile", 0),), 4)
        for sweep in range(SWEEPS):
            extent = widened.shape[0]
            widened = sweep_rows(
                widened, label_ext[sweep : sweep + extent], start - 4 + sweep, total_rows
            )
        current = widened
    return current[None]


def solution(mesh):
    placed = (
        P(("parts", "view"), "tile", None, None),
        P(("parts", "view"), "tile", None, None),
        P("view", None, None),
        P("view", None),
    )
    return jax.shard_map(
        on_device,
        mesh=mesh,
        in_specs=placed,
        out_specs=P(("parts", "view"), "tile", None, None),
        check_vma=False,
    )
```

profile of v0, /device:TPU:0, one launch (start us, length us, event | category | flops | bytes accessed | tf_op | source)
XLA Modules:
  0.0 105.1 jit_solution(9000438772449605279)
XLA Ops:
  0.0 0.8 reduce_sum.18
  0.8 1.0 copy.55
  1.9 0.6 copy-done.3
  2.6 0.1 select_reduce_fusion
  2.8 0.2 fusion
  3.1 0.3 fusion.43
  3.5 0.8 reshape.145
  4.3 6.3 %all-to-all-start = ((f32[4,1,3072]{2,1,0:T(1,128)}), f32[4,1,3072]{2,1,0:T(1,128)S(1)}, u32[]{:S(2)}, u32[]{:S(2)}) async-start(f32[4,1,3072]{2,1,0:T(1,128)} %reshape.145), calls=%async_computation | async-start | bytes 98304 | tf_op jit(solution)/shard_map/all_to_all | solution.py:111
  10.6 3.9 %collective-permute-start.4 = (s32[4,48,32]{1,2,0:T(8,128)S(1)}, s32[4,48,32]{1,2,0:T(8,128)S(1)}, u32[]{:S(2)}, u32[]{:S(2)}) collective-permute-start(s32[4,48,32]{1,2,0:T(8,128)S(1)} %get-tuple-element.31), channel_id=1, source_target_pairs={{0,1},{1,2},{2,3},{4,5},{5,6},{6,7},{8,9},{9,10},{10,11},{12,13},{... | collective-permute-start | bytes 73736 | tf_op jit(solution)/shard_map/ppermute | solution.py:22
  14.6 1.3 %collective-permute-start.5 = (s32[4,48,32]{1,2,0:T(8,128)S(1)}, s32[4,48,32]{1,2,0:T(8,128)S(1)}, u32[]{:S(2)}, u32[]{:S(2)}) collective-permute-start(s32[4,48,32]{1,2,0:T(8,128)S(1)} %get-tuple-element.32), channel_id=1, source_target_pairs={{1,0},{2,1},{3,2},{5,4},{6,5},{7,6},{9,8},{10,9},{11,10},{13,12},{... | collective-permute-start | bytes 73736 | tf_op jit(solution)/shard_map/ppermute | solution.py:24
  16.0 0.3 all-to-all-done
  16.3 0.6 broadcast.193
  16.9 0.7 reduce.1
  17.9 0.8 reshape.147
  18.6 5.4 %all-to-all-start.1 = ((f32[4,1,3072]{2,1,0:T(1,128)}), f32[4,1,3072]{2,1,0:T(1,128)S(1)}, u32[]{:S(2)}, u32[]{:S(2)}) async-start(f32[4,1,3072]{2,1,0:T(1,128)} %reshape.147), calls=%async_computation.1 | async-start | bytes 98304 | tf_op jit(solution)/shard_map/all_to_all | solution.py:111
  24.1 5.7 %all-to-all-done.1 = f32[4,1,3072]{2,1,0:T(1,128)S(1)} async-done(((f32[4,1,3072]{2,1,0:T(1,128)}), f32[4,1,3072]{2,1,0:T(1,128)S(1)}, u32[]{:S(2)}, u32[]{:S(2)}) %all-to-all-start.1) | async-done | bytes 49184 | tf_op jit(solution)/shard_map/all_to_all | solution.py:111
  29.8 0.7 reduce.2
  30.5 0.1 reshape.148
  30.7 1.6 %collective-permute-start = (f32[8,48,32]{1,2,0:T(8,128)S(1)}, f32[8,48,32]{1,2,0:T(8,128)S(1)}, u32[]{:S(2)}, u32[]{:S(2)}) collective-permute-start(f32[8,48,32]{1,2,0:T(8,128)S(1)} %bitcast.122), channel_id=1, source_target_pairs={{0,8},{8,0},{4,12},{12,4},{1,9},{9,1},{5,13},{13,5},{2,10},{10,2},... | collective-permute-start | bytes 147464 | tf_op jit(solution)/shard_map/ppermute | solution.py:38
  32.3 3.4 %collective-permute-done = f32[8,48,32]{1,2,0:T(8,128)S(1)} collective-permute-done((f32[8,48,32]{1,2,0:T(8,128)S(1)}, f32[8,48,32]{1,2,0:T(8,128)S(1)}, u32[]{:S(2)}, u32[]{:S(2)}) %collective-permute-start) | collective-permute-done | bytes 49184 | tf_op jit(solution)/shard_map/ppermute | solution.py:38
  35.9 0.8 reshape.149
  36.7 3.3 %all-to-all-start.2 = ((f32[4,1,3072]{2,1,0:T(1,128)}), f32[4,1,3072]{2,1,0:T(1,128)S(1)}, u32[]{:S(2)}, u32[]{:S(2)}) async-start(f32[4,1,3072]{2,1,0:T(1,128)} %reshape.149), calls=%async_computation.2 | async-start | bytes 98304 | tf_op jit(solution)/shard_map/all_to_all | solution.py:120
  40.0 5.7 %all-to-all-done.2 = f32[4,1,3072]{2,1,0:T(1,128)S(1)} async-done(((f32[4,1,3072]{2,1,0:T(1,128)}), f32[4,1,3072]{2,1,0:T(1,128)S(1)}, u32[]{:S(2)}, u32[]{:S(2)}) %all-to-all-start.2) | async-done | bytes 49184 | tf_op jit(solution)/shard_map/all_to_all | solution.py:120
  45.6 0.7 reduce.3
  46.7 1.3 %collective-permute-done.1 = f32[8,48,32]{1,2,0:T(8,128)S(1)} collective-permute-done((f32[8,48,32]{1,2,0:T(8,128)S(1)}, f32[8,48,32]{1,2,0:T(8,128)S(1)}, u32[]{:S(2)}, u32[]{:S(2)}) %collective-permute-start.1) | collective-permute-done | bytes 49184 | tf_op jit(solution)/shard_map/ppermute | solution.py:38
  48.0 2.7 %collective-permute-start.2 = (f32[4,48,32]{1,2,0:T(8,128)S(1)}, f32[4,48,32]{1,2,0:T(8,128)S(1)}, u32[]{:S(2)}, u32[]{:S(2)}) collective-permute-start(f32[4,48,32]{1,2,0:T(8,128)S(1)} %get-tuple-element.33), channel_id=1, source_target_pairs={{0,1},{1,2},{2,3},{4,5},{5,6},{6,7},{8,9},{9,10},{10,11},{12,13},{... | collective-permute-start | bytes 73736 | tf_op jit(solution)/shard_map/ppermute | solution.py:22
  50.8 1.3 %collective-permute-start.3 = (f32[4,48,32]{1,2,0:T(8,128)S(1)}, f32[4,48,32]{1,2,0:T(8,128)S(1)}, u32[]{:S(2)}, u32[]{:S(2)}) collective-permute-start(f32[4,48,32]{1,2,0:T(8,128)S(1)} %get-tuple-element.34), channel_id=1, source_target_pairs={{1,0},{2,1},{3,2},{5,4},{6,5},{7,6},{9,8},{10,9},{11,10},{13,12},{... | collective-permute-start | bytes 73736 | tf_op jit(solution)/shard_map/ppermute | solution.py:24
  52.1 0.5 collective-permute-done.2
  52.7 4.3 %collective-permute-done.3 = f32[4,48,32]{1,2,0:T(8,128)S(1)} collective-permute-done((f32[4,48,32]{1,2,0:T(8,128)S(1)}, f32[4,48,32]{1,2,0:T(8,128)S(1)}, u32[]{:S(2)}, u32[]{:S(2)}) %collective-permute-start.3) | collective-permute-done | bytes 24608 | tf_op jit(solution)/shard_map/ppermute | solution.py:24
  57.0 0.2 select_multiply_fusion.3
  57.3 0.1 fusion.2
  57.4 0.2 fusion.10
  57.5 0.2 select_multiply_fusion.7
  57.9 0.1 fusion.20
  58.1 0.2 select_multiply_fusion.11
  58.4 0.1 fusion.30
  58.5 0.1 select_multiply_fusion.15
  58.8 0.1 fusion.42
  58.9 0.3 convolution_divide_fusion
  59.2 0.3 fusion.45
  59.6 0.2 reshape.151
  59.8 8.1 %all_to_all.30 = f32[4,1,3072]{2,1,0:T(1,128)S(1)} all-to-all(f32[4,1,3072]{2,1,0:T(1,128)S(1)} %reshape.151), channel_id=1, replica_groups=mesh['parts'=2,'view'=4,'tile'=4] {'tile'}, dimensions={0} | all-to-all | bytes 98304 | tf_op jit(solution)/shard_map/all_to_all | solution.py:111
  67.9 0.7 reduce.4
  68.9 0.2 reshape.153
  69.0 8.1 %all_to_all.31 = f32[4,1,3072]{2,1,0:T(1,128)S(1)} all-to-all(f32[4,1,3072]{2,1,0:T(1,128)S(1)} %reshape.153), channel_id=1, replica_groups=mesh['parts'=2,'view'=4,'tile'=4] {'tile'}, dimensions={0} | all-to-all | bytes 98304 | tf_op jit(solution)/shard_map/all_to_all | solution.py:111
  77.1 0.7 reduce.5
  78.0 1.6 %collective-permute-start.6 = (f32[8,48,32]{1,2,0:T(8,128)S(1)}, f32[8,48,32]{1,2,0:T(8,128)S(1)}, u32[]{:S(2)}, u32[]{:S(2)}) collective-permute-start(f32[8,48,32]{1,2,0:T(8,128)S(1)} %bitcast.123), channel_id=1, source_target_pairs={{0,8},{8,0},{4,12},{12,4},{1,9},{9,1},{5,13},{13,5},{2,10},{10,2},... | collective-permute-start | bytes 147464 | tf_op jit(solution)/shard_map/ppermute | solution.py:38
  79.5 3.5 %collective-permute-done.6 = f32[8,48,32]{1,2,0:T(8,128)S(1)} collective-permute-done((f32[8,48,32]{1,2,0:T(8,128)S(1)}, f32[8,48,32]{1,2,0:T(8,128)S(1)}, u32[]{:S(2)}, u32[]{:S(2)}) %collective-permute-start.6) | collective-permute-done | bytes 49184 | tf_op jit(solution)/shard_map/ppermute | solution.py:38
  83.2 0.2 reshape.155
  83.3 8.1 %all_to_all.32 = f32[4,1,3072]{2,1,0:T(1,128)S(1)} all-to-all(f32[4,1,3072]{2,1,0:T(1,128)S(1)} %reshape.155), channel_id=1, replica_groups=mesh['parts'=2,'view'=4,'tile'=4] {'tile'}, dimensions={0} | all-to-all | bytes 98304 | tf_op jit(solution)/shard_map/all_to_all | solution.py:120
  91.4 0.7 reduce.6
  92.4 1.3 %collective-permute-done.7 = f32[8,48,32]{1,2,0:T(8,128)S(1)} collective-permute-done((f32[8,48,32]{1,2,0:T(8,128)S(1)}, f32[8,48,32]{1,2,0:T(8,128)S(1)}, u32[]{:S(2)}, u32[]{:S(2)}) %collective-permute-start.7) | collective-permute-done | bytes 49184 | tf_op jit(solution)/shard_map/ppermute | solution.py:38
  93.8 2.7 %collective-permute-start.8 = (f32[4,48,32]{1,2,0:T(8,128)S(1)}, f32[4,48,32]{1,2,0:T(8,128)S(1)}, u32[]{:S(2)}, u32[]{:S(2)}) collective-permute-start(f32[4,48,32]{1,2,0:T(8,128)S(1)} %get-tuple-element.29), channel_id=1, source_target_pairs={{0,1},{1,2},{2,3},{4,5},{5,6},{6,7},{8,9},{9,10},{10,11},{12,13},{... | collective-permute-start | bytes 73736 | tf_op jit(solution)/shard_map/ppermute | solution.py:22
  96.6 1.3 %collective-permute-start.9 = (f32[4,48,32]{1,2,0:T(8,128)S(1)}, f32[4,48,32]{1,2,0:T(8,128)S(1)}, u32[]{:S(2)}, u32[]{:S(2)}) collective-permute-start(f32[4,48,32]{1,2,0:T(8,128)S(1)} %get-tuple-element.30), channel_id=1, source_target_pairs={{1,0},{2,1},{3,2},{5,4},{6,5},{7,6},{9,8},{10,9},{11,10},{13,12},{... | collective-permute-start | bytes 73736 | tf_op jit(solution)/shard_map/ppermute | solution.py:24
  97.9 0.6 collective-permute-done.8
  98.4 4.3 %collective-permute-done.9 = f32[4,48,32]{1,2,0:T(8,128)S(1)} collective-permute-done((f32[4,48,32]{1,2,0:T(8,128)S(1)}, f32[4,48,32]{1,2,0:T(8,128)S(1)}, u32[]{:S(2)}, u32[]{:S(2)}) %collective-permute-start.9) | collective-permute-done | bytes 24608 | tf_op jit(solution)/shard_map/ppermute | solution.py:24
  102.7 0.1 select_multiply_fusion.2
  102.9 0.1 fusion.1
  103.1 0.2 fusion.6
  103.2 0.1 select_multiply_fusion.6
  103.5 0.1 fusion.16
  103.7 0.1 select_multiply_fusion.10
  103.9 0.1 fusion.26
  104.3 0.8 fusion.38
  (78 shorter events, 3.5 us)
Async XLA Ops:
  0.0 0.8 copy-start.2
  1.9 0.7 copy-start.3
  3.5 7.1 %copy-start = (s32[1,8,48,32]{2,3,1,0:T(8,128)S(1)}, s32[1,8,48,32]{2,3,1,0:T(8,128)}, u32[]{:S(2)}) copy-start(s32[1,8,48,32]{2,3,1,0:T(8,128)} %param.5) | copy-start | bytes 147460
  4.3 12.0 %all-to-all-start = ((f32[4,1,3072]{2,1,0:T(1,128)}), f32[4,1,3072]{2,1,0:T(1,128)S(1)}, u32[]{:S(2)}, u32[]{:S(2)}) async-start(f32[4,1,3072]{2,1,0:T(1,128)} %reshape.145), calls=%async_computation | async-start | bytes 98304 | tf_op jit(solution)/shard_map/all_to_all | solution.py:111
  10.6 41.5 %collective-permute-start.4 = (s32[4,48,32]{1,2,0:T(8,128)S(1)}, s32[4,48,32]{1,2,0:T(8,128)S(1)}, u32[]{:S(2)}, u32[]{:S(2)}) collective-permute-start(s32[4,48,32]{1,2,0:T(8,128)S(1)} %get-tuple-element.31), channel_id=1, source_target_pairs={{0,1},{1,2},{2,3},{4,5},{5,6},{6,7},{8,9},{9,10},{10,11},{12,13},{... | collective-permute-start | bytes 73736 | tf_op jit(solution)/shard_map/ppermute | solution.py:22
  14.6 37.5 %collective-permute-start.5 = (s32[4,48,32]{1,2,0:T(8,128)S(1)}, s32[4,48,32]{1,2,0:T(8,128)S(1)}, u32[]{:S(2)}, u32[]{:S(2)}) collective-permute-start(s32[4,48,32]{1,2,0:T(8,128)S(1)} %get-tuple-element.32), channel_id=1, source_target_pairs={{1,0},{2,1},{3,2},{5,4},{6,5},{7,6},{9,8},{10,9},{11,10},{13,12},{... | collective-permute-start | bytes 73736 | tf_op jit(solution)/shard_map/ppermute | solution.py:24
  18.6 11.1 %all-to-all-start.1 = ((f32[4,1,3072]{2,1,0:T(1,128)}), f32[4,1,3072]{2,1,0:T(1,128)S(1)}, u32[]{:S(2)}, u32[]{:S(2)}) async-start(f32[4,1,3072]{2,1,0:T(1,128)} %reshape.147), calls=%async_computation.1 | async-start | bytes 98304 | tf_op jit(solution)/shard_map/all_to_all | solution.py:111
  30.7 5.0 %collective-permute-start = (f32[8,48,32]{1,2,0:T(8,128)S(1)}, f32[8,48,32]{1,2,0:T(8,128)S(1)}, u32[]{:S(2)}, u32[]{:S(2)}) collective-permute-start(f32[8,48,32]{1,2,0:T(8,128)S(1)} %bitcast.122), channel_id=1, source_target_pairs={{0,8},{8,0},{4,12},{12,4},{1,9},{9,1},{5,13},{13,5},{2,10},{10,2},... | collective-permute-start | bytes 147464 | tf_op jit(solution)/shard_map/ppermute | solution.py:38
  36.7 8.9 %all-to-all-start.2 = ((f32[4,1,3072]{2,1,0:T(1,128)}), f32[4,1,3072]{2,1,0:T(1,128)S(1)}, u32[]{:S(2)}, u32[]{:S(2)}) async-start(f32[4,1,3072]{2,1,0:T(1,128)} %reshape.149), calls=%async_computation.2 | async-start | bytes 98304 | tf_op jit(solution)/shard_map/all_to_all | solution.py:120
  46.5 1.5 %copy-start.1 = (f32[1,8,48,32]{2,3,1,0:T(8,128)S(1)}, f32[1,8,48,32]{2,3,1,0:T(8,128)}, u32[]{:S(2)}) copy-start(f32[1,8,48,32]{2,3,1,0:T(8,128)} %param.4) | copy-start | bytes 147460
  46.6 1.4 %collective-permute-start.1 = (f32[8,48,32]{1,2,0:T(8,128)S(1)}, f32[8,48,32]{1,2,0:T(8,128)S(1)}, u32[]{:S(2)}, u32[]{:S(2)}) collective-permute-start(f32[8,48,32]{1,2,0:T(8,128)S(1)} %broadcast_select_fusion.3), channel_id=1, source_target_pairs={{0,4},{4,0},{8,12},{12,8},{1,5},{5,1},{9,13},{13,9},{2,6},{6,2},{1... | collective-permute-start | bytes 147464 | tf_op jit(solution)/shard_map/ppermute | solution.py:38
  48.0 4.6 %collective-permute-start.2 = (f32[4,48,32]{1,2,0:T(8,128)S(1)}, f32[4,48,32]{1,2,0:T(8,128)S(1)}, u32[]{:S(2)}, u32[]{:S(2)}) collective-permute-start(f32[4,48,32]{1,2,0:T(8,128)S(1)} %get-tuple-element.33), channel_id=1, source_target_pairs={{0,1},{1,2},{2,3},{4,5},{5,6},{6,7},{8,9},{9,10},{10,11},{12,13},{... | collective-permute-start | bytes 73736 | tf_op jit(solution)/shard_map/ppermute | solution.py:22
  50.8 6.2 %collective-permute-start.3 = (f32[4,48,32]{1,2,0:T(8,128)S(1)}, f32[4,48,32]{1,2,0:T(8,128)S(1)}, u32[]{:S(2)}, u32[]{:S(2)}) collective-permute-start(f32[4,48,32]{1,2,0:T(8,128)S(1)} %get-tuple-element.34), channel_id=1, source_target_pairs={{1,0},{2,1},{3,2},{5,4},{6,5},{7,6},{9,8},{10,9},{11,10},{13,12},{... | collective-permute-start | bytes 73736 | tf_op jit(solution)/shard_map/ppermute | solution.py:24
  78.0 5.0 %collective-permute-start.6 = (f32[8,48,32]{1,2,0:T(8,128)S(1)}, f32[8,48,32]{1,2,0:T(8,128)S(1)}, u32[]{:S(2)}, u32[]{:S(2)}) collective-permute-start(f32[8,48,32]{1,2,0:T(8,128)S(1)} %bitcast.123), channel_id=1, source_target_pairs={{0,8},{8,0},{4,12},{12,4},{1,9},{9,1},{5,13},{13,5},{2,10},{10,2},... | collective-permute-start | bytes 147464 | tf_op jit(solution)/shard_map/ppermute | solution.py:38
  92.3 1.4 %collective-permute-start.7 = (f32[8,48,32]{1,2,0:T(8,128)S(1)}, f32[8,48,32]{1,2,0:T(8,128)S(1)}, u32[]{:S(2)}, u32[]{:S(2)}) collective-permute-start(f32[8,48,32]{1,2,0:T(8,128)S(1)} %broadcast_select_fusion.2), channel_id=1, source_target_pairs={{0,4},{4,0},{8,12},{12,8},{1,5},{5,1},{9,13},{13,9},{2,6},{6,2},{1... | collective-permute-start | bytes 147464 | tf_op jit(solution)/shard_map/ppermute | solution.py:38
  93.8 4.6 %collective-permute-start.8 = (f32[4,48,32]{1,2,0:T(8,128)S(1)}, f32[4,48,32]{1,2,0:T(8,128)S(1)}, u32[]{:S(2)}, u32[]{:S(2)}) collective-permute-start(f32[4,48,32]{1,2,0:T(8,128)S(1)} %get-tuple-element.29), channel_id=1, source_target_pairs={{0,1},{1,2},{2,3},{4,5},{5,6},{6,7},{8,9},{9,10},{10,11},{12,13},{... | collective-permute-start | bytes 73736 | tf_op jit(solution)/shard_map/ppermute | solution.py:22
  96.6 6.2 %collective-permute-start.9 = (f32[4,48,32]{1,2,0:T(8,128)S(1)}, f32[4,48,32]{1,2,0:T(8,128)S(1)}, u32[]{:S(2)}, u32[]{:S(2)}) collective-permute-start(f32[4,48,32]{1,2,0:T(8,128)S(1)} %get-tuple-element.30), channel_id=1, source_target_pairs={{1,0},{2,1},{3,2},{5,4},{6,5},{7,6},{9,8},{10,9},{11,10},{13,12},{... | collective-permute-start | bytes 73736 | tf_op jit(solution)/shard_map/ppermute | solution.py:24
where the time goes:
time: 106 us; the launch traced here: 105 us
  starting transfers between devices  31.6 us (30%)
  waiting for transfers between devices  30.8 us (29%)
  blocking collectives  24.2 us (23%)
  other arithmetic  9.94 us (9%)
  local copies, waits for them, and re-layouts  6.87 us (6%)
  matrix products  1.06 us (1%)
    all_to_all x2, blocking collectives, on_device(): lax.all_to_all(jnp.flip(turned, 2), 'tile', split_axis=2, concat_axis=2,...  16.1 us
    all_to_all x2, starting transfers between devices, on_device(): lax.all_to_all(jnp.flip(turned, 2), 'tile', split_axis=2, concat_axis=2,...  11.7 us
    ppermute x4, waiting for transfers between devices, swapped(): return lax.ppermute(block, axis, route)  9.46 us
    ppermute x3, starting transfers between devices, extended(): lax.ppermute(tail, axis, [(i, (i + 1) % count) for i in range(ends)])  9.4 us
    ppermute x3, waiting for transfers between devices, extended(): lax.ppermute(head, axis, [((i + 1) % count, i) for i in range(ends)])  8.55 us
    all_to_all x1, blocking collectives, on_device(): lax.all_to_all(outgoing, 'tile', split_axis=2, concat_axis=2, tiled=True)  8.06 us
    all_to_all x2, waiting for transfers between devices, on_device(): lax.all_to_all(jnp.flip(turned, 2), 'tile', split_axis=2, concat_axis=2,...  5.97 us
    all_to_all x1, waiting for transfers between devices, on_device(): lax.all_to_all(outgoing, 'tile', split_axis=2, concat_axis=2, tiled=True)  5.65 us
  transfers between devices with their start and end apart: 13, of which 11 were waited for; matrix products, arithmetic and copies ran while one was open for 5% of the time, Pallas kernels for 0%

commit v1 on v0

--- a/solution.py
+++ b/solution.py
@@ -1,4 +1,8 @@
+import functools
+
 import jax
+import jax.experimental.pallas as pl
+import jax.experimental.pallas.tpu as pltpu
 import jax.numpy as jnp
 from jax import lax
 from jax.sharding import PartitionSpec as P
@@ -6,9 +10,12 @@
 ITERS = 2
 SWEEPS = 4
 
-
 WEAK = 0.2
 TAU = 0.15
+
+LANES = 128
+ROWS = 8
+VIEWS = 4
 
 
 def extended(cells, sides, width):
@@ -85,7 +92,7 @@
     return blocks.transpose(3, 1, 2, 0).reshape(depth_cells // tiles, rows, depth_cells)
 
 
-def on_device(data, labels, kernel, offsets):
+def by_slabs(data, labels, kernel, offsets):
     recorded = data[0]
     region = labels[0]
     index, weight = band(kernel[0], offsets[0])
@@ -96,7 +103,13 @@
     parity = lax.axis_index("view") % 2
     columns = jnp.arange(depth_cells, dtype=jnp.int32)
     matrix = jnp.sum(weight[:, :, None] * (index[:, :, None] == columns[None, None, :]), axis=1)
-    label_ext = extended(region, (("tile", 0),), 4)
+    label_ext = extended(region, (("tile", 0),), SWEEPS)
+    views = lax.axis_size("view")
+    half_turn = [
+        (v * tiles + t, (v + 2) % views * tiles + tiles - 1 - t)
+        for v in range(views)
+        for t in range(tiles)
+    ]
     current = recorded
     for step in range(ITERS):
         forward_flat = jnp.dot(
@@ -105,15 +118,7 @@
         field = recorded / forward_flat.reshape(current.shape)
         flat = jnp.dot(field.reshape(-1, depth_cells), matrix, precision=lax.Precision.HIGHEST)
         correction = flat.reshape(field.shape)
-        turned = correction
-        for repeat in range(2):
-            turned = regroup(
-                lax.all_to_all(
-                    jnp.flip(turned, 2), "tile", split_axis=2, concat_axis=2, tiled=True
-                ),
-                tiles,
-            )
-        turned = swapped(turned, "view", 1)
+        turned = jnp.flip(lax.ppermute(correction, ("view", "tile"), half_turn), (0, 2))
         paired = jnp.sqrt(correction * turned)
         outgoing = jnp.where(parity == 0, jnp.flip(paired, 2), paired)
         rotated = regroup(
@@ -122,14 +127,366 @@
         rotated = jnp.where(parity == 1, jnp.flip(rotated, 2), rotated)
         partner = swapped(rotated, "view", 0)
         current = current * jnp.sqrt(paired * partner)
-        widened = extended(current, (("tile", 0),), 4)
+        widened = extended(current, (("tile", 0),), SWEEPS)
         for sweep in range(SWEEPS):
             extent = widened.shape[0]
             widened = sweep_rows(
-                widened, label_ext[sweep : sweep + extent], start - 4 + sweep, total_rows
+                widened,
+                label_ext[sweep : sweep + extent],
+                start - SWEEPS + sweep,
+                total_rows,
             )
         current = widened
     return current[None]
+
+
+def rows_reversed():
+    v = lax.axis_index("view")
+    return lax.rem(v + 1, VIEWS) >= 2
+
+
+def depth_reversed():
+    return lax.axis_index("view") >= 2
+
+
+def own_slot(tiles):
+    t = lax.axis_index("tile")
+    return jnp.where(rows_reversed(), tiles - 1 - t, t)
+
+
+def lane_order(shape, depth_cells):
+    lane = lax.broadcasted_iota(jnp.int32, shape, 1)
+    base = lane // depth_cells * depth_cells
+    return jnp.where(depth_reversed(), base + (base + depth_cells - 1 - lane), lane)
+
+
+def pack_one(source, held, target, groups):
+    slab, rows, depth_cells = held.shape
+    turn = rows_reversed()
+    for i in range(slab):
+        held[i] = source[0, jnp.where(turn, slab - 1 - i, i)]
+    part = rows // groups
+    cells = jnp.swapaxes(held[...], 0, 1)
+    cells = jnp.concatenate([cells[g * part : (g + 1) * part] for g in range(groups)], axis=2)
+    flat = cells.reshape(part * slab, groups * depth_cells)
+    order = lane_order(flat.shape, depth_cells)
+    flat = jnp.take_along_axis(flat, order, axis=1)
+    target[...] = flat.reshape(target.shape)
+
+
+def pack_kernel(groups, data, labels, data_out, labels_out, held, held_labels):
+    pack_one(data, held, data_out, groups)
+    pack_one(labels, held_labels, labels_out, groups)
+
+
+def band_kernel(kernel, offsets, band_out):
+    depth_cells, taps = kernel.shape[1:]
+    span = band_out.shape[0]
+    turn = depth_reversed()
+    row = lax.broadcasted_iota(jnp.int32, (depth_cells, depth_cells), 0)
+    col = lax.broadcasted_iota(jnp.int32, (depth_cells, depth_cells), 1)
+    pick = col == jnp.where(turn, depth_cells - 1 - row, row)
+    shift = jnp.sum(
+        jnp.where(pick, jnp.broadcast_to(offsets[...], pick.shape), 0), axis=1, keepdims=True
+    )
+    depth = row[:, :1]
+    depth = jnp.where(turn, depth_cells - 1 - depth, depth)
+    taps_by_row = jnp.dot(
+        pick.astype(jnp.float32),
+        kernel[0],
+        precision=lax.Precision.HIGHEST,
+        preferred_element_type=jnp.float32,
+    )
+    weight = taps_by_row / jnp.sum(taps_by_row, axis=1, keepdims=True)
+    lane = lax.broadcasted_iota(jnp.int32, (depth_cells, span), 1)
+    within = lax.rem(lane, depth_cells)
+    within = jnp.where(turn, depth_cells - 1 - within, within)
+    total = jnp.zeros((depth_cells, span), jnp.float32)
+    for k in range(taps):
+        index = jnp.clip(depth + (k - 4) + shift, 0, depth_cells - 1)
+        total = total + jnp.where(index == within, weight[:, k : k + 1], 0.0)
+    for g in range(span // depth_cells):
+        mine = lane // depth_cells == g
+        band_out[g * depth_cells : (g + 1) * depth_cells, :] = jnp.where(mine, total, 0.0)
+
+
+def corrected(recorded, estimate, matrix):
+    blurred = lax.dot_general(
+        estimate,
+        matrix,
+        (((1,), (1,)), ((), ())),
+        precision=lax.Precision.HIGHEST,
+        preferred_element_type=jnp.float32,
+    )
+    return jnp.dot(
+        recorded / blurred,
+        matrix,
+        precision=lax.Precision.HIGHEST,
+        preferred_element_type=jnp.float32,
+    )
+
+
+def first_kernel(tiles, band_in, *refs):
+    blocks, (whole, correction) = refs[:tiles], refs[tiles:]
+    slot = own_slot(tiles)
+    matrix = band_in[...]
+    part, slab, lanes = blocks[0].shape
+    for k in range(tiles):
+        block = blocks[k][...]
+        at = pl.ds(pl.multiple_of((slot ^ k) * slab, slab), slab)
+        whole[:, at, :] = block
+        flat = block.reshape(part * slab, lanes)
+        correction[:, at, :] = corrected(flat, flat, matrix).reshape(block.shape)
+
+
+def edges_kernel(tiles, depth_cells, *refs):
+    blocks, (along_x, along_y, along_z, whole) = refs[:tiles], refs[tiles:]
+    slot = own_slot(tiles)
+    part, slab, lanes = blocks[0].shape
+    for k in range(tiles):
+        at = pl.ds(pl.multiple_of((slot ^ k) * slab, slab), slab)
+        whole[:, at, :] = blocks[k][...]
+    total_rows = tiles * slab
+    region = whole[...].reshape(part * total_rows, lanes)
+    row = lax.broadcasted_iota(jnp.int32, region.shape, 0)
+    lane = lax.broadcasted_iota(jnp.int32, region.shape, 1)
+
+    def weighted(upper, inside, target):
+        same = jnp.where(upper == region, TAU, TAU * WEAK)
+        target[...] = jnp.where(inside, same, 0.0).reshape(target.shape)
+
+    weighted(up_rows(region), lax.rem(row, total_rows) != total_rows - 1, along_x)
+    weighted(
+        up_second(region, total_rows, depth_cells),
+        (row < (part - 1) * total_rows) | (lane < lanes - depth_cells),
+        along_y,
+    )
+    weighted(up_depth(region), lax.rem(lane, depth_cells) != depth_cells - 1, along_z)
+
+
+def up_rows(cells):
+    return pltpu.roll(cells, cells.shape[0] - 1, 0)
+
+
+def up_depth(cells):
+    return pltpu.roll(cells, cells.shape[1] - 1, 1)
+
+
+def up_second(cells, total_rows, depth_cells):
+    first = pltpu.roll(cells[:total_rows], cells.shape[1] - depth_cells, 1)
+    return jnp.concatenate([cells[total_rows:], first], axis=0)
+
+
+def down_second(cells, total_rows, depth_cells):
+    last = pltpu.roll(cells[-total_rows:], depth_cells, 1)
+    return jnp.concatenate([last, cells[:-total_rows]], axis=0)
+
+
+def swept(cells, along_x, along_y, along_z, total_rows, depth_cells):
+    flux_x = along_x * (up_rows(cells) - cells)
+    flux_y = along_y * (up_second(cells, total_rows, depth_cells) - cells)
+    flux_z = along_z * (up_depth(cells) - cells)
+    return (
+        cells
+        + (flux_x - pltpu.roll(flux_x, 1, 0))
+        + (flux_y - down_second(flux_y, total_rows, depth_cells))
+        + (flux_z - pltpu.roll(flux_z, 1, 1))
+    )
+
+
+def exchanged(cells, depth_cells):
+    part, rows, lanes = cells.shape
+    groups = lanes // depth_cells
+    lane_group = lax.broadcasted_iota(jnp.int32, (rows, lanes), 1) // depth_cells
+    out = []
+    for first in range(0, part, groups):
+        turned = cells[first : first + groups].reshape(groups * rows, lanes).T
+        for a in range(groups):
+            plane = None
+            for b in range(groups):
+                piece = turned[b * rows : (b + 1) * rows]
+                moved = (b - a) % groups * depth_cells
+                if moved:
+                    piece = pltpu.roll(piece, moved, 1)
+                plane = piece if plane is None else jnp.where(lane_group == b, piece, plane)
+            out.append(plane)
+    return jnp.stack(out)
+
+
+def product_kernel(depth_cells, own, other, product):
+    product[...] = own[...] * exchanged(other[...], depth_cells)
+
+
+def window(ref, slot, tiles, slab, margin):
+    parts = []
+    for step in (-1, 0, 1):
+        at = lax.rem(slot + step + tiles, tiles) * slab
+        parts.append(ref[:, pl.ds(pl.multiple_of(at, slab), slab), :])
+    return jnp.concatenate(parts, axis=1)[:, slab - margin : 2 * slab + margin, :]
+
+
+def second_kernel(
+    depth_cells, band_in, recorded, product, received, along_x, along_y, along_z, estimate, correction
+):
+    part, total_rows, lanes = recorded.shape
+    flat = (part * total_rows, lanes)
+    joined = jnp.sqrt(jnp.sqrt(product[...] * received[...]))
+    cells = (recorded[...] * joined).reshape(flat)
+    edges = [ref[...].reshape(flat) for ref in (along_x, along_y, along_z)]
+    for _ in range(SWEEPS):
+        cells = swept(cells, *edges, total_rows, depth_cells)
+    estimate[...] = cells.reshape(estimate.shape)
+    correction[...] = corrected(recorded[...].reshape(flat), cells, band_in[...]).reshape(
+        correction.shape
+    )
+
+
+def windows_kernel(tiles, depth_cells, own, other, kept, sent, product):
+    product[...] = own[...] * exchanged(other[...], depth_cells)
+    slab = product.shape[1] // tiles
+    slot = own_slot(tiles)
+    kept[...] = window(product, slot, tiles, slab, SWEEPS)
+    sent[...] = window(product, tiles - 1 - slot, tiles, slab, SWEEPS)
+
+
+def near_kernel(tiles, estimate, along_x, along_y, along_z, *outs):
+    slot = own_slot(tiles)
+    slab = estimate.shape[1] // tiles
+    for ref, out in zip((estimate, along_x, along_y, along_z), outs):
+        out[...] = window(ref, slot, tiles, slab, SWEEPS)
+
+
+def last_kernel(groups, depth_cells, estimate, kept, received, along_x, along_y, along_z, out, held):
+    part, extent, lanes = estimate.shape
+    slab = extent - 2 * SWEEPS
+    flat = (part * extent, lanes)
+    joined = jnp.sqrt(jnp.sqrt(kept[...] * received[...]))
+    cells = (estimate[...] * joined).reshape(flat)
+    edges = [ref[...].reshape(flat) for ref in (along_x, along_y, along_z)]
+    for _ in range(SWEEPS):
+        cells = swept(cells, *edges, extent, depth_cells)
+    cells = cells.reshape(part, extent, lanes)[:, SWEEPS : SWEEPS + slab]
+    cells = cells.reshape(part * slab, lanes)
+    cells = jnp.take_along_axis(cells, lane_order(cells.shape, depth_cells), axis=1)
+    cells = cells.reshape(part, slab, lanes)
+    cells = jnp.concatenate(
+        [cells[:, :, g * depth_cells : (g + 1) * depth_cells] for g in range(groups)], axis=0
+    )
+    held[...] = jnp.swapaxes(cells, 0, 1)
+    turn = rows_reversed()
+    for i in range(slab):
+        out[0, i] = held[jnp.where(turn, slab - 1 - i, i)]
+
+
+def whole_views(data, labels, kernel, offsets):
+    tiles = lax.axis_size("tile")
+    _, slab, rows, depth_cells = data.shape
+    groups = LANES // depth_cells
+    part = rows // groups
+    total_rows = slab * tiles
+    extent = slab + 2 * SWEEPS
+    f32 = jnp.float32
+    block = (part, slab, LANES)
+    view = (part, total_rows, LANES)
+    near = (part, extent, LANES)
+    vmem = pl.BlockSpec(memory_space=pltpu.VMEM)
+
+    def call(body, outs, scratch, *args):
+        shapes = tuple(jax.ShapeDtypeStruct(s, d) for s, d in outs)
+        return pl.pallas_call(
+            body,
+            out_shape=shapes,
+            in_specs=[vmem] * len(args),
+            out_specs=tuple(vmem for _ in shapes),
+            scratch_shapes=scratch,
+            compiler_params=pltpu.CompilerParams(vmem_limit_bytes=32 << 20),
+        )(*args)
+
+    def gathered(own):
+        return [own] + [
+            lax.ppermute(own, "tile", [(i, i ^ k) for i in range(tiles)]) for k in range(1, tiles)
+        ]
+
+    def swap(cells, bit):
+        return lax.ppermute(cells, "view", [(i, i ^ bit) for i in range(VIEWS)])
+
+    packed, packed_labels = call(
+        functools.partial(pack_kernel, groups),
+        [(block, f32), (block, jnp.int32)],
+        [pltpu.VMEM(data.shape[1:], f32), pltpu.VMEM(data.shape[1:], jnp.int32)],
+        data,
+        labels,
+    )
+    (matrix,) = call(band_kernel, [((LANES, LANES), f32)], [], kernel, offsets)
+    blocks = gathered(packed)
+    label_blocks = gathered(packed_labels)
+    recorded, correction = call(
+        functools.partial(first_kernel, tiles), [(view, f32)] * 2, [], matrix, *blocks
+    )
+    other = swap(correction, 1)
+    (product,) = call(
+        functools.partial(product_kernel, depth_cells), [(view, f32)], [], correction, other
+    )
+    edges = call(
+        functools.partial(edges_kernel, tiles, depth_cells),
+        [(view, f32)] * 3,
+        [pltpu.VMEM(view, jnp.int32)],
+        *label_blocks,
+    )
+    received = swap(product, 2)
+    estimate, correction = call(
+        functools.partial(second_kernel, depth_cells),
+        [(view, f32)] * 2,
+        [],
+        matrix,
+        recorded,
+        product,
+        received,
+        *edges,
+    )
+    other = swap(correction, 1)
+    near_cells = call(
+        functools.partial(near_kernel, tiles), [(near, f32)] * 4, [], estimate, *edges
+    )
+    kept, sent = call(
+        functools.partial(windows_kernel, tiles, depth_cells),
+        [(near, f32)] * 2,
+        [pltpu.VMEM(view, f32)],
+        correction,
+        other,
+    )
+    received = swap(sent, 2)
+    (out,) = call(
+        functools.partial(last_kernel, groups, depth_cells),
+        [(data.shape, f32)],
+        [pltpu.VMEM(data.shape[1:], f32)],
+        near_cells[0],
+        kept,
+        received,
+        *near_cells[1:],
+    )
+    return out
+
+
+def fits_whole(shape):
+    _, slab, rows, depth_cells = shape
+    tiles = lax.axis_size("tile")
+    return (
+        lax.axis_size("view") == VIEWS
+        and ITERS == 2
+        and slab % ROWS == 0
+        and slab >= SWEEPS
+        and slab * tiles == depth_cells
+        and tiles & (tiles - 1) == 0
+        and LANES % depth_cells == 0
+        and rows % (LANES // depth_cells) ** 2 == 0
+        and (2 * SWEEPS) % ROWS == 0
+    )
+
+
+def on_device(data, labels, kernel, offsets):
+    form = whole_views if fits_whole(data.shape) else by_slabs
+    return form(data, labels, kernel, offsets)
 
 
 def solution(mesh):

time: 106 us -> 34.6 us (0.33)
  blocking collectives: 24.2 us -> 0 us
  starting transfers between devices: 31.6 us -> 12.4 us
  waiting for transfers between devices: 30.8 us -> 14.3 us
  other arithmetic: 9.94 us -> 0 us
  Pallas kernels: 0 us -> 5.63 us
  local copies, waits for them, and re-layouts: 6.87 us -> 2.03 us
  matrix products: 1.06 us -> 0 us
    all_to_all x3 -> x0, blocking collectives: 24.2 us -> none  [the longest x2 16.1 us: on_device(): lax.all_to_all(jnp.flip(turned, 2), 'tile', split_axis=2, concat_axis=2,...]
    all_to_all x3 -> x0, starting transfers between devices: 15 us -> none  [the longest x2 11.7 us: on_device(): lax.all_to_all(jnp.flip(turned, 2), 'tile', split_axis=2, concat_axis=2,...]
    all_to_all x3 -> x0, waiting for transfers between devices: 11.6 us -> none  [the longest x2 5.97 us: on_device(): lax.all_to_all(jnp.flip(turned, 2), 'tile', split_axis=2, concat_axis=2,...]
    pallas_call x0 -> x9, Pallas kernels: none -> 5.63 us  [call(): pl.pallas_call(body, out_shape=shapes, in_specs=[vmem] * len(args), out_s...]
    ppermute x10, waiting for transfers between devices: 19.1 us -> 14.3 us  [the longest x6 7.22 us: gathered(): lax.ppermute(own, 'tile', [(i, i ^ k) for i in range(tiles)])]
    all_to_all x6 -> x0, other arithmetic: 4.47 us -> none  [the longest x4 2.98 us: on_device(): lax.all_to_all(jnp.flip(turned, 2), 'tile', split_axis=2, concat_axis=2,...]
    ppermute x10, starting transfers between devices: 16.5 us -> 12.4 us  [the longest x6 10.1 us: gathered(): lax.ppermute(own, 'tile', [(i, i ^ k) for i in range(tiles)])]
    unnamed x21 -> x9, local copies, waits for them, and re-layouts: 5.07 us -> 1.26 us
  transfers between devices with their start and end apart: 13 -> 10, of which waited for: 11 -> 7; matrix products, arithmetic and copies ran while one was open for 5% -> 0% of each run, Pallas kernels for 0% -> 2%
where the time goes in v1:
time: 34.6 us; the launch traced here: 34.5 us
  waiting for transfers between devices  14.3 us (41%)
  starting transfers between devices  12.4 us (36%)
  Pallas kernels  5.63 us (16%)
  local copies, waits for them, and re-layouts  2.03 us (6%)
    ppermute x6, starting transfers between devices, gathered(): lax.ppermute(own, 'tile', [(i, i ^ k) for i in range(tiles)])  10.1 us
    ppermute x6, waiting for transfers between devices, gathered(): lax.ppermute(own, 'tile', [(i, i ^ k) for i in range(tiles)])  7.22 us
    ppermute x4, waiting for transfers between devices, swap(): return lax.ppermute(cells, 'view', [(i, i ^ bit) for i in range(VIEWS)])  7.08 us
    pallas_call x9, Pallas kernels, call(): pl.pallas_call(body, out_shape=shapes, in_specs=[vmem] * len(args), out_s...  5.63 us
    ppermute x4, starting transfers between devices, swap(): return lax.ppermute(cells, 'view', [(i, i ^ bit) for i in range(VIEWS)])  2.3 us
    unnamed x9, local copies, waits for them, and re-layouts  1.26 us
    pallas_call x1, local copies, waits for them, and re-layouts, call(): pl.pallas_call(body, out_shape=shapes, in_specs=[vmem] * len(args), out_s...  0.77 us
  transfers between devices with their start and end apart: 10, of which 7 were waited for; matrix products, arithmetic and copies ran while one was open for 0% of the time, Pallas kernels for 2%

profile of v1, /device:TPU:0, one launch (start us, length us, event | category | flops | bytes accessed | tf_op | source)
XLA Modules:
  0.0 34.5 jit_solution(9469707509450151917)
XLA Ops:
  0.0 0.0 copy-start.1
  0.0 1.0 %copy.6.data = f32[1,8,48,32]{3,2,1,0:T(8,128)S(1)} copy(f32[1,8,48,32]{2,3,1,0:T(8,128)} %param.4) | data formatting | bytes 98304 | tf_op args[0]
  1.1 0.0 copy-done.1
  1.1 0.1 copy.7.labels
  1.2 0.0 copy-start.2
  1.2 0.3 shard_map.47
  1.5 0.0 copy-start
  1.5 5.1 %collective-permute-start.2 = (f32[12,8,128]{2,1,0:T(8,128)S(1)}, f32[12,8,128]{2,1,0:T(8,128)S(1)}, u32[]{:S(2)}, u32[]{:S(2)}) collective-permute-start(f32[12,8,128]{2,1,0:T(8,128)S(1)} %get-tuple-element.20.refs_0_), channel_id=1, source_target_pairs={{0,3},{1,2},{2,1},{3,0},{4,7},{5,6},{6,5},{7,4},{8,11},{9,10},{10,... | collective-permute-start | bytes 147464 | tf_op jit(solution)/shard_map/ppermute | solution.py:407
  6.6 0.0 collective-permute-start.1
  6.6 0.6 %collective-permute-start = (f32[12,8,128]{2,1,0:T(8,128)S(1)}, f32[12,8,128]{2,1,0:T(8,128)S(1)}, u32[]{:S(2)}, u32[]{:S(2)}) collective-permute-start(f32[12,8,128]{2,1,0:T(8,128)S(1)} %get-tuple-element.20.refs_0_), channel_id=1, source_target_pairs={{0,1},{1,0},{2,3},{3,2},{4,5},{5,4},{6,7},{7,6},{8,9},{9,8},{10,11... | collective-permute-start | bytes 147464 | tf_op jit(solution)/shard_map/ppermute | solution.py:407
  7.2 0.0 copy-done.2
  7.2 0.1 copy.5.kernel
  7.3 0.0 copy-done
  7.3 0.4 %shard_map.46.band_in = f32[128,128]{1,0:T(8,128)S(1)} custom-call(f32[1,32,9]{2,1,0:T(8,128)S(1)} %copy.5.kernel, s32[1,32]{1,0:T(1,128)S(1)} %copy-done), custom_call_target="tpu_custom_call" | custom-call | tf_op jit(solution)/shard_map/pallas_call | solution.py:396
  7.7 1.1 %collective-permute-done.2.refs_3_ = f32[12,8,128]{2,1,0:T(8,128)S(1)} collective-permute-done((f32[12,8,128]{2,1,0:T(8,128)S(1)}, f32[12,8,128]{2,1,0:T(8,128)S(1)}, u32[]{:S(2)}, u32[]{:S(2)}) %collective-permute-start.2) | collective-permute-done | bytes 49184 | tf_op jit(solution)/shard_map/ppermute | solution.py:407
  8.8 2.8 %collective-permute-done.1.refs_2_ = f32[12,8,128]{2,1,0:T(8,128)S(1)} collective-permute-done((f32[12,8,128]{2,1,0:T(8,128)S(1)}, f32[12,8,128]{2,1,0:T(8,128)S(1)}, u32[]{:S(2)}, u32[]{:S(2)}) %collective-permute-start.1) | collective-permute-done | bytes 49184 | tf_op jit(solution)/shard_map/ppermute | solution.py:407
  11.6 0.0 collective-permute-done.refs_1_
  11.6 1.8 %shard_map.48 = (f32[12,32,128]{2,1,0:T(8,128)S(1)}, f32[12,32,128]{2,1,0:T(8,128)S(1)}) custom-call(f32[128,128]{1,0:T(8,128)S(1)} %shard_map.46.band_in, f32[12,8,128]{2,1,0:T(8,128)S(1)} %get-tuple-element.20.refs_0_, f32[12,8,128]{2,1,0:T(8,128)S(1)} %collective-permute-done.refs_1_, f32[12,8,128]{2,1,0:T(8,128)S(1)} %collective-permute-done.1.refs_2_, ...), custom_call_target="tpu_custom_call" | custom-call | tf_op jit(solution)/shard_map/pallas_call | solution.py:396
  13.3 0.1 collective-permute-start.3
  13.4 1.4 %collective-permute-done.3.other = f32[12,32,128]{2,1,0:T(8,128)S(1)} collective-permute-done((f32[12,32,128]{2,1,0:T(8,128)S(1)}, f32[12,32,128]{2,1,0:T(8,128)S(1)}, u32[]{:S(2)}, u32[]{:S(2)}) %collective-permute-start.3) | collective-permute-done | bytes 196640 | tf_op jit(solution)/shard_map/ppermute | solution.py:411
  14.8 0.3 shard_map.49.product
  15.2 1.6 %collective-permute-start.4 = (f32[12,32,128]{2,1,0:T(8,128)S(1)}, f32[12,32,128]{2,1,0:T(8,128)S(1)}, u32[]{:S(2)}, u32[]{:S(2)}) collective-permute-start(f32[12,32,128]{2,1,0:T(8,128)S(1)} %shard_map.49.product), channel_id=1, source_target_pairs={{0,8},{4,12},{8,0},{12,4},{1,9},{5,13},{9,1},{13,5},{2,10},{6,14},... | collective-permute-start | bytes 589832 | tf_op jit(solution)/shard_map/ppermute | solution.py:411
  16.7 2.1 %collective-permute-start.7 = (s32[12,8,128]{2,1,0:T(8,128)S(1)}, s32[12,8,128]{2,1,0:T(8,128)S(1)}, u32[]{:S(2)}, u32[]{:S(2)}) collective-permute-start(s32[12,8,128]{2,1,0:T(8,128)S(1)} %get-tuple-element.23.refs_0_), channel_id=1, source_target_pairs={{0,3},{1,2},{2,1},{3,0},{4,7},{5,6},{6,5},{7,4},{8,11},{9,10},{10,... | collective-permute-start | bytes 147464 | tf_op jit(solution)/shard_map/ppermute | solution.py:407
  18.8 0.0 collective-permute-start.6
  18.8 2.3 %collective-permute-start.5 = (s32[12,8,128]{2,1,0:T(8,128)S(1)}, s32[12,8,128]{2,1,0:T(8,128)S(1)}, u32[]{:S(2)}, u32[]{:S(2)}) collective-permute-start(s32[12,8,128]{2,1,0:T(8,128)S(1)} %get-tuple-element.23.refs_0_), channel_id=1, source_target_pairs={{0,1},{1,0},{2,3},{3,2},{4,5},{5,4},{6,7},{7,6},{8,9},{9,8},{10,11... | collective-permute-start | bytes 147464 | tf_op jit(solution)/shard_map/ppermute | solution.py:407
  21.1 1.9 %collective-permute-done.7.refs_3_ = s32[12,8,128]{2,1,0:T(8,128)S(1)} collective-permute-done((s32[12,8,128]{2,1,0:T(8,128)S(1)}, s32[12,8,128]{2,1,0:T(8,128)S(1)}, u32[]{:S(2)}, u32[]{:S(2)}) %collective-permute-start.7) | collective-permute-done | bytes 49184 | tf_op jit(solution)/shard_map/ppermute | solution.py:407
  23.0 1.5 %collective-permute-done.6.refs_2_ = s32[12,8,128]{2,1,0:T(8,128)S(1)} collective-permute-done((s32[12,8,128]{2,1,0:T(8,128)S(1)}, s32[12,8,128]{2,1,0:T(8,128)S(1)}, u32[]{:S(2)}, u32[]{:S(2)}) %collective-permute-start.6) | collective-permute-done | bytes 49184 | tf_op jit(solution)/shard_map/ppermute | solution.py:407
  24.5 0.0 collective-permute-done.5.refs_1_
  24.5 0.2 shard_map.50
  24.6 0.0 collective-permute-done.4.received
  24.6 1.5 %shard_map.51 = (f32[12,32,128]{2,1,0:T(8,128)S(1)}, f32[12,32,128]{2,1,0:T(8,128)S(1)}) custom-call(f32[128,128]{1,0:T(8,128)S(1)} %shard_map.46.band_in, f32[12,32,128]{2,1,0:T(8,128)S(1)} %get-tuple-element.21.recorded, f32[12,32,128]{2,1,0:T(8,128)S(1)} %shard_map.49.product, f32[12,32,128]{2,1,0:T(8,128)S(1)} %collective-permute-done.4.received, ...), custom_call_target="tpu_custom_call" | custom-call | tf_op jit(solution)/shard_map/pallas_call | solution.py:396
  26.2 0.1 collective-permute-start.8
  26.2 1.4 %collective-permute-done.8.other = f32[12,32,128]{2,1,0:T(8,128)S(1)} collective-permute-done((f32[12,32,128]{2,1,0:T(8,128)S(1)}, f32[12,32,128]{2,1,0:T(8,128)S(1)}, u32[]{:S(2)}, u32[]{:S(2)}) %collective-permute-start.8) | collective-permute-done | bytes 196640 | tf_op jit(solution)/shard_map/ppermute | solution.py:411
  27.7 0.3 %shard_map.53 = (f32[12,16,128]{2,1,0:T(8,128)S(1)}, f32[12,16,128]{2,1,0:T(8,128)S(1)}) custom-call(f32[12,32,128]{2,1,0:T(8,128)S(1)} %get-tuple-element.29.own, f32[12,32,128]{2,1,0:T(8,128)S(1)} %collective-permute-done.8.other), custom_call_target="tpu_custom_call" | custom-call | tf_op jit(solution)/shard_map/pallas_call | solution.py:396
  28.0 0.6 %collective-permute-start.9 = (f32[12,16,128]{2,1,0:T(8,128)S(1)}, f32[12,16,128]{2,1,0:T(8,128)S(1)}, u32[]{:S(2)}, u32[]{:S(2)}) collective-permute-start(f32[12,16,128]{2,1,0:T(8,128)S(1)} %get-tuple-element.31), channel_id=1, source_target_pairs={{0,8},{4,12},{8,0},{12,4},{1,9},{5,13},{9,1},{13,5},{2,10},{6,14},... | collective-permute-start | bytes 294920 | tf_op jit(solution)/shard_map/ppermute | solution.py:411
  28.6 0.1 shard_map.52
  28.7 4.2 %collective-permute-done.9.received = f32[12,16,128]{2,1,0:T(8,128)S(1)} collective-permute-done((f32[12,16,128]{2,1,0:T(8,128)S(1)}, f32[12,16,128]{2,1,0:T(8,128)S(1)}, u32[]{:S(2)}, u32[]{:S(2)}) %collective-permute-start.9) | collective-permute-done | bytes 98336 | tf_op jit(solution)/shard_map/ppermute | solution.py:411
  32.9 0.8 %shard_map.54 = f32[1,8,48,32]{3,2,1,0:T(8,128)S(1)} custom-call(f32[12,16,128]{2,1,0:T(8,128)S(1)} %get-tuple-element.28.estimate, f32[12,16,128]{2,1,0:T(8,128)S(1)} %get-tuple-element.30.kept, f32[12,16,128]{2,1,0:T(8,128)S(1)} %collective-permute-done.9.received, f32[12,16,128]{2,1,0:T(8,128)S(1)} %get-tuple-element.32.along_x, ...), custom_call_target="tpu_custom_call" | custom-call | tf_op jit(solution)/shard_map/pallas_call | solution.py:396
  33.7 0.8 %copy.8 = f32[1,8,48,32]{2,3,1,0:T(8,128)} copy(f32[1,8,48,32]{3,2,1,0:T(8,128)S(1)} %shard_map.54) | data formatting | bytes 98304 | tf_op jit(solution)/shard_map/pallas_call | solution.py:396
Async XLA Ops:
  0.0 1.1 %copy-start.1 = (s32[1,8,48,32]{2,3,1,0:T(8,128)S(1)}, s32[1,8,48,32]{2,3,1,0:T(8,128)}, u32[]{:S(2)}) copy-start(s32[1,8,48,32]{2,3,1,0:T(8,128)} %param.5) | copy-start | bytes 147460
  1.2 6.0 %copy-start.2 = (f32[1,32,9]{1,0,2:T(1,128)S(1)}, f32[1,32,9]{1,0,2:T(1,128)}, u32[]{:S(2)}) copy-start(f32[1,32,9]{1,0,2:T(1,128)} %param.6) | copy-start | bytes 3460
  1.5 5.8 %copy-start = (s32[1,32]{1,0:T(1,128)S(1)}, s32[1,32]{1,0:T(1,128)}, u32[]{:S(2)}) copy-start(s32[1,32]{1,0:T(1,128)} %offsets.1) | copy-start | bytes 388
  1.5 7.3 %collective-permute-start.2 = (f32[12,8,128]{2,1,0:T(8,128)S(1)}, f32[12,8,128]{2,1,0:T(8,128)S(1)}, u32[]{:S(2)}, u32[]{:S(2)}) collective-permute-start(f32[12,8,128]{2,1,0:T(8,128)S(1)} %get-tuple-element.20.refs_0_), channel_id=1, source_target_pairs={{0,3},{1,2},{2,1},{3,0},{4,7},{5,6},{6,5},{7,4},{8,11},{9,10},{10,... | collective-permute-start | bytes 147464 | tf_op jit(solution)/shard_map/ppermute | solution.py:407
  6.6 5.0 %collective-permute-start.1 = (f32[12,8,128]{2,1,0:T(8,128)S(1)}, f32[12,8,128]{2,1,0:T(8,128)S(1)}, u32[]{:S(2)}, u32[]{:S(2)}) collective-permute-start(f32[12,8,128]{2,1,0:T(8,128)S(1)} %get-tuple-element.20.refs_0_), channel_id=1, source_target_pairs={{0,2},{1,3},{2,0},{3,1},{4,6},{5,7},{6,4},{7,5},{8,10},{9,11},{10,... | collective-permute-start | bytes 147464 | tf_op jit(solution)/shard_map/ppermute | solution.py:407
  6.6 5.0 %collective-permute-start = (f32[12,8,128]{2,1,0:T(8,128)S(1)}, f32[12,8,128]{2,1,0:T(8,128)S(1)}, u32[]{:S(2)}, u32[]{:S(2)}) collective-permute-start(f32[12,8,128]{2,1,0:T(8,128)S(1)} %get-tuple-element.20.refs_0_), channel_id=1, source_target_pairs={{0,1},{1,0},{2,3},{3,2},{4,5},{5,4},{6,7},{7,6},{8,9},{9,8},{10,11... | collective-permute-start | bytes 147464 | tf_op jit(solution)/shard_map/ppermute | solution.py:407
  13.3 1.5 %collective-permute-start.3 = (f32[12,32,128]{2,1,0:T(8,128)S(1)}, f32[12,32,128]{2,1,0:T(8,128)S(1)}, u32[]{:S(2)}, u32[]{:S(2)}) collective-permute-start(f32[12,32,128]{2,1,0:T(8,128)S(1)} %get-tuple-element.22.own), channel_id=1, source_target_pairs={{0,4},{4,0},{8,12},{12,8},{1,5},{5,1},{9,13},{13,9},{2,6},{6,2},{1... | collective-permute-start | bytes 589832 | tf_op jit(solution)/shard_map/ppermute | solution.py:411
  15.2 9.4 %collective-permute-start.4 = (f32[12,32,128]{2,1,0:T(8,128)S(1)}, f32[12,32,128]{2,1,0:T(8,128)S(1)}, u32[]{:S(2)}, u32[]{:S(2)}) collective-permute-start(f32[12,32,128]{2,1,0:T(8,128)S(1)} %shard_map.49.product), channel_id=1, source_target_pairs={{0,8},{4,12},{8,0},{12,4},{1,9},{5,13},{9,1},{13,5},{2,10},{6,14},... | collective-permute-start | bytes 589832 | tf_op jit(solution)/shard_map/ppermute | solution.py:411
  16.7 6.3 %collective-permute-start.7 = (s32[12,8,128]{2,1,0:T(8,128)S(1)}, s32[12,8,128]{2,1,0:T(8,128)S(1)}, u32[]{:S(2)}, u32[]{:S(2)}) collective-permute-start(s32[12,8,128]{2,1,0:T(8,128)S(1)} %get-tuple-element.23.refs_0_), channel_id=1, source_target_pairs={{0,3},{1,2},{2,1},{3,0},{4,7},{5,6},{6,5},{7,4},{8,11},{9,10},{10,... | collective-permute-start | bytes 147464 | tf_op jit(solution)/shard_map/ppermute | solution.py:407
  18.8 5.6 %collective-permute-start.6 = (s32[12,8,128]{2,1,0:T(8,128)S(1)}, s32[12,8,128]{2,1,0:T(8,128)S(1)}, u32[]{:S(2)}, u32[]{:S(2)}) collective-permute-start(s32[12,8,128]{2,1,0:T(8,128)S(1)} %get-tuple-element.23.refs_0_), channel_id=1, source_target_pairs={{0,2},{1,3},{2,0},{3,1},{4,6},{5,7},{6,4},{7,5},{8,10},{9,11},{10,... | collective-permute-start | bytes 147464 | tf_op jit(solution)/shard_map/ppermute | solution.py:407
  18.8 5.6 %collective-permute-start.5 = (s32[12,8,128]{2,1,0:T(8,128)S(1)}, s32[12,8,128]{2,1,0:T(8,128)S(1)}, u32[]{:S(2)}, u32[]{:S(2)}) collective-permute-start(s32[12,8,128]{2,1,0:T(8,128)S(1)} %get-tuple-element.23.refs_0_), channel_id=1, source_target_pairs={{0,1},{1,0},{2,3},{3,2},{4,5},{5,4},{6,7},{7,6},{8,9},{9,8},{10,11... | collective-permute-start | bytes 147464 | tf_op jit(solution)/shard_map/ppermute | solution.py:407
  26.2 1.5 %collective-permute-start.8 = (f32[12,32,128]{2,1,0:T(8,128)S(1)}, f32[12,32,128]{2,1,0:T(8,128)S(1)}, u32[]{:S(2)}, u32[]{:S(2)}) collective-permute-start(f32[12,32,128]{2,1,0:T(8,128)S(1)} %get-tuple-element.29.own), channel_id=1, source_target_pairs={{0,4},{4,0},{8,12},{12,8},{1,5},{5,1},{9,13},{13,9},{2,6},{6,2},{1... | collective-permute-start | bytes 589832 | tf_op jit(solution)/shard_map/ppermute | solution.py:411
  28.0 4.9 %collective-permute-start.9 = (f32[12,16,128]{2,1,0:T(8,128)S(1)}, f32[12,16,128]{2,1,0:T(8,128)S(1)}, u32[]{:S(2)}, u32[]{:S(2)}) collective-permute-start(f32[12,16,128]{2,1,0:T(8,128)S(1)} %get-tuple-element.31), channel_id=1, source_target_pairs={{0,8},{4,12},{8,0},{12,4},{1,9},{5,13},{9,1},{13,5},{2,10},{6,14},... | collective-permute-start | bytes 294920 | tf_op jit(solution)/shard_map/ppermute | solution.py:411

commit v2 on v1

--- a/solution.py
+++ b/solution.py
@@ -171,17 +171,24 @@
     flat = cells.reshape(part * slab, groups * depth_cells)
     order = lane_order(flat.shape, depth_cells)
     flat = jnp.take_along_axis(flat, order, axis=1)
-    target[...] = flat.reshape(target.shape)
-
-
-def pack_kernel(groups, data, labels, data_out, labels_out, held, held_labels):
+    target[...] = flat.reshape(target.shape).astype(target.dtype)
+
+
+def pack_kernel(groups, data, labels, data_out, both_out, held, held_labels):
     pack_one(data, held, data_out, groups)
-    pack_one(labels, held_labels, labels_out, groups)
-
-
-def band_kernel(kernel, offsets, band_out):
+    part = data_out.shape[0]
+    both_out[:part] = data_out[...]
+    pack_one(labels, held_labels, both_out.at[part:], groups)
+
+
+def split(cells):
+    high = cells.astype(jnp.bfloat16)
+    return high, (cells - high.astype(jnp.float32)).astype(jnp.bfloat16)
+
+
+def band_kernel(kernel, offsets, blur_out, adjoint_out):
     depth_cells, taps = kernel.shape[1:]
-    span = band_out.shape[0]
+    span = blur_out.shape[0] // 2
     turn = depth_reversed()
     row = lax.broadcasted_iota(jnp.int32, (depth_cells, depth_cells), 0)
     col = lax.broadcasted_iota(jnp.int32, (depth_cells, depth_cells), 1)
@@ -205,47 +212,74 @@
     for k in range(taps):
         index = jnp.clip(depth + (k - 4) + shift, 0, depth_cells - 1)
         total = total + jnp.where(index == within, weight[:, k : k + 1], 0.0)
-    for g in range(span // depth_cells):
-        mine = lane // depth_cells == g
-        band_out[g * depth_cells : (g + 1) * depth_cells, :] = jnp.where(mine, total, 0.0)
-
-
-def corrected(recorded, estimate, matrix):
-    blurred = lax.dot_general(
-        estimate,
-        matrix,
-        (((1,), (1,)), ((), ())),
-        precision=lax.Precision.HIGHEST,
-        preferred_element_type=jnp.float32,
-    )
-    return jnp.dot(
-        recorded / blurred,
-        matrix,
-        precision=lax.Precision.HIGHEST,
-        preferred_element_type=jnp.float32,
-    )
-
-
-def first_kernel(tiles, band_in, *refs):
-    blocks, (whole, correction) = refs[:tiles], refs[tiles:]
+    matrix = jnp.concatenate(
+        [jnp.where(lane // depth_cells == g, total, 0.0) for g in range(span // depth_cells)], axis=0
+    )
+    for cells, out in ((matrix.T, blur_out), (matrix, adjoint_out)):
+        high, low = split(cells)
+        for half in range(2):
+            out[half * span : (half + 1) * span, :span] = high
+            out[half * span : (half + 1) * span, span:] = low
+
+
+def banded(cells, band):
+    high, low = split(cells)
+    both = jnp.dot(
+        jnp.concatenate([high, low], axis=1), band[...], preferred_element_type=jnp.float32
+    )
+    lanes = cells.shape[1]
+    return both[:, :lanes] + both[:, lanes:]
+
+
+def corrected(recorded, estimate, blur_band, adjoint_band):
+    return banded(recorded / banded(estimate, blur_band), adjoint_band)
+
+
+def first_correction(block, blur_band, adjoint_band):
+    flat = block.reshape(-1, block.shape[-1])
+    return corrected(flat, flat, blur_band, adjoint_band).reshape(block.shape)
+
+
+def place(target, slot, block):
+    slab = block.shape[1]
+    target[:, pl.ds(pl.multiple_of(slot * slab, slab), slab), :] = block
+
+
+def block_kernel(blur_band, adjoint_band, block, correction):
+    correction[...] = first_correction(block[...], blur_band, adjoint_band)
+
+
+def beside_kernel(blur_band, adjoint_band, own_both, both, correction, labels_out):
+    part = both.shape[0] // 2
+    correction[...] = first_correction(both[:part], blur_band, adjoint_band)
+    labels_out[:part] = own_both[part:]
+    labels_out[part:] = both[part:]
+
+
+def last_block_kernel(tiles, k, others, blur_band, adjoint_band, block, *refs):
+    correction = refs[-1]
     slot = own_slot(tiles)
-    matrix = band_in[...]
-    part, slab, lanes = blocks[0].shape
+    for j, ref in zip(others, refs):
+        place(correction, slot ^ j, ref[...])
+    place(correction, slot ^ k, first_correction(block[...], blur_band, adjoint_band))
+
+
+def recorded_kernel(tiles, own, both, *refs):
+    far, recorded = refs[:-1], refs[-1]
+    slot = own_slot(tiles)
+    place(recorded, slot, own[...])
+    place(recorded, slot ^ 1, both[: own.shape[0]])
+    for k, ref in enumerate(far):
+        place(recorded, slot ^ (k + 2), ref[...])
+
+
+def edges_kernel(tiles, depth_cells, near, far, along_x, along_y, along_z, whole):
+    slot = own_slot(tiles)
+    slab, lanes = near.shape[1:]
+    part = near.shape[0] // 2
     for k in range(tiles):
-        block = blocks[k][...]
-        at = pl.ds(pl.multiple_of((slot ^ k) * slab, slab), slab)
-        whole[:, at, :] = block
-        flat = block.reshape(part * slab, lanes)
-        correction[:, at, :] = corrected(flat, flat, matrix).reshape(block.shape)
-
-
-def edges_kernel(tiles, depth_cells, *refs):
-    blocks, (along_x, along_y, along_z, whole) = refs[:tiles], refs[tiles:]
-    slot = own_slot(tiles)
-    part, slab, lanes = blocks[0].shape
-    for k in range(tiles):
-        at = pl.ds(pl.multiple_of((slot ^ k) * slab, slab), slab)
-        whole[:, at, :] = blocks[k][...]
+        source = (near, far)[k // 2]
+        place(whole, slot ^ k, source[k % 2 * part : (k % 2 + 1) * part])
     total_rows = tiles * slab
     region = whole[...].reshape(part * total_rows, lanes)
     row = lax.broadcasted_iota(jnp.int32, region.shape, 0)
@@ -326,19 +360,29 @@
 
 
 def second_kernel(
-    depth_cells, band_in, recorded, product, received, along_x, along_y, along_z, estimate, correction
+    depth_cells,
+    blur_band,
+    adjoint_band,
+    recorded,
+    product,
+    received,
+    along_x,
+    along_y,
+    along_z,
+    estimate,
+    correction,
 ):
     part, total_rows, lanes = recorded.shape
     flat = (part * total_rows, lanes)
-    joined = jnp.sqrt(jnp.sqrt(product[...] * received[...]))
+    joined = lax.rsqrt(lax.rsqrt(product[...] * received[...]))
     cells = (recorded[...] * joined).reshape(flat)
     edges = [ref[...].reshape(flat) for ref in (along_x, along_y, along_z)]
     for _ in range(SWEEPS):
         cells = swept(cells, *edges, total_rows, depth_cells)
     estimate[...] = cells.reshape(estimate.shape)
-    correction[...] = corrected(recorded[...].reshape(flat), cells, band_in[...]).reshape(
-        correction.shape
-    )
+    correction[...] = corrected(
+        recorded[...].reshape(flat), cells, blur_band, adjoint_band
+    ).reshape(correction.shape)
 
 
 def windows_kernel(tiles, depth_cells, own, other, kept, sent, product):
@@ -360,7 +404,7 @@
     part, extent, lanes = estimate.shape
     slab = extent - 2 * SWEEPS
     flat = (part * extent, lanes)
-    joined = jnp.sqrt(jnp.sqrt(kept[...] * received[...]))
+    joined = lax.rsqrt(lax.rsqrt(kept[...] * received[...]))
     cells = (estimate[...] * joined).reshape(flat)
     edges = [ref[...].reshape(flat) for ref in (along_x, along_y, along_z)]
     for _ in range(SWEEPS):
@@ -402,27 +446,47 @@
             compiler_params=pltpu.CompilerParams(vmem_limit_bytes=32 << 20),
         )(*args)
 
-    def gathered(own):
-        return [own] + [
-            lax.ppermute(own, "tile", [(i, i ^ k) for i in range(tiles)]) for k in range(1, tiles)
-        ]
+    def across(cells, k):
+        return lax.ppermute(cells, "tile", [(i, i ^ k) for i in range(tiles)])
 
     def swap(cells, bit):
         return lax.ppermute(cells, "view", [(i, i ^ bit) for i in range(VIEWS)])
 
-    packed, packed_labels = call(
+    packed, both = call(
         functools.partial(pack_kernel, groups),
-        [(block, f32), (block, jnp.int32)],
+        [(block, f32), ((2 * part,) + block[1:], f32)],
         [pltpu.VMEM(data.shape[1:], f32), pltpu.VMEM(data.shape[1:], jnp.int32)],
         data,
         labels,
     )
-    (matrix,) = call(band_kernel, [((LANES, LANES), f32)], [], kernel, offsets)
-    blocks = gathered(packed)
-    label_blocks = gathered(packed_labels)
-    recorded, correction = call(
-        functools.partial(first_kernel, tiles), [(view, f32)] * 2, [], matrix, *blocks
-    )
+    bands = call(band_kernel, [((2 * LANES, 2 * LANES), jnp.bfloat16)] * 2, [], kernel, offsets)
+    blocks = {k: across(packed, k) for k in range(tiles - 1, 1, -1)}
+    beside = across(both, 1)
+    (made_own,) = call(block_kernel, [(block, f32)], [], *bands, packed)
+    made_beside, near_labels = call(
+        beside_kernel, [(block, f32), ((2 * part,) + block[1:], f32)], [], *bands, both, beside
+    )
+    (made_far,) = call(block_kernel, [(block, f32)], [], *bands, blocks[3])
+    (correction,) = call(
+        functools.partial(last_block_kernel, tiles, 2, (0, 1, 3)),
+        [(view, f32)],
+        [],
+        *bands,
+        blocks[2],
+        made_own,
+        made_beside,
+        made_far,
+    )
+    (recorded,) = call(
+        functools.partial(recorded_kernel, tiles),
+        [(view, f32)],
+        [],
+        packed,
+        beside,
+        blocks[2],
+        blocks[3],
+    )
+    far_labels = across(near_labels, 2)
     other = swap(correction, 1)
     (product,) = call(
         functools.partial(product_kernel, depth_cells), [(view, f32)], [], correction, other
@@ -430,15 +494,16 @@
     edges = call(
         functools.partial(edges_kernel, tiles, depth_cells),
         [(view, f32)] * 3,
-        [pltpu.VMEM(view, jnp.int32)],
-        *label_blocks,
+        [pltpu.VMEM(view, f32)],
+        near_labels,
+        far_labels,
     )
     received = swap(product, 2)
     estimate, correction = call(
         functools.partial(second_kernel, depth_cells),
         [(view, f32)] * 2,
         [],
-        matrix,
+        *bands,
         recorded,
         product,
         received,
@@ -477,7 +542,7 @@
         and slab % ROWS == 0
         and slab >= SWEEPS
         and slab * tiles == depth_cells
-        and tiles & (tiles - 1) == 0
+        and tiles == 4
         and LANES % depth_cells == 0
         and rows % (LANES // depth_cells) ** 2 == 0
         and (2 * SWEEPS) % ROWS == 0

time: 34.6 us -> 33.1 us (0.957)
  starting transfers between devices: 12.4 us -> 9.31 us
  waiting for transfers between devices: 14.3 us -> 16.8 us
  Pallas kernels: 5.63 us -> 4.72 us
    ppermute x6 -> x4, starting transfers between devices: 10.1 us -> 7 us  [across(): return lax.ppermute(cells, 'tile', [(i, i ^ k) for i in range(tiles)])]
    ppermute x6 -> x4, waiting for transfers between devices: 7.22 us -> 9.69 us  [across(): return lax.ppermute(cells, 'tile', [(i, i ^ k) for i in range(tiles)])]
    pallas_call x9 -> x13, Pallas kernels: 5.63 us -> 4.72 us  [call(): pl.pallas_call(body, out_shape=shapes, in_specs=[vmem] * len(args), out_s...]
  transfers between devices with their start and end apart: 10 -> 8, of which waited for: 7 -> 6; matrix products, arithmetic and copies ran while one was open for 0% -> 0% of each run, Pallas kernels for 2% -> 5%
where the time goes in v2:
time: 33.1 us; the launch traced here: 33 us
  waiting for transfers between devices  16.8 us (51%)
  starting transfers between devices  9.31 us (28%)
  Pallas kernels  4.72 us (14%)
  local copies, waits for them, and re-layouts  2.03 us (6%)
    ppermute x4, waiting for transfers between devices, across(): return lax.ppermute(cells, 'tile', [(i, i ^ k) for i in range(tiles)])  9.69 us
    ppermute x4, waiting for transfers between devices, swap(): return lax.ppermute(cells, 'view', [(i, i ^ bit) for i in range(VIEWS)])  7.07 us
    ppermute x4, starting transfers between devices, across(): return lax.ppermute(cells, 'tile', [(i, i ^ k) for i in range(tiles)])  7 us
    pallas_call x13, Pallas kernels, call(): pl.pallas_call(body, out_shape=shapes, in_specs=[vmem] * len(args), out_s...  4.72 us
    ppermute x4, starting transfers between devices, swap(): return lax.ppermute(cells, 'view', [(i, i ^ bit) for i in range(VIEWS)])  2.31 us
    unnamed x9, local copies, waits for them, and re-layouts  1.26 us
    pallas_call x1, local copies, waits for them, and re-layouts, call(): pl.pallas_call(body, out_shape=shapes, in_specs=[vmem] * len(args), out_s...  0.77 us
  transfers between devices with their start and end apart: 8, of which 6 were waited for; matrix products, arithmetic and copies ran while one was open for 0% of the time, Pallas kernels for 5%

profile of v2, /device:TPU:0, one launch (start us, length us, event | category | flops | bytes accessed | tf_op | source)
XLA Modules:
  0.0 33.0 jit_solution(8823182030485408506)
XLA Ops:
  0.0 0.0 copy-start.1
  0.0 1.0 %copy.6.data = f32[1,8,48,32]{3,2,1,0:T(8,128)S(1)} copy(f32[1,8,48,32]{2,3,1,0:T(8,128)} %param.4) | data formatting | bytes 98304 | tf_op args[0]
  1.1 0.0 copy-done.1
  1.1 0.1 copy.7.labels
  1.2 0.0 copy-start.2
  1.2 0.3 shard_map.47
  1.5 3.1 %collective-permute-start = (f32[24,8,128]{2,1,0:T(8,128)S(1)}, f32[24,8,128]{2,1,0:T(8,128)S(1)}, u32[]{:S(2)}, u32[]{:S(2)}) collective-permute-start(f32[24,8,128]{2,1,0:T(8,128)S(1)} %get-tuple-element.25.own_both), channel_id=1, source_target_pairs={{0,1},{1,0},{2,3},{3,2},{4,5},{5,4},{6,7},{7,6},{8,9},{9,8},{10,11... | collective-permute-start | bytes 294920 | tf_op jit(solution)/shard_map/ppermute | solution.py:450
  4.5 0.0 copy-start
  4.5 2.5 %collective-permute-start.2 = (f32[12,8,128]{2,1,0:T(8,128)S(1)}, f32[12,8,128]{2,1,0:T(8,128)S(1)}, u32[]{:S(2)}, u32[]{:S(2)}) collective-permute-start(f32[12,8,128]{2,1,0:T(8,128)S(1)} %get-tuple-element.24.own.block), channel_id=1, source_target_pairs={{0,3},{1,2},{2,1},{3,0},{4,7},{5,6},{6,5},{7,4},{8,11},{9,10},{10,... | collective-permute-start | bytes 147464 | tf_op jit(solution)/shard_map/ppermute | solution.py:450
  7.0 0.1 collective-permute-start.1
  7.1 0.0 copy-done.2
  7.1 0.1 copy.5.kernel
  7.2 0.0 copy-done
  7.2 0.5 %shard_map.46 = (bf16[256,256]{1,0:T(8,128)(2,1)S(1)}, bf16[256,256]{1,0:T(8,128)(2,1)S(1)}) custom-call(f32[1,32,9]{2,1,0:T(8,128)S(1)} %copy.5.kernel, s32[1,32]{1,0:T(1,128)S(1)} %copy-done), custom_call_target="tpu_custom_call" | custom-call | tf_op jit(solution)/shard_map/pallas_call | solution.py:440
  7.7 0.3 shard_map.49.refs_0_
  8.0 3.2 %collective-permute-done.2.refs_1_.block = f32[12,8,128]{2,1,0:T(8,128)S(1)} collective-permute-done((f32[12,8,128]{2,1,0:T(8,128)S(1)}, f32[12,8,128]{2,1,0:T(8,128)S(1)}, u32[]{:S(2)}, u32[]{:S(2)}) %collective-permute-start.2) | collective-permute-done | bytes 49184 | tf_op jit(solution)/shard_map/ppermute | solution.py:450
  11.2 0.3 shard_map.51.refs_2_
  11.5 0.0 collective-permute-done.both
  11.5 0.3 shard_map.50
  11.8 0.7 %collective-permute-done.1.refs_0_.block = f32[12,8,128]{2,1,0:T(8,128)S(1)} collective-permute-done((f32[12,8,128]{2,1,0:T(8,128)S(1)}, f32[12,8,128]{2,1,0:T(8,128)S(1)}, u32[]{:S(2)}, u32[]{:S(2)}) %collective-permute-start.1) | collective-permute-done | bytes 49184 | tf_op jit(solution)/shard_map/ppermute | solution.py:450
  12.5 0.3 shard_map.52.own
  12.8 0.1 collective-permute-start.3
  12.9 1.4 %collective-permute-done.3.other = f32[12,32,128]{2,1,0:T(8,128)S(1)} collective-permute-done((f32[12,32,128]{2,1,0:T(8,128)S(1)}, f32[12,32,128]{2,1,0:T(8,128)S(1)}, u32[]{:S(2)}, u32[]{:S(2)}) %collective-permute-start.3) | collective-permute-done | bytes 196640 | tf_op jit(solution)/shard_map/ppermute | solution.py:453
  14.3 0.3 shard_map.53.product
  14.7 1.6 %collective-permute-start.4 = (f32[12,32,128]{2,1,0:T(8,128)S(1)}, f32[12,32,128]{2,1,0:T(8,128)S(1)}, u32[]{:S(2)}, u32[]{:S(2)}) collective-permute-start(f32[12,32,128]{2,1,0:T(8,128)S(1)} %shard_map.53.product), channel_id=1, source_target_pairs={{0,8},{4,12},{8,0},{12,4},{1,9},{5,13},{9,1},{13,5},{2,10},{6,14},... | collective-permute-start | bytes 589832 | tf_op jit(solution)/shard_map/ppermute | solution.py:453
  16.2 1.3 %collective-permute-start.5 = (f32[24,8,128]{2,1,0:T(8,128)S(1)}, f32[24,8,128]{2,1,0:T(8,128)S(1)}, u32[]{:S(2)}, u32[]{:S(2)}) collective-permute-start(f32[24,8,128]{2,1,0:T(8,128)S(1)} %get-tuple-element.27.near), channel_id=1, source_target_pairs={{0,2},{1,3},{2,0},{3,1},{4,6},{5,7},{6,4},{7,5},{8,10},{9,11},{10,... | collective-permute-start | bytes 294920 | tf_op jit(solution)/shard_map/ppermute | solution.py:450
  17.6 5.8 %collective-permute-done.5.far = f32[24,8,128]{2,1,0:T(8,128)S(1)} collective-permute-done((f32[24,8,128]{2,1,0:T(8,128)S(1)}, f32[24,8,128]{2,1,0:T(8,128)S(1)}, u32[]{:S(2)}, u32[]{:S(2)}) %collective-permute-start.5) | collective-permute-done | bytes 98336 | tf_op jit(solution)/shard_map/ppermute | solution.py:450
  23.4 0.1 shard_map.54
  23.5 0.0 collective-permute-done.4.received
  23.6 1.1 %shard_map.55 = (f32[12,32,128]{2,1,0:T(8,128)S(1)}, f32[12,32,128]{2,1,0:T(8,128)S(1)}) custom-call(bf16[256,256]{1,0:T(8,128)(2,1)S(1)} %get-tuple-element.22.blur_band, bf16[256,256]{1,0:T(8,128)(2,1)S(1)} %get-tuple-element.23.adjoint_band, f32[12,32,128]{2,1,0:T(8,128)S(1)} %shard_map.48.recorded, f32[12,32,128]{2,1,0:T(8,128)S(1)} %shard_map.53.product, ...), custom_call_target="tpu_custom_call" | custom-call | tf_op jit(solution)/shard_map/pallas_call | solution.py:440
  24.6 0.1 collective-permute-start.6
  24.7 1.4 %collective-permute-done.6.other = f32[12,32,128]{2,1,0:T(8,128)S(1)} collective-permute-done((f32[12,32,128]{2,1,0:T(8,128)S(1)}, f32[12,32,128]{2,1,0:T(8,128)S(1)}, u32[]{:S(2)}, u32[]{:S(2)}) %collective-permute-start.6) | collective-permute-done | bytes 196640 | tf_op jit(solution)/shard_map/ppermute | solution.py:453
  26.1 0.3 %shard_map.57 = (f32[12,16,128]{2,1,0:T(8,128)S(1)}, f32[12,16,128]{2,1,0:T(8,128)S(1)}) custom-call(f32[12,32,128]{2,1,0:T(8,128)S(1)} %get-tuple-element.33.own, f32[12,32,128]{2,1,0:T(8,128)S(1)} %collective-permute-done.6.other), custom_call_target="tpu_custom_call" | custom-call | tf_op jit(solution)/shard_map/pallas_call | solution.py:440
  26.5 0.6 %collective-permute-start.7 = (f32[12,16,128]{2,1,0:T(8,128)S(1)}, f32[12,16,128]{2,1,0:T(8,128)S(1)}, u32[]{:S(2)}, u32[]{:S(2)}) collective-permute-start(f32[12,16,128]{2,1,0:T(8,128)S(1)} %get-tuple-element.35), channel_id=1, source_target_pairs={{0,8},{4,12},{8,0},{12,4},{1,9},{5,13},{9,1},{13,5},{2,10},{6,14},... | collective-permute-start | bytes 294920 | tf_op jit(solution)/shard_map/ppermute | solution.py:453
  27.1 0.1 shard_map.56
  27.2 4.2 %collective-permute-done.7.received = f32[12,16,128]{2,1,0:T(8,128)S(1)} collective-permute-done((f32[12,16,128]{2,1,0:T(8,128)S(1)}, f32[12,16,128]{2,1,0:T(8,128)S(1)}, u32[]{:S(2)}, u32[]{:S(2)}) %collective-permute-start.7) | collective-permute-done | bytes 98336 | tf_op jit(solution)/shard_map/ppermute | solution.py:453
  31.4 0.8 %shard_map.58 = f32[1,8,48,32]{3,2,1,0:T(8,128)S(1)} custom-call(f32[12,16,128]{2,1,0:T(8,128)S(1)} %get-tuple-element.32.estimate, f32[12,16,128]{2,1,0:T(8,128)S(1)} %get-tuple-element.34.kept, f32[12,16,128]{2,1,0:T(8,128)S(1)} %collective-permute-done.7.received, f32[12,16,128]{2,1,0:T(8,128)S(1)} %get-tuple-element.36.along_x, ...), custom_call_target="tpu_custom_call" | custom-call | tf_op jit(solution)/shard_map/pallas_call | solution.py:440
  32.2 0.8 %copy.8 = f32[1,8,48,32]{2,3,1,0:T(8,128)} copy(f32[1,8,48,32]{3,2,1,0:T(8,128)S(1)} %shard_map.58) | data formatting | bytes 98304 | tf_op jit(solution)/shard_map/pallas_call | solution.py:440
  (1 shorter events, 0.0 us)
Async XLA Ops:
  0.0 1.1 %copy-start.1 = (s32[1,8,48,32]{2,3,1,0:T(8,128)S(1)}, s32[1,8,48,32]{2,3,1,0:T(8,128)}, u32[]{:S(2)}) copy-start(s32[1,8,48,32]{2,3,1,0:T(8,128)} %param.5) | copy-start | bytes 147460
  1.2 6.0 %copy-start.2 = (f32[1,32,9]{1,0,2:T(1,128)S(1)}, f32[1,32,9]{1,0,2:T(1,128)}, u32[]{:S(2)}) copy-start(f32[1,32,9]{1,0,2:T(1,128)} %param.6) | copy-start | bytes 3460
  1.5 10.1 %collective-permute-start = (f32[24,8,128]{2,1,0:T(8,128)S(1)}, f32[24,8,128]{2,1,0:T(8,128)S(1)}, u32[]{:S(2)}, u32[]{:S(2)}) collective-permute-start(f32[24,8,128]{2,1,0:T(8,128)S(1)} %get-tuple-element.25.own_both), channel_id=1, source_target_pairs={{0,1},{1,0},{2,3},{3,2},{4,5},{5,4},{6,7},{7,6},{8,9},{9,8},{10,11... | collective-permute-start | bytes 294920 | tf_op jit(solution)/shard_map/ppermute | solution.py:450
  4.5 2.7 %copy-start = (s32[1,32]{1,0:T(1,128)S(1)}, s32[1,32]{1,0:T(1,128)}, u32[]{:S(2)}) copy-start(s32[1,32]{1,0:T(1,128)} %offsets.1) | copy-start | bytes 388
  4.5 6.7 %collective-permute-start.2 = (f32[12,8,128]{2,1,0:T(8,128)S(1)}, f32[12,8,128]{2,1,0:T(8,128)S(1)}, u32[]{:S(2)}, u32[]{:S(2)}) collective-permute-start(f32[12,8,128]{2,1,0:T(8,128)S(1)} %get-tuple-element.24.own.block), channel_id=1, source_target_pairs={{0,3},{1,2},{2,1},{3,0},{4,7},{5,6},{6,5},{7,4},{8,11},{9,10},{10,... | collective-permute-start | bytes 147464 | tf_op jit(solution)/shard_map/ppermute | solution.py:450
  7.0 5.5 %collective-permute-start.1 = (f32[12,8,128]{2,1,0:T(8,128)S(1)}, f32[12,8,128]{2,1,0:T(8,128)S(1)}, u32[]{:S(2)}, u32[]{:S(2)}) collective-permute-start(f32[12,8,128]{2,1,0:T(8,128)S(1)} %get-tuple-element.24.own.block), channel_id=1, source_target_pairs={{0,2},{1,3},{2,0},{3,1},{4,6},{5,7},{6,4},{7,5},{8,10},{9,11},{10,... | collective-permute-start | bytes 147464 | tf_op jit(solution)/shard_map/ppermute | solution.py:450
  12.8 1.5 %collective-permute-start.3 = (f32[12,32,128]{2,1,0:T(8,128)S(1)}, f32[12,32,128]{2,1,0:T(8,128)S(1)}, u32[]{:S(2)}, u32[]{:S(2)}) collective-permute-start(f32[12,32,128]{2,1,0:T(8,128)S(1)} %shard_map.52.own), channel_id=1, source_target_pairs={{0,4},{4,0},{8,12},{12,8},{1,5},{5,1},{9,13},{13,9},{2,6},{6,2},{1... | collective-permute-start | bytes 589832 | tf_op jit(solution)/shard_map/ppermute | solution.py:453
  14.7 8.9 %collective-permute-start.4 = (f32[12,32,128]{2,1,0:T(8,128)S(1)}, f32[12,32,128]{2,1,0:T(8,128)S(1)}, u32[]{:S(2)}, u32[]{:S(2)}) collective-permute-start(f32[12,32,128]{2,1,0:T(8,128)S(1)} %shard_map.53.product), channel_id=1, source_target_pairs={{0,8},{4,12},{8,0},{12,4},{1,9},{5,13},{9,1},{13,5},{2,10},{6,14},... | collective-permute-start | bytes 589832 | tf_op jit(solution)/shard_map/ppermute | solution.py:453
  16.2 7.2 %collective-permute-start.5 = (f32[24,8,128]{2,1,0:T(8,128)S(1)}, f32[24,8,128]{2,1,0:T(8,128)S(1)}, u32[]{:S(2)}, u32[]{:S(2)}) collective-permute-start(f32[24,8,128]{2,1,0:T(8,128)S(1)} %get-tuple-element.27.near), channel_id=1, source_target_pairs={{0,2},{1,3},{2,0},{3,1},{4,6},{5,7},{6,4},{7,5},{8,10},{9,11},{10,... | collective-permute-start | bytes 294920 | tf_op jit(solution)/shard_map/ppermute | solution.py:450
  24.6 1.5 %collective-permute-start.6 = (f32[12,32,128]{2,1,0:T(8,128)S(1)}, f32[12,32,128]{2,1,0:T(8,128)S(1)}, u32[]{:S(2)}, u32[]{:S(2)}) collective-permute-start(f32[12,32,128]{2,1,0:T(8,128)S(1)} %get-tuple-element.33.own), channel_id=1, source_target_pairs={{0,4},{4,0},{8,12},{12,8},{1,5},{5,1},{9,13},{13,9},{2,6},{6,2},{1... | collective-permute-start | bytes 589832 | tf_op jit(solution)/shard_map/ppermute | solution.py:453
  26.5 4.9 %collective-permute-start.7 = (f32[12,16,128]{2,1,0:T(8,128)S(1)}, f32[12,16,128]{2,1,0:T(8,128)S(1)}, u32[]{:S(2)}, u32[]{:S(2)}) collective-permute-start(f32[12,16,128]{2,1,0:T(8,128)S(1)} %get-tuple-element.35), channel_id=1, source_target_pairs={{0,8},{4,12},{8,0},{12,4},{1,9},{5,13},{9,1},{13,5},{2,10},{6,14},... | collective-permute-start | bytes 294920 | tf_op jit(solution)/shard_map/ppermute | solution.py:453

commit v3 on v2

--- a/solution.py
+++ b/solution.py
@@ -16,6 +16,9 @@
 LANES = 128
 ROWS = 8
 VIEWS = 4
+
+LABELS_WITH = 3
+LABELS_BY = 1
 
 
 def extended(cells, sides, width):
@@ -245,32 +248,38 @@
     target[:, pl.ds(pl.multiple_of(slot * slab, slab), slab), :] = block
 
 
-def block_kernel(blur_band, adjoint_band, block, correction):
-    correction[...] = first_correction(block[...], blur_band, adjoint_band)
-
-
-def beside_kernel(blur_band, adjoint_band, own_both, both, correction, labels_out):
+def blocks_kernel(blur_band, adjoint_band, *refs):
+    blocks, correction = refs[:-1], refs[-1]
+    part = correction.shape[0] // len(blocks)
+    cells = jnp.concatenate([block[:part] for block in blocks], axis=0)
+    correction[...] = first_correction(cells, blur_band, adjoint_band)
+
+
+def relay_kernel(own_both, both, labels_out):
     part = both.shape[0] // 2
-    correction[...] = first_correction(both[:part], blur_band, adjoint_band)
     labels_out[:part] = own_both[part:]
     labels_out[part:] = both[part:]
 
 
-def last_block_kernel(tiles, k, others, blur_band, adjoint_band, block, *refs):
-    correction = refs[-1]
+def pair_kernel(tiles, *refs):
+    own, far, products = refs[:2], refs[2:4], refs[4:]
+    pair = own[0].shape[0]
+    part = pair // 2
     slot = own_slot(tiles)
-    for j, ref in zip(others, refs):
-        place(correction, slot ^ j, ref[...])
-    place(correction, slot ^ k, first_correction(block[...], blur_band, adjoint_band))
-
-
-def recorded_kernel(tiles, own, both, *refs):
-    far, recorded = refs[:-1], refs[-1]
+    for k in range(tiles):
+        mine, theirs = k * part, (tiles - 1 - k) * part
+        near = own[mine // pair][mine % pair : mine % pair + part]
+        cells = near * far[theirs // pair][theirs % pair : theirs % pair + part]
+        for i, product in enumerate(products):
+            size = product.shape[0]
+            place(product, slot ^ k, cells[i * size : (i + 1) * size])
+
+
+def recorded_kernel(tiles, *refs):
+    blocks, recorded = refs[:-1], refs[-1]
     slot = own_slot(tiles)
-    place(recorded, slot, own[...])
-    place(recorded, slot ^ 1, both[: own.shape[0]])
-    for k, ref in enumerate(far):
-        place(recorded, slot ^ (k + 2), ref[...])
+    for k, ref in enumerate(blocks):
+        place(recorded, slot ^ k, ref[: recorded.shape[0]])
 
 
 def edges_kernel(tiles, depth_cells, near, far, along_x, along_y, along_z, whole):
@@ -278,8 +287,11 @@
     slab, lanes = near.shape[1:]
     part = near.shape[0] // 2
     for k in range(tiles):
-        source = (near, far)[k // 2]
-        place(whole, slot ^ k, source[k % 2 * part : (k % 2 + 1) * part])
+        if k in (0, LABELS_WITH):
+            cells = near[part:] if k else near[:part]
+        else:
+            cells = far[:part] if k == LABELS_BY else far[part:]
+        place(whole, slot ^ k, cells)
     total_rows = tiles * slab
     region = whole[...].reshape(part * total_rows, lanes)
     row = lax.broadcasted_iota(jnp.int32, region.shape, 0)
@@ -347,10 +359,6 @@
     return jnp.stack(out)
 
 
-def product_kernel(depth_cells, own, other, product):
-    product[...] = own[...] * exchanged(other[...], depth_cells)
-
-
 def window(ref, slot, tiles, slab, margin):
     parts = []
     for step in (-1, 0, 1):
@@ -364,17 +372,17 @@
     blur_band,
     adjoint_band,
     recorded,
-    product,
-    received,
-    along_x,
-    along_y,
-    along_z,
-    estimate,
-    correction,
+    *refs,
 ):
+    *pieces, along_x, along_y, along_z, estimate, correction = refs
+    pairs = len(pieces) // 2
     part, total_rows, lanes = recorded.shape
     flat = (part * total_rows, lanes)
-    joined = lax.rsqrt(lax.rsqrt(product[...] * received[...]))
+    joined = [
+        lax.rsqrt(lax.rsqrt(own[...] * exchanged(other[...], depth_cells)))
+        for own, other in zip(pieces[:pairs], pieces[pairs:])
+    ]
+    joined = jnp.concatenate(joined, axis=0)
     cells = (recorded[...] * joined).reshape(flat)
     edges = [ref[...].reshape(flat) for ref in (along_x, along_y, along_z)]
     for _ in range(SWEEPS):
@@ -460,37 +468,30 @@
         labels,
     )
     bands = call(band_kernel, [((2 * LANES, 2 * LANES), jnp.bfloat16)] * 2, [], kernel, offsets)
-    blocks = {k: across(packed, k) for k in range(tiles - 1, 1, -1)}
-    beside = across(both, 1)
-    (made_own,) = call(block_kernel, [(block, f32)], [], *bands, packed)
-    made_beside, near_labels = call(
-        beside_kernel, [(block, f32), ((2 * part,) + block[1:], f32)], [], *bands, both, beside
-    )
-    (made_far,) = call(block_kernel, [(block, f32)], [], *bands, blocks[3])
-    (correction,) = call(
-        functools.partial(last_block_kernel, tiles, 2, (0, 1, 3)),
-        [(view, f32)],
+    blocks = [packed] + [across(both if k == LABELS_WITH else packed, k) for k in range(1, tiles)]
+    two = ((2 * part,) + block[1:], f32)
+    (near_labels,) = call(relay_kernel, [two], [], both, blocks[LABELS_WITH])
+    made = [
+        call(blocks_kernel, [two], [], *bands, *blocks[:2])[0],
+        call(blocks_kernel, [two], [], *bands, *blocks[2:])[0],
+    ]
+    opposite = [swap(cells, 2) for cells in made]
+    pieces = part // groups
+    products = call(
+        functools.partial(pair_kernel, tiles),
+        [((groups,) + view[1:], f32)] * pieces,
         [],
-        *bands,
-        blocks[2],
-        made_own,
-        made_beside,
-        made_far,
+        *made,
+        *opposite,
     )
     (recorded,) = call(
         functools.partial(recorded_kernel, tiles),
         [(view, f32)],
         [],
-        packed,
-        beside,
-        blocks[2],
-        blocks[3],
-    )
-    far_labels = across(near_labels, 2)
-    other = swap(correction, 1)
-    (product,) = call(
-        functools.partial(product_kernel, depth_cells), [(view, f32)], [], correction, other
-    )
+        *blocks,
+    )
+    far_labels = across(near_labels, LABELS_BY)
+    others = [swap(product, 1) for product in products]
     edges = call(
         functools.partial(edges_kernel, tiles, depth_cells),
         [(view, f32)] * 3,
@@ -498,15 +499,14 @@
         near_labels,
         far_labels,
     )
-    received = swap(product, 2)
     estimate, correction = call(
         functools.partial(second_kernel, depth_cells),
         [(view, f32)] * 2,
         [],
         *bands,
         recorded,
-        product,
-        received,
+        *products,
+        *others,
         *edges,
     )
     other = swap(correction, 1)

time: 33.1 us -> 29.6 us (0.89)
  waiting for transfers between devices: 16.8 us -> 11.6 us
  starting transfers between devices: 9.31 us -> 11.7 us
  Pallas kernels: 4.72 us -> 4.07 us
    ppermute x4, waiting for transfers between devices: 9.69 us -> 3.31 us  [across(): return lax.ppermute(cells, 'tile', [(i, i ^ k) for i in range(tiles)])]
    ppermute x4 -> x7, starting transfers between devices: 2.31 us -> 4.38 us  [swap(): return lax.ppermute(cells, 'view', [(i, i ^ bit) for i in range(VIEWS)])]
    ppermute x4 -> x7, waiting for transfers between devices: 7.07 us -> 8.27 us  [swap(): return lax.ppermute(cells, 'view', [(i, i ^ bit) for i in range(VIEWS)])]
    pallas_call x13 -> x12, Pallas kernels: 4.72 us -> 4.07 us  [call(): pl.pallas_call(body, out_shape=shapes, in_specs=[vmem] * len(args), out_s...]
  transfers between devices with their start and end apart: 8 -> 11, of which waited for: 6 -> 9; matrix products, arithmetic and copies ran while one was open for 0% -> 0% of each run, Pallas kernels for 5% -> 5%
where the time goes in v3:
time: 29.6 us; the launch traced here: 29.5 us
  starting transfers between devices  11.7 us (40%)
  waiting for transfers between devices  11.6 us (39%)
  Pallas kernels  4.07 us (14%)
  local copies, waits for them, and re-layouts  2.03 us (7%)
    ppermute x7, waiting for transfers between devices, swap(): return lax.ppermute(cells, 'view', [(i, i ^ bit) for i in range(VIEWS)])  8.27 us
    ppermute x4, starting transfers between devices, across(): return lax.ppermute(cells, 'tile', [(i, i ^ k) for i in range(tiles)])  7.29 us
    ppermute x7, starting transfers between devices, swap(): return lax.ppermute(cells, 'view', [(i, i ^ bit) for i in range(VIEWS)])  4.38 us
    pallas_call x12, Pallas kernels, call(): pl.pallas_call(body, out_shape=shapes, in_specs=[vmem] * len(args), out_s...  4.07 us
    ppermute x4, waiting for transfers between devices, across(): return lax.ppermute(cells, 'tile', [(i, i ^ k) for i in range(tiles)])  3.31 us
    unnamed x9, local copies, waits for them, and re-layouts  1.26 us
    pallas_call x1, local copies, waits for them, and re-layouts, call(): pl.pallas_call(body, out_shape=shapes, in_specs=[vmem] * len(args), out_s...  0.77 us
  transfers between devices with their start and end apart: 11, of which 9 were waited for; matrix products, arithmetic and copies ran while one was open for 0% of the time, Pallas kernels for 5%

profile of v3, /device:TPU:0, one launch (start us, length us, event | category | flops | bytes accessed | tf_op | source)
XLA Modules:
  0.0 29.5 jit_solution(11721357256715710222)
XLA Ops:
  0.0 0.0 copy-start.1
  0.0 1.0 %copy.6.data = f32[1,8,48,32]{3,2,1,0:T(8,128)S(1)} copy(f32[1,8,48,32]{2,3,1,0:T(8,128)} %param.4) | data formatting | bytes 98304 | tf_op args[0]
  1.1 0.0 copy-done.1
  1.1 0.1 copy.7.labels
  1.2 0.0 copy-start.2
  1.2 0.3 shard_map.47
  1.5 5.1 %collective-permute-start.2 = (f32[24,8,128]{2,1,0:T(8,128)S(1)}, f32[24,8,128]{2,1,0:T(8,128)S(1)}, u32[]{:S(2)}, u32[]{:S(2)}) collective-permute-start(f32[24,8,128]{2,1,0:T(8,128)S(1)} %get-tuple-element.26.own_both), channel_id=1, source_target_pairs={{0,3},{1,2},{2,1},{3,0},{4,7},{5,6},{6,5},{7,4},{8,11},{9,10},{10,... | collective-permute-start | bytes 294920 | tf_op jit(solution)/shard_map/ppermute | solution.py:458
  6.6 0.0 copy-start
  6.6 0.0 collective-permute-start
  6.6 0.6 %collective-permute-start.1 = (f32[12,8,128]{2,1,0:T(8,128)S(1)}, f32[12,8,128]{2,1,0:T(8,128)S(1)}, u32[]{:S(2)}, u32[]{:S(2)}) collective-permute-start(f32[12,8,128]{2,1,0:T(8,128)S(1)} %get-tuple-element.25.refs_0_), channel_id=1, source_target_pairs={{0,2},{1,3},{2,0},{3,1},{4,6},{5,7},{6,4},{7,5},{8,10},{9,11},{10,... | collective-permute-start | bytes 147464 | tf_op jit(solution)/shard_map/ppermute | solution.py:458
  7.2 0.0 copy-done.2
  7.2 0.1 copy.5.kernel
  7.3 0.0 copy-done
  7.3 0.5 %shard_map.46 = (bf16[256,256]{1,0:T(8,128)(2,1)S(1)}, bf16[256,256]{1,0:T(8,128)(2,1)S(1)}) custom-call(f32[1,32,9]{2,1,0:T(8,128)S(1)} %copy.5.kernel, s32[1,32]{1,0:T(1,128)S(1)} %copy-done), custom_call_target="tpu_custom_call" | custom-call | tf_op jit(solution)/shard_map/pallas_call | solution.py:448
  7.8 3.2 %collective-permute-done.refs_1_ = f32[12,8,128]{2,1,0:T(8,128)S(1)} collective-permute-done((f32[12,8,128]{2,1,0:T(8,128)S(1)}, f32[12,8,128]{2,1,0:T(8,128)S(1)}, u32[]{:S(2)}, u32[]{:S(2)}) %collective-permute-start) | collective-permute-done | bytes 49184 | tf_op jit(solution)/shard_map/ppermute | solution.py:458
  11.0 0.3 %shard_map.49.refs_0_ = f32[24,8,128]{2,1,0:T(8,128)S(1)} custom-call(bf16[256,256]{1,0:T(8,128)(2,1)S(1)} %get-tuple-element.23.blur_band, bf16[256,256]{1,0:T(8,128)(2,1)S(1)} %get-tuple-element.24.adjoint_band, f32[12,8,128]{2,1,0:T(8,128)S(1)} %get-tuple-element.25.refs_0_, f32[12,8,128]{2,1,0:T(8,128)S(1)} %collective-permute-done.refs_1_), custom_call_target="tpu_custom_call" | custom-call | tf_op jit(solution)/shard_map/pallas_call | solution.py:448
  11.4 1.6 %collective-permute-start.3 = (f32[24,8,128]{2,1,0:T(8,128)S(1)}, f32[24,8,128]{2,1,0:T(8,128)S(1)}, u32[]{:S(2)}, u32[]{:S(2)}) collective-permute-start(f32[24,8,128]{2,1,0:T(8,128)S(1)} %shard_map.49.refs_0_), channel_id=1, source_target_pairs={{0,8},{4,12},{8,0},{12,4},{1,9},{5,13},{9,1},{13,5},{2,10},{6,14},... | collective-permute-start | bytes 294920 | tf_op jit(solution)/shard_map/ppermute | solution.py:461
  13.0 0.0 collective-permute-done.1.refs_2_.refs_0_
  13.0 0.0 collective-permute-done.2.refs_3_.refs_1_.both
  13.0 0.3 %shard_map.50.refs_1_ = f32[24,8,128]{2,1,0:T(8,128)S(1)} custom-call(bf16[256,256]{1,0:T(8,128)(2,1)S(1)} %get-tuple-element.23.blur_band, bf16[256,256]{1,0:T(8,128)(2,1)S(1)} %get-tuple-element.24.adjoint_band, f32[12,8,128]{2,1,0:T(8,128)S(1)} %collective-permute-done.1.refs_2_.refs_0_, f32[24,8,128]{2,1,0:T(8,128)S(1)} %collective-permute-done.2.refs_3_.refs_1_.both), custom_call_target="tpu_custom_call" | custom-call | tf_op jit(solution)/shard_map/pallas_call | solution.py:448
  13.3 0.8 %collective-permute-start.4 = (f32[24,8,128]{2,1,0:T(8,128)S(1)}, f32[24,8,128]{2,1,0:T(8,128)S(1)}, u32[]{:S(2)}, u32[]{:S(2)}) collective-permute-start(f32[24,8,128]{2,1,0:T(8,128)S(1)} %shard_map.50.refs_1_), channel_id=1, source_target_pairs={{0,8},{4,12},{8,0},{12,4},{1,9},{5,13},{9,1},{13,5},{2,10},{6,14},... | collective-permute-start | bytes 294920 | tf_op jit(solution)/shard_map/ppermute | solution.py:461
  14.1 1.5 %collective-permute-start.8 = (f32[24,8,128]{2,1,0:T(8,128)S(1)}, f32[24,8,128]{2,1,0:T(8,128)S(1)}, u32[]{:S(2)}, u32[]{:S(2)}) collective-permute-start(f32[24,8,128]{2,1,0:T(8,128)S(1)} %shard_map.52.near), channel_id=1, source_target_pairs={{0,1},{1,0},{2,3},{3,2},{4,5},{5,4},{6,7},{7,6},{8,9},{9,8},{10,11... | collective-permute-start | bytes 294920 | tf_op jit(solution)/shard_map/ppermute | solution.py:458
  15.6 1.1 %collective-permute-done.3.refs_2_ = f32[24,8,128]{2,1,0:T(8,128)S(1)} collective-permute-done((f32[24,8,128]{2,1,0:T(8,128)S(1)}, f32[24,8,128]{2,1,0:T(8,128)S(1)}, u32[]{:S(2)}, u32[]{:S(2)}) %collective-permute-start.3) | collective-permute-done | bytes 98336 | tf_op jit(solution)/shard_map/ppermute | solution.py:461
  16.8 1.2 %collective-permute-done.4.refs_3_ = f32[24,8,128]{2,1,0:T(8,128)S(1)} collective-permute-done((f32[24,8,128]{2,1,0:T(8,128)S(1)}, f32[24,8,128]{2,1,0:T(8,128)S(1)}, u32[]{:S(2)}, u32[]{:S(2)}) %collective-permute-start.4) | collective-permute-done | bytes 98336 | tf_op jit(solution)/shard_map/ppermute | solution.py:461
  18.0 0.1 collective-permute-start.5
  18.1 0.5 %collective-permute-start.6 = (f32[4,32,128]{2,1,0:T(8,128)S(1)}, f32[4,32,128]{2,1,0:T(8,128)S(1)}, u32[]{:S(2)}, u32[]{:S(2)}) collective-permute-start(f32[4,32,128]{2,1,0:T(8,128)S(1)} %get-tuple-element.28.refs_1_), channel_id=1, source_target_pairs={{0,4},{4,0},{8,12},{12,8},{1,5},{5,1},{9,13},{13,9},{2,6},{6,2},{1... | collective-permute-start | bytes 196616 | tf_op jit(solution)/shard_map/ppermute | solution.py:461
  18.6 0.1 collective-permute-start.7
  18.7 0.1 collective-permute-done.8.far
  18.8 0.1 shard_map.53
  18.9 0.4 %collective-permute-done.5.refs_3_ = f32[4,32,128]{2,1,0:T(8,128)S(1)} collective-permute-done((f32[4,32,128]{2,1,0:T(8,128)S(1)}, f32[4,32,128]{2,1,0:T(8,128)S(1)}, u32[]{:S(2)}, u32[]{:S(2)}) %collective-permute-start.5) | collective-permute-done | bytes 65568 | tf_op jit(solution)/shard_map/ppermute | solution.py:461
  19.3 0.2 collective-permute-done.6.refs_4_
  19.5 0.4 %collective-permute-done.7.refs_5_ = f32[4,32,128]{2,1,0:T(8,128)S(1)} collective-permute-done((f32[4,32,128]{2,1,0:T(8,128)S(1)}, f32[4,32,128]{2,1,0:T(8,128)S(1)}, u32[]{:S(2)}, u32[]{:S(2)}) %collective-permute-start.7) | collective-permute-done | bytes 65568 | tf_op jit(solution)/shard_map/ppermute | solution.py:461
  19.9 1.2 %shard_map.54 = (f32[12,32,128]{2,1,0:T(8,128)S(1)}, f32[12,32,128]{2,1,0:T(8,128)S(1)}) custom-call(bf16[256,256]{1,0:T(8,128)(2,1)S(1)} %get-tuple-element.23.blur_band, bf16[256,256]{1,0:T(8,128)(2,1)S(1)} %get-tuple-element.24.adjoint_band, f32[12,32,128]{2,1,0:T(8,128)S(1)} %shard_map.48.recorded, f32[4,32,128]{2,1,0:T(8,128)S(1)} %get-tuple-element.27.refs_0_, ...), custom_call_target="tpu_custom_call" | custom-call | tf_op jit(solution)/shard_map/pallas_call | solution.py:448
  21.1 0.2 collective-permute-start.9
  21.3 1.3 %collective-permute-done.9.other = f32[12,32,128]{2,1,0:T(8,128)S(1)} collective-permute-done((f32[12,32,128]{2,1,0:T(8,128)S(1)}, f32[12,32,128]{2,1,0:T(8,128)S(1)}, u32[]{:S(2)}, u32[]{:S(2)}) %collective-permute-start.9) | collective-permute-done | bytes 196640 | tf_op jit(solution)/shard_map/ppermute | solution.py:461
  22.6 0.3 %shard_map.56 = (f32[12,16,128]{2,1,0:T(8,128)S(1)}, f32[12,16,128]{2,1,0:T(8,128)S(1)}) custom-call(f32[12,32,128]{2,1,0:T(8,128)S(1)} %get-tuple-element.35.own, f32[12,32,128]{2,1,0:T(8,128)S(1)} %collective-permute-done.9.other), custom_call_target="tpu_custom_call" | custom-call | tf_op jit(solution)/shard_map/pallas_call | solution.py:448
  23.0 1.1 %collective-permute-start.10 = (f32[12,16,128]{2,1,0:T(8,128)S(1)}, f32[12,16,128]{2,1,0:T(8,128)S(1)}, u32[]{:S(2)}, u32[]{:S(2)}) collective-permute-start(f32[12,16,128]{2,1,0:T(8,128)S(1)} %get-tuple-element.37), channel_id=1, source_target_pairs={{0,8},{4,12},{8,0},{12,4},{1,9},{5,13},{9,1},{13,5},{2,10},{6,14},... | collective-permute-start | bytes 294920 | tf_op jit(solution)/shard_map/ppermute | solution.py:461
  24.1 0.1 shard_map.55
  24.2 3.7 %collective-permute-done.10.received = f32[12,16,128]{2,1,0:T(8,128)S(1)} collective-permute-done((f32[12,16,128]{2,1,0:T(8,128)S(1)}, f32[12,16,128]{2,1,0:T(8,128)S(1)}, u32[]{:S(2)}, u32[]{:S(2)}) %collective-permute-start.10) | collective-permute-done | bytes 98336 | tf_op jit(solution)/shard_map/ppermute | solution.py:461
  27.9 0.8 %shard_map.57 = f32[1,8,48,32]{3,2,1,0:T(8,128)S(1)} custom-call(f32[12,16,128]{2,1,0:T(8,128)S(1)} %get-tuple-element.34.estimate, f32[12,16,128]{2,1,0:T(8,128)S(1)} %get-tuple-element.36.kept, f32[12,16,128]{2,1,0:T(8,128)S(1)} %collective-permute-done.10.received, f32[12,16,128]{2,1,0:T(8,128)S(1)} %get-tuple-element.38.along_x, ...), custom_call_target="tpu_custom_call" | custom-call | tf_op jit(solution)/shard_map/pallas_call | solution.py:448
  28.7 0.8 %copy.8 = f32[1,8,48,32]{2,3,1,0:T(8,128)} copy(f32[1,8,48,32]{3,2,1,0:T(8,128)S(1)} %shard_map.57) | data formatting | bytes 98304 | tf_op jit(solution)/shard_map/pallas_call | solution.py:448
  (3 shorter events, 0.1 us)
Async XLA Ops:
  0.0 1.1 %copy-start.1 = (s32[1,8,48,32]{2,3,1,0:T(8,128)S(1)}, s32[1,8,48,32]{2,3,1,0:T(8,128)}, u32[]{:S(2)}) copy-start(s32[1,8,48,32]{2,3,1,0:T(8,128)} %param.5) | copy-start | bytes 147460
  1.2 6.0 %copy-start.2 = (f32[1,32,9]{1,0,2:T(1,128)S(1)}, f32[1,32,9]{1,0,2:T(1,128)}, u32[]{:S(2)}) copy-start(f32[1,32,9]{1,0,2:T(1,128)} %param.6) | copy-start | bytes 3460
  1.5 11.5 %collective-permute-start.2 = (f32[24,8,128]{2,1,0:T(8,128)S(1)}, f32[24,8,128]{2,1,0:T(8,128)S(1)}, u32[]{:S(2)}, u32[]{:S(2)}) collective-permute-start(f32[24,8,128]{2,1,0:T(8,128)S(1)} %get-tuple-element.26.own_both), channel_id=1, source_target_pairs={{0,3},{1,2},{2,1},{3,0},{4,7},{5,6},{6,5},{7,4},{8,11},{9,10},{10,... | collective-permute-start | bytes 294920 | tf_op jit(solution)/shard_map/ppermute | solution.py:458
  6.6 0.7 %copy-start = (s32[1,32]{1,0:T(1,128)S(1)}, s32[1,32]{1,0:T(1,128)}, u32[]{:S(2)}) copy-start(s32[1,32]{1,0:T(1,128)} %offsets.1) | copy-start | bytes 388
  6.6 4.5 %collective-permute-start = (f32[12,8,128]{2,1,0:T(8,128)S(1)}, f32[12,8,128]{2,1,0:T(8,128)S(1)}, u32[]{:S(2)}, u32[]{:S(2)}) collective-permute-start(f32[12,8,128]{2,1,0:T(8,128)S(1)} %get-tuple-element.25.refs_0_), channel_id=1, source_target_pairs={{0,1},{1,0},{2,3},{3,2},{4,5},{5,4},{6,7},{7,6},{8,9},{9,8},{10,11... | collective-permute-start | bytes 147464 | tf_op jit(solution)/shard_map/ppermute | solution.py:458
  6.6 6.4 %collective-permute-start.1 = (f32[12,8,128]{2,1,0:T(8,128)S(1)}, f32[12,8,128]{2,1,0:T(8,128)S(1)}, u32[]{:S(2)}, u32[]{:S(2)}) collective-permute-start(f32[12,8,128]{2,1,0:T(8,128)S(1)} %get-tuple-element.25.refs_0_), channel_id=1, source_target_pairs={{0,2},{1,3},{2,0},{3,1},{4,6},{5,7},{6,4},{7,5},{8,10},{9,11},{10,... | collective-permute-start | bytes 147464 | tf_op jit(solution)/shard_map/ppermute | solution.py:458
  11.4 5.4 %collective-permute-start.3 = (f32[24,8,128]{2,1,0:T(8,128)S(1)}, f32[24,8,128]{2,1,0:T(8,128)S(1)}, u32[]{:S(2)}, u32[]{:S(2)}) collective-permute-start(f32[24,8,128]{2,1,0:T(8,128)S(1)} %shard_map.49.refs_0_), channel_id=1, source_target_pairs={{0,8},{4,12},{8,0},{12,4},{1,9},{5,13},{9,1},{13,5},{2,10},{6,14},... | collective-permute-start | bytes 294920 | tf_op jit(solution)/shard_map/ppermute | solution.py:461
  13.3 4.7 %collective-permute-start.4 = (f32[24,8,128]{2,1,0:T(8,128)S(1)}, f32[24,8,128]{2,1,0:T(8,128)S(1)}, u32[]{:S(2)}, u32[]{:S(2)}) collective-permute-start(f32[24,8,128]{2,1,0:T(8,128)S(1)} %shard_map.50.refs_1_), channel_id=1, source_target_pairs={{0,8},{4,12},{8,0},{12,4},{1,9},{5,13},{9,1},{13,5},{2,10},{6,14},... | collective-permute-start | bytes 294920 | tf_op jit(solution)/shard_map/ppermute | solution.py:461
  14.1 4.7 %collective-permute-start.8 = (f32[24,8,128]{2,1,0:T(8,128)S(1)}, f32[24,8,128]{2,1,0:T(8,128)S(1)}, u32[]{:S(2)}, u32[]{:S(2)}) collective-permute-start(f32[24,8,128]{2,1,0:T(8,128)S(1)} %shard_map.52.near), channel_id=1, source_target_pairs={{0,1},{1,0},{2,3},{3,2},{4,5},{5,4},{6,7},{7,6},{8,9},{9,8},{10,11... | collective-permute-start | bytes 294920 | tf_op jit(solution)/shard_map/ppermute | solution.py:458
  18.0 1.3 %collective-permute-start.5 = (f32[4,32,128]{2,1,0:T(8,128)S(1)}, f32[4,32,128]{2,1,0:T(8,128)S(1)}, u32[]{:S(2)}, u32[]{:S(2)}) collective-permute-start(f32[4,32,128]{2,1,0:T(8,128)S(1)} %get-tuple-element.27.refs_0_), channel_id=1, source_target_pairs={{0,4},{4,0},{8,12},{12,8},{1,5},{5,1},{9,13},{13,9},{2,6},{6,2},{1... | collective-permute-start | bytes 196616 | tf_op jit(solution)/shard_map/ppermute | solution.py:461
  18.1 1.4 %collective-permute-start.6 = (f32[4,32,128]{2,1,0:T(8,128)S(1)}, f32[4,32,128]{2,1,0:T(8,128)S(1)}, u32[]{:S(2)}, u32[]{:S(2)}) collective-permute-start(f32[4,32,128]{2,1,0:T(8,128)S(1)} %get-tuple-element.28.refs_1_), channel_id=1, source_target_pairs={{0,4},{4,0},{8,12},{12,8},{1,5},{5,1},{9,13},{13,9},{2,6},{6,2},{1... | collective-permute-start | bytes 196616 | tf_op jit(solution)/shard_map/ppermute | solution.py:461
  18.6 1.3 %collective-permute-start.7 = (f32[4,32,128]{2,1,0:T(8,128)S(1)}, f32[4,32,128]{2,1,0:T(8,128)S(1)}, u32[]{:S(2)}, u32[]{:S(2)}) collective-permute-start(f32[4,32,128]{2,1,0:T(8,128)S(1)} %get-tuple-element.29.refs_2_), channel_id=1, source_target_pairs={{0,4},{4,0},{8,12},{12,8},{1,5},{5,1},{9,13},{13,9},{2,6},{6,2},{1... | collective-permute-start | bytes 196616 | tf_op jit(solution)/shard_map/ppermute | solution.py:461
  21.1 1.5 %collective-permute-start.9 = (f32[12,32,128]{2,1,0:T(8,128)S(1)}, f32[12,32,128]{2,1,0:T(8,128)S(1)}, u32[]{:S(2)}, u32[]{:S(2)}) collective-permute-start(f32[12,32,128]{2,1,0:T(8,128)S(1)} %get-tuple-element.35.own), channel_id=1, source_target_pairs={{0,4},{4,0},{8,12},{12,8},{1,5},{5,1},{9,13},{13,9},{2,6},{6,2},{1... | collective-permute-start | bytes 589832 | tf_op jit(solution)/shard_map/ppermute | solution.py:461
  23.0 4.9 %collective-permute-start.10 = (f32[12,16,128]{2,1,0:T(8,128)S(1)}, f32[12,16,128]{2,1,0:T(8,128)S(1)}, u32[]{:S(2)}, u32[]{:S(2)}) collective-permute-start(f32[12,16,128]{2,1,0:T(8,128)S(1)} %get-tuple-element.37), channel_id=1, source_target_pairs={{0,8},{4,12},{8,0},{12,4},{1,9},{5,13},{9,1},{13,5},{2,10},{6,14},... | collective-permute-start | bytes 294920 | tf_op jit(solution)/shard_map/ppermute | solution.py:461

commit v4 on v3

--- a/solution.py
+++ b/solution.py
@@ -16,6 +16,7 @@
 LANES = 128
 ROWS = 8
 VIEWS = 4
+SHARES = 7
 
 LABELS_WITH = 3
 LABELS_BY = 1
@@ -282,7 +283,8 @@
         place(recorded, slot ^ k, ref[: recorded.shape[0]])
 
 
-def edges_kernel(tiles, depth_cells, near, far, along_x, along_y, along_z, whole):
+def weights_kernel(tiles, depth_cells, near, far, *refs):
+    outs, whole = refs[:-1], refs[-1]
     slot = own_slot(tiles)
     slab, lanes = near.shape[1:]
     part = near.shape[0] // 2
@@ -297,17 +299,27 @@
     row = lax.broadcasted_iota(jnp.int32, region.shape, 0)
     lane = lax.broadcasted_iota(jnp.int32, region.shape, 1)
 
-    def weighted(upper, inside, target):
+    def weighted(upper, inside):
         same = jnp.where(upper == region, TAU, TAU * WEAK)
-        target[...] = jnp.where(inside, same, 0.0).reshape(target.shape)
-
-    weighted(up_rows(region), lax.rem(row, total_rows) != total_rows - 1, along_x)
-    weighted(
+        return jnp.where(inside, same, 0.0)
+
+    along_x = weighted(up_rows(region), lax.rem(row, total_rows) != total_rows - 1)
+    along_y = weighted(
         up_second(region, total_rows, depth_cells),
         (row < (part - 1) * total_rows) | (lane < lanes - depth_cells),
+    )
+    along_z = weighted(up_depth(region), lax.rem(lane, depth_cells) != depth_cells - 1)
+    shares = [
+        along_x,
+        down_rows(along_x),
         along_y,
-    )
-    weighted(up_depth(region), lax.rem(lane, depth_cells) != depth_cells - 1, along_z)
+        down_second(along_y, total_rows, depth_cells),
+        along_z,
+        down_depth(along_z),
+    ]
+    shares.append(1.0 - sum(shares[1:], shares[0]))
+    for share, out in zip(shares, outs):
+        out[...] = share.reshape(out.shape)
 
 
 def up_rows(cells):
@@ -328,15 +340,26 @@
     return jnp.concatenate([last, cells[:-total_rows]], axis=0)
 
 
-def swept(cells, along_x, along_y, along_z, total_rows, depth_cells):
-    flux_x = along_x * (up_rows(cells) - cells)
-    flux_y = along_y * (up_second(cells, total_rows, depth_cells) - cells)
-    flux_z = along_z * (up_depth(cells) - cells)
+def down_rows(cells):
+    return pltpu.roll(cells, 1, 0)
+
+
+def down_depth(cells):
+    return pltpu.roll(cells, 1, 1)
+
+
+def swept(cells, shares, total_rows, depth_cells):
+    up_x, down_x, up_y, down_y, up_z, down_z, kept = [
+        ref[...].reshape(cells.shape) for ref in shares
+    ]
     return (
-        cells
-        + (flux_x - pltpu.roll(flux_x, 1, 0))
-        + (flux_y - down_second(flux_y, total_rows, depth_cells))
-        + (flux_z - pltpu.roll(flux_z, 1, 1))
+        (up_z * up_depth(cells) + down_z * down_depth(cells))
+        + (up_x * up_rows(cells) + down_x * down_rows(cells))
+        + (
+            up_y * up_second(cells, total_rows, depth_cells)
+            + down_y * down_second(cells, total_rows, depth_cells)
+        )
+        + kept * cells
     )
 
 
@@ -374,7 +397,8 @@
     recorded,
     *refs,
 ):
-    *pieces, along_x, along_y, along_z, estimate, correction = refs
+    refs, (estimate, correction) = refs[:-2], refs[-2:]
+    pieces, shares = refs[:-SHARES], refs[-SHARES:]
     pairs = len(pieces) // 2
     part, total_rows, lanes = recorded.shape
     flat = (part * total_rows, lanes)
@@ -384,9 +408,8 @@
     ]
     joined = jnp.concatenate(joined, axis=0)
     cells = (recorded[...] * joined).reshape(flat)
-    edges = [ref[...].reshape(flat) for ref in (along_x, along_y, along_z)]
     for _ in range(SWEEPS):
-        cells = swept(cells, *edges, total_rows, depth_cells)
+        cells = swept(cells, shares, total_rows, depth_cells)
     estimate[...] = cells.reshape(estimate.shape)
     correction[...] = corrected(
         recorded[...].reshape(flat), cells, blur_band, adjoint_band
@@ -401,22 +424,23 @@
     sent[...] = window(product, tiles - 1 - slot, tiles, slab, SWEEPS)
 
 
-def near_kernel(tiles, estimate, along_x, along_y, along_z, *outs):
+def near_kernel(tiles, *refs):
     slot = own_slot(tiles)
-    slab = estimate.shape[1] // tiles
-    for ref, out in zip((estimate, along_x, along_y, along_z), outs):
+    slab = refs[0].shape[1] // tiles
+    half = len(refs) // 2
+    for ref, out in zip(refs[:half], refs[half:]):
         out[...] = window(ref, slot, tiles, slab, SWEEPS)
 
 
-def last_kernel(groups, depth_cells, estimate, kept, received, along_x, along_y, along_z, out, held):
+def last_kernel(groups, depth_cells, estimate, kept, received, *refs):
+    *shares, out, held = refs
     part, extent, lanes = estimate.shape
     slab = extent - 2 * SWEEPS
     flat = (part * extent, lanes)
     joined = lax.rsqrt(lax.rsqrt(kept[...] * received[...]))
     cells = (estimate[...] * joined).reshape(flat)
-    edges = [ref[...].reshape(flat) for ref in (along_x, along_y, along_z)]
     for _ in range(SWEEPS):
-        cells = swept(cells, *edges, extent, depth_cells)
+        cells = swept(cells, shares, extent, depth_cells)
     cells = cells.reshape(part, extent, lanes)[:, SWEEPS : SWEEPS + slab]
     cells = cells.reshape(part * slab, lanes)
     cells = jnp.take_along_axis(cells, lane_order(cells.shape, depth_cells), axis=1)
@@ -492,9 +516,9 @@
     )
     far_labels = across(near_labels, LABELS_BY)
     others = [swap(product, 1) for product in products]
-    edges = call(
-        functools.partial(edges_kernel, tiles, depth_cells),
-        [(view, f32)] * 3,
+    shares = call(
+        functools.partial(weights_kernel, tiles, depth_cells),
+        [(view, f32)] * SHARES,
         [pltpu.VMEM(view, f32)],
         near_labels,
         far_labels,
@@ -507,11 +531,11 @@
         recorded,
         *products,
         *others,
-        *edges,
+        *shares,
     )
     other = swap(correction, 1)
     near_cells = call(
-        functools.partial(near_kernel, tiles), [(near, f32)] * 4, [], estimate, *edges
+        functools.partial(near_kernel, tiles), [(near, f32)] * (1 + SHARES), [], estimate, *shares
     )
     kept, sent = call(
         functools.partial(windows_kernel, tiles, depth_cells),

time: 29.6 us -> 29.4 us (level)
  no operation moved by 1% of the time
where the time goes in v4:
time: 29.4 us; the launch traced here: 29.3 us
  starting transfers between devices  11.7 us (40%)
  waiting for transfers between devices  11.4 us (39%)
  Pallas kernels  4.02 us (14%)
  local copies, waits for them, and re-layouts  2.03 us (7%)
    ppermute x7, waiting for transfers between devices, swap(): return lax.ppermute(cells, 'view', [(i, i ^ bit) for i in range(VIEWS)])  8.11 us
    ppermute x4, starting transfers between devices, across(): return lax.ppermute(cells, 'tile', [(i, i ^ k) for i in range(tiles)])  7.29 us
    ppermute x7, starting transfers between devices, swap(): return lax.ppermute(cells, 'view', [(i, i ^ bit) for i in range(VIEWS)])  4.38 us
    pallas_call x12, Pallas kernels, call(): pl.pallas_call(body, out_shape=shapes, in_specs=[vmem] * len(args), out_s...  4.02 us
    ppermute x4, waiting for transfers between devices, across(): return lax.ppermute(cells, 'tile', [(i, i ^ k) for i in range(tiles)])  3.31 us
    unnamed x9, local copies, waits for them, and re-layouts  1.26 us
    pallas_call x1, local copies, waits for them, and re-layouts, call(): pl.pallas_call(body, out_shape=shapes, in_specs=[vmem] * len(args), out_s...  0.77 us
  transfers between devices with their start and end apart: 11, of which 9 were waited for; matrix products, arithmetic and copies ran while one was open for 0% of the time, Pallas kernels for 5%

profile of v4, /device:TPU:0, one launch (start us, length us, event | category | flops | bytes accessed | tf_op | source)
XLA Modules:
  0.0 29.3 jit_solution(12678833340644396642)
XLA Ops:
  0.0 0.0 copy-start.1
  0.0 1.0 %copy.6.data = f32[1,8,48,32]{3,2,1,0:T(8,128)S(1)} copy(f32[1,8,48,32]{2,3,1,0:T(8,128)} %param.4) | data formatting | bytes 98304 | tf_op args[0]
  1.1 0.0 copy-done.1
  1.1 0.1 copy.7.labels
  1.2 0.0 copy-start.2
  1.2 0.3 shard_map.47
  1.5 5.1 %collective-permute-start.2 = (f32[24,8,128]{2,1,0:T(8,128)S(1)}, f32[24,8,128]{2,1,0:T(8,128)S(1)}, u32[]{:S(2)}, u32[]{:S(2)}) collective-permute-start(f32[24,8,128]{2,1,0:T(8,128)S(1)} %get-tuple-element.34.own_both), channel_id=1, source_target_pairs={{0,3},{1,2},{2,1},{3,0},{4,7},{5,6},{6,5},{7,4},{8,11},{9,10},{10,... | collective-permute-start | bytes 294920 | tf_op jit(solution)/shard_map/ppermute | solution.py:482
  6.6 0.0 copy-start
  6.6 0.0 collective-permute-start
  6.6 0.6 %collective-permute-start.1 = (f32[12,8,128]{2,1,0:T(8,128)S(1)}, f32[12,8,128]{2,1,0:T(8,128)S(1)}, u32[]{:S(2)}, u32[]{:S(2)}) collective-permute-start(f32[12,8,128]{2,1,0:T(8,128)S(1)} %get-tuple-element.33.refs_0_), channel_id=1, source_target_pairs={{0,2},{1,3},{2,0},{3,1},{4,6},{5,7},{6,4},{7,5},{8,10},{9,11},{10,... | collective-permute-start | bytes 147464 | tf_op jit(solution)/shard_map/ppermute | solution.py:482
  7.2 0.0 copy-done.2
  7.2 0.1 copy.5.kernel
  7.3 0.0 copy-done
  7.3 0.5 %shard_map.46 = (bf16[256,256]{1,0:T(8,128)(2,1)S(1)}, bf16[256,256]{1,0:T(8,128)(2,1)S(1)}) custom-call(f32[1,32,9]{2,1,0:T(8,128)S(1)} %copy.5.kernel, s32[1,32]{1,0:T(1,128)S(1)} %copy-done), custom_call_target="tpu_custom_call" | custom-call | tf_op jit(solution)/shard_map/pallas_call | solution.py:472
  7.8 3.2 %collective-permute-done.refs_1_ = f32[12,8,128]{2,1,0:T(8,128)S(1)} collective-permute-done((f32[12,8,128]{2,1,0:T(8,128)S(1)}, f32[12,8,128]{2,1,0:T(8,128)S(1)}, u32[]{:S(2)}, u32[]{:S(2)}) %collective-permute-start) | collective-permute-done | bytes 49184 | tf_op jit(solution)/shard_map/ppermute | solution.py:482
  11.0 0.3 %shard_map.49.refs_0_ = f32[24,8,128]{2,1,0:T(8,128)S(1)} custom-call(bf16[256,256]{1,0:T(8,128)(2,1)S(1)} %get-tuple-element.31.blur_band, bf16[256,256]{1,0:T(8,128)(2,1)S(1)} %get-tuple-element.32.adjoint_band, f32[12,8,128]{2,1,0:T(8,128)S(1)} %get-tuple-element.33.refs_0_, f32[12,8,128]{2,1,0:T(8,128)S(1)} %collective-permute-done.refs_1_), custom_call_target="tpu_custom_call" | custom-call | tf_op jit(solution)/shard_map/pallas_call | solution.py:472
  11.4 1.6 %collective-permute-start.3 = (f32[24,8,128]{2,1,0:T(8,128)S(1)}, f32[24,8,128]{2,1,0:T(8,128)S(1)}, u32[]{:S(2)}, u32[]{:S(2)}) collective-permute-start(f32[24,8,128]{2,1,0:T(8,128)S(1)} %shard_map.49.refs_0_), channel_id=1, source_target_pairs={{0,8},{4,12},{8,0},{12,4},{1,9},{5,13},{9,1},{13,5},{2,10},{6,14},... | collective-permute-start | bytes 294920 | tf_op jit(solution)/shard_map/ppermute | solution.py:485
  13.0 0.0 collective-permute-done.1.refs_2_.refs_0_
  13.0 0.0 collective-permute-done.2.refs_3_.refs_1_.both
  13.0 0.3 %shard_map.50.refs_1_ = f32[24,8,128]{2,1,0:T(8,128)S(1)} custom-call(bf16[256,256]{1,0:T(8,128)(2,1)S(1)} %get-tuple-element.31.blur_band, bf16[256,256]{1,0:T(8,128)(2,1)S(1)} %get-tuple-element.32.adjoint_band, f32[12,8,128]{2,1,0:T(8,128)S(1)} %collective-permute-done.1.refs_2_.refs_0_, f32[24,8,128]{2,1,0:T(8,128)S(1)} %collective-permute-done.2.refs_3_.refs_1_.both), custom_call_target="tpu_custom_call" | custom-call | tf_op jit(solution)/shard_map/pallas_call | solution.py:472
  13.3 0.8 %collective-permute-start.4 = (f32[24,8,128]{2,1,0:T(8,128)S(1)}, f32[24,8,128]{2,1,0:T(8,128)S(1)}, u32[]{:S(2)}, u32[]{:S(2)}) collective-permute-start(f32[24,8,128]{2,1,0:T(8,128)S(1)} %shard_map.50.refs_1_), channel_id=1, source_target_pairs={{0,8},{4,12},{8,0},{12,4},{1,9},{5,13},{9,1},{13,5},{2,10},{6,14},... | collective-permute-start | bytes 294920 | tf_op jit(solution)/shard_map/ppermute | solution.py:485
  14.1 1.5 %collective-permute-start.8 = (f32[24,8,128]{2,1,0:T(8,128)S(1)}, f32[24,8,128]{2,1,0:T(8,128)S(1)}, u32[]{:S(2)}, u32[]{:S(2)}) collective-permute-start(f32[24,8,128]{2,1,0:T(8,128)S(1)} %shard_map.52.near), channel_id=1, source_target_pairs={{0,1},{1,0},{2,3},{3,2},{4,5},{5,4},{6,7},{7,6},{8,9},{9,8},{10,11... | collective-permute-start | bytes 294920 | tf_op jit(solution)/shard_map/ppermute | solution.py:482
  15.6 1.1 %collective-permute-done.3.refs_2_ = f32[24,8,128]{2,1,0:T(8,128)S(1)} collective-permute-done((f32[24,8,128]{2,1,0:T(8,128)S(1)}, f32[24,8,128]{2,1,0:T(8,128)S(1)}, u32[]{:S(2)}, u32[]{:S(2)}) %collective-permute-start.3) | collective-permute-done | bytes 98336 | tf_op jit(solution)/shard_map/ppermute | solution.py:485
  16.8 1.2 %collective-permute-done.4.refs_3_ = f32[24,8,128]{2,1,0:T(8,128)S(1)} collective-permute-done((f32[24,8,128]{2,1,0:T(8,128)S(1)}, f32[24,8,128]{2,1,0:T(8,128)S(1)}, u32[]{:S(2)}, u32[]{:S(2)}) %collective-permute-start.4) | collective-permute-done | bytes 98336 | tf_op jit(solution)/shard_map/ppermute | solution.py:485
  18.0 0.1 collective-permute-start.5
  18.1 0.5 %collective-permute-start.6 = (f32[4,32,128]{2,1,0:T(8,128)S(1)}, f32[4,32,128]{2,1,0:T(8,128)S(1)}, u32[]{:S(2)}, u32[]{:S(2)}) collective-permute-start(f32[4,32,128]{2,1,0:T(8,128)S(1)} %get-tuple-element.36.refs_1_), channel_id=1, source_target_pairs={{0,4},{4,0},{8,12},{12,8},{1,5},{5,1},{9,13},{13,9},{2,6},{6,2},{1... | collective-permute-start | bytes 196616 | tf_op jit(solution)/shard_map/ppermute | solution.py:485
  18.6 0.1 collective-permute-start.7
  18.7 0.1 collective-permute-done.8.far
  18.8 0.2 shard_map.53
  19.0 0.3 %collective-permute-done.5.refs_3_ = f32[4,32,128]{2,1,0:T(8,128)S(1)} collective-permute-done((f32[4,32,128]{2,1,0:T(8,128)S(1)}, f32[4,32,128]{2,1,0:T(8,128)S(1)}, u32[]{:S(2)}, u32[]{:S(2)}) %collective-permute-start.5) | collective-permute-done | bytes 65568 | tf_op jit(solution)/shard_map/ppermute | solution.py:485
  19.3 0.2 collective-permute-done.6.refs_4_
  19.5 0.4 %collective-permute-done.7.refs_5_ = f32[4,32,128]{2,1,0:T(8,128)S(1)} collective-permute-done((f32[4,32,128]{2,1,0:T(8,128)S(1)}, f32[4,32,128]{2,1,0:T(8,128)S(1)}, u32[]{:S(2)}, u32[]{:S(2)}) %collective-permute-start.7) | collective-permute-done | bytes 65568 | tf_op jit(solution)/shard_map/ppermute | solution.py:485
  19.9 1.1 %shard_map.54 = (f32[12,32,128]{2,1,0:T(8,128)S(1)}, f32[12,32,128]{2,1,0:T(8,128)S(1)}) custom-call(bf16[256,256]{1,0:T(8,128)(2,1)S(1)} %get-tuple-element.31.blur_band, bf16[256,256]{1,0:T(8,128)(2,1)S(1)} %get-tuple-element.32.adjoint_band, f32[12,32,128]{2,1,0:T(8,128)S(1)} %shard_map.48.recorded, f32[4,32,128]{2,1,0:T(8,128)S(1)} %get-tuple-element.35.refs_0_, ...), custom_call_target="tpu_custom_call" | custom-call | tf_op jit(solution)/shard_map/pallas_call | solution.py:472
  21.0 0.2 collective-permute-start.9
  21.2 1.3 %collective-permute-done.9.other = f32[12,32,128]{2,1,0:T(8,128)S(1)} collective-permute-done((f32[12,32,128]{2,1,0:T(8,128)S(1)}, f32[12,32,128]{2,1,0:T(8,128)S(1)}, u32[]{:S(2)}, u32[]{:S(2)}) %collective-permute-start.9) | collective-permute-done | bytes 196640 | tf_op jit(solution)/shard_map/ppermute | solution.py:485
  22.5 0.3 %shard_map.56 = (f32[12,16,128]{2,1,0:T(8,128)S(1)}, f32[12,16,128]{2,1,0:T(8,128)S(1)}) custom-call(f32[12,32,128]{2,1,0:T(8,128)S(1)} %get-tuple-element.47.own, f32[12,32,128]{2,1,0:T(8,128)S(1)} %collective-permute-done.9.other), custom_call_target="tpu_custom_call" | custom-call | tf_op jit(solution)/shard_map/pallas_call | solution.py:472
  22.8 1.1 %collective-permute-start.10 = (f32[12,16,128]{2,1,0:T(8,128)S(1)}, f32[12,16,128]{2,1,0:T(8,128)S(1)}, u32[]{:S(2)}, u32[]{:S(2)}) collective-permute-start(f32[12,16,128]{2,1,0:T(8,128)S(1)} %get-tuple-element.49), channel_id=1, source_target_pairs={{0,8},{4,12},{8,0},{12,4},{1,9},{5,13},{9,1},{13,5},{2,10},{6,14},... | collective-permute-start | bytes 294920 | tf_op jit(solution)/shard_map/ppermute | solution.py:485
  24.0 0.2 shard_map.55
  24.1 3.6 %collective-permute-done.10.received = f32[12,16,128]{2,1,0:T(8,128)S(1)} collective-permute-done((f32[12,16,128]{2,1,0:T(8,128)S(1)}, f32[12,16,128]{2,1,0:T(8,128)S(1)}, u32[]{:S(2)}, u32[]{:S(2)}) %collective-permute-start.10) | collective-permute-done | bytes 98336 | tf_op jit(solution)/shard_map/ppermute | solution.py:485
  27.8 0.7 %shard_map.57 = f32[1,8,48,32]{3,2,1,0:T(8,128)S(1)} custom-call(f32[12,16,128]{2,1,0:T(8,128)S(1)} %get-tuple-element.46.estimate, f32[12,16,128]{2,1,0:T(8,128)S(1)} %get-tuple-element.48.kept, f32[12,16,128]{2,1,0:T(8,128)S(1)} %collective-permute-done.10.received, f32[12,16,128]{2,1,0:T(8,128)S(1)} %get-tuple-element.50.refs_0_, ...), custom_call_target="tpu_custom_call" | custom-call | tf_op jit(solution)/shard_map/pallas_call | solution.py:472
  28.5 0.8 %copy.8 = f32[1,8,48,32]{2,3,1,0:T(8,128)} copy(f32[1,8,48,32]{3,2,1,0:T(8,128)S(1)} %shard_map.57) | data formatting | bytes 98304 | tf_op jit(solution)/shard_map/pallas_call | solution.py:472
  (3 shorter events, 0.1 us)
Async XLA Ops:
  0.0 1.1 %copy-start.1 = (s32[1,8,48,32]{2,3,1,0:T(8,128)S(1)}, s32[1,8,48,32]{2,3,1,0:T(8,128)}, u32[]{:S(2)}) copy-start(s32[1,8,48,32]{2,3,1,0:T(8,128)} %param.5) | copy-start | bytes 147460
  1.2 6.0 %copy-start.2 = (f32[1,32,9]{1,0,2:T(1,128)S(1)}, f32[1,32,9]{1,0,2:T(1,128)}, u32[]{:S(2)}) copy-start(f32[1,32,9]{1,0,2:T(1,128)} %param.6) | copy-start | bytes 3460
  1.5 11.5 %collective-permute-start.2 = (f32[24,8,128]{2,1,0:T(8,128)S(1)}, f32[24,8,128]{2,1,0:T(8,128)S(1)}, u32[]{:S(2)}, u32[]{:S(2)}) collective-permute-start(f32[24,8,128]{2,1,0:T(8,128)S(1)} %get-tuple-element.34.own_both), channel_id=1, source_target_pairs={{0,3},{1,2},{2,1},{3,0},{4,7},{5,6},{6,5},{7,4},{8,11},{9,10},{10,... | collective-permute-start | bytes 294920 | tf_op jit(solution)/shard_map/ppermute | solution.py:482
  6.6 0.7 %copy-start = (s32[1,32]{1,0:T(1,128)S(1)}, s32[1,32]{1,0:T(1,128)}, u32[]{:S(2)}) copy-start(s32[1,32]{1,0:T(1,128)} %offsets.1) | copy-start | bytes 388
  6.6 4.5 %collective-permute-start = (f32[12,8,128]{2,1,0:T(8,128)S(1)}, f32[12,8,128]{2,1,0:T(8,128)S(1)}, u32[]{:S(2)}, u32[]{:S(2)}) collective-permute-start(f32[12,8,128]{2,1,0:T(8,128)S(1)} %get-tuple-element.33.refs_0_), channel_id=1, source_target_pairs={{0,1},{1,0},{2,3},{3,2},{4,5},{5,4},{6,7},{7,6},{8,9},{9,8},{10,11... | collective-permute-start | bytes 147464 | tf_op jit(solution)/shard_map/ppermute | solution.py:482
  6.6 6.4 %collective-permute-start.1 = (f32[12,8,128]{2,1,0:T(8,128)S(1)}, f32[12,8,128]{2,1,0:T(8,128)S(1)}, u32[]{:S(2)}, u32[]{:S(2)}) collective-permute-start(f32[12,8,128]{2,1,0:T(8,128)S(1)} %get-tuple-element.33.refs_0_), channel_id=1, source_target_pairs={{0,2},{1,3},{2,0},{3,1},{4,6},{5,7},{6,4},{7,5},{8,10},{9,11},{10,... | collective-permute-start | bytes 147464 | tf_op jit(solution)/shard_map/ppermute | solution.py:482
  11.4 5.4 %collective-permute-start.3 = (f32[24,8,128]{2,1,0:T(8,128)S(1)}, f32[24,8,128]{2,1,0:T(8,128)S(1)}, u32[]{:S(2)}, u32[]{:S(2)}) collective-permute-start(f32[24,8,128]{2,1,0:T(8,128)S(1)} %shard_map.49.refs_0_), channel_id=1, source_target_pairs={{0,8},{4,12},{8,0},{12,4},{1,9},{5,13},{9,1},{13,5},{2,10},{6,14},... | collective-permute-start | bytes 294920 | tf_op jit(solution)/shard_map/ppermute | solution.py:485
  13.3 4.7 %collective-permute-start.4 = (f32[24,8,128]{2,1,0:T(8,128)S(1)}, f32[24,8,128]{2,1,0:T(8,128)S(1)}, u32[]{:S(2)}, u32[]{:S(2)}) collective-permute-start(f32[24,8,128]{2,1,0:T(8,128)S(1)} %shard_map.50.refs_1_), channel_id=1, source_target_pairs={{0,8},{4,12},{8,0},{12,4},{1,9},{5,13},{9,1},{13,5},{2,10},{6,14},... | collective-permute-start | bytes 294920 | tf_op jit(solution)/shard_map/ppermute | solution.py:485
  14.1 4.7 %collective-permute-start.8 = (f32[24,8,128]{2,1,0:T(8,128)S(1)}, f32[24,8,128]{2,1,0:T(8,128)S(1)}, u32[]{:S(2)}, u32[]{:S(2)}) collective-permute-start(f32[24,8,128]{2,1,0:T(8,128)S(1)} %shard_map.52.near), channel_id=1, source_target_pairs={{0,1},{1,0},{2,3},{3,2},{4,5},{5,4},{6,7},{7,6},{8,9},{9,8},{10,11... | collective-permute-start | bytes 294920 | tf_op jit(solution)/shard_map/ppermute | solution.py:482
  18.0 1.3 %collective-permute-start.5 = (f32[4,32,128]{2,1,0:T(8,128)S(1)}, f32[4,32,128]{2,1,0:T(8,128)S(1)}, u32[]{:S(2)}, u32[]{:S(2)}) collective-permute-start(f32[4,32,128]{2,1,0:T(8,128)S(1)} %get-tuple-element.35.refs_0_), channel_id=1, source_target_pairs={{0,4},{4,0},{8,12},{12,8},{1,5},{5,1},{9,13},{13,9},{2,6},{6,2},{1... | collective-permute-start | bytes 196616 | tf_op jit(solution)/shard_map/ppermute | solution.py:485
  18.1 1.4 %collective-permute-start.6 = (f32[4,32,128]{2,1,0:T(8,128)S(1)}, f32[4,32,128]{2,1,0:T(8,128)S(1)}, u32[]{:S(2)}, u32[]{:S(2)}) collective-permute-start(f32[4,32,128]{2,1,0:T(8,128)S(1)} %get-tuple-element.36.refs_1_), channel_id=1, source_target_pairs={{0,4},{4,0},{8,12},{12,8},{1,5},{5,1},{9,13},{13,9},{2,6},{6,2},{1... | collective-permute-start | bytes 196616 | tf_op jit(solution)/shard_map/ppermute | solution.py:485
  18.6 1.3 %collective-permute-start.7 = (f32[4,32,128]{2,1,0:T(8,128)S(1)}, f32[4,32,128]{2,1,0:T(8,128)S(1)}, u32[]{:S(2)}, u32[]{:S(2)}) collective-permute-start(f32[4,32,128]{2,1,0:T(8,128)S(1)} %get-tuple-element.37.refs_2_), channel_id=1, source_target_pairs={{0,4},{4,0},{8,12},{12,8},{1,5},{5,1},{9,13},{13,9},{2,6},{6,2},{1... | collective-permute-start | bytes 196616 | tf_op jit(solution)/shard_map/ppermute | solution.py:485
  21.0 1.5 %collective-permute-start.9 = (f32[12,32,128]{2,1,0:T(8,128)S(1)}, f32[12,32,128]{2,1,0:T(8,128)S(1)}, u32[]{:S(2)}, u32[]{:S(2)}) collective-permute-start(f32[12,32,128]{2,1,0:T(8,128)S(1)} %get-tuple-element.47.own), channel_id=1, source_target_pairs={{0,4},{4,0},{8,12},{12,8},{1,5},{5,1},{9,13},{13,9},{2,6},{6,2},{1... | collective-permute-start | bytes 589832 | tf_op jit(solution)/shard_map/ppermute | solution.py:485
  22.8 4.9 %collective-permute-start.10 = (f32[12,16,128]{2,1,0:T(8,128)S(1)}, f32[12,16,128]{2,1,0:T(8,128)S(1)}, u32[]{:S(2)}, u32[]{:S(2)}) collective-permute-start(f32[12,16,128]{2,1,0:T(8,128)S(1)} %get-tuple-element.49), channel_id=1, source_target_pairs={{0,8},{4,12},{8,0},{12,4},{1,9},{5,13},{9,1},{13,5},{2,10},{6,14},... | collective-permute-start | bytes 294920 | tf_op jit(solution)/shard_map/ppermute | solution.py:485

commit v5 on v4

--- a/solution.py
+++ b/solution.py
@@ -348,13 +348,15 @@
     return pltpu.roll(cells, 1, 1)
 
 
-def swept(cells, shares, total_rows, depth_cells):
+def swept(cells, shares, held, total_rows, depth_cells):
     up_x, down_x, up_y, down_y, up_z, down_z, kept = [
         ref[...].reshape(cells.shape) for ref in shares
     ]
+    rows = cells.shape[0]
+    held[ROWS : ROWS + rows] = cells
     return (
         (up_z * up_depth(cells) + down_z * down_depth(cells))
-        + (up_x * up_rows(cells) + down_x * down_rows(cells))
+        + (up_x * held[ROWS + 1 : ROWS + 1 + rows] + down_x * held[ROWS - 1 : ROWS - 1 + rows])
         + (
             up_y * up_second(cells, total_rows, depth_cells)
             + down_y * down_second(cells, total_rows, depth_cells)
@@ -397,19 +399,21 @@
     recorded,
     *refs,
 ):
-    refs, (estimate, correction) = refs[:-2], refs[-2:]
+    refs, (estimate, correction, shifted) = refs[:-3], refs[-3:]
+    shifted[:ROWS] = jnp.zeros_like(shifted[:ROWS])
+    shifted[-ROWS:] = jnp.zeros_like(shifted[-ROWS:])
     pieces, shares = refs[:-SHARES], refs[-SHARES:]
     pairs = len(pieces) // 2
     part, total_rows, lanes = recorded.shape
     flat = (part * total_rows, lanes)
-    joined = [
-        lax.rsqrt(lax.rsqrt(own[...] * exchanged(other[...], depth_cells)))
-        for own, other in zip(pieces[:pairs], pieces[pairs:])
+    own, other = [
+        jnp.concatenate([piece[...] for piece in half], axis=0)
+        for half in (pieces[:pairs], pieces[pairs:])
     ]
-    joined = jnp.concatenate(joined, axis=0)
+    joined = lax.rsqrt(lax.rsqrt(own * exchanged(other, depth_cells)))
     cells = (recorded[...] * joined).reshape(flat)
     for _ in range(SWEEPS):
-        cells = swept(cells, shares, total_rows, depth_cells)
+        cells = swept(cells, shares, shifted, total_rows, depth_cells)
     estimate[...] = cells.reshape(estimate.shape)
     correction[...] = corrected(
         recorded[...].reshape(flat), cells, blur_band, adjoint_band
@@ -433,14 +437,16 @@
 
 
 def last_kernel(groups, depth_cells, estimate, kept, received, *refs):
-    *shares, out, held = refs
+    *shares, out, held, shifted = refs
+    shifted[:ROWS] = jnp.zeros_like(shifted[:ROWS])
+    shifted[-ROWS:] = jnp.zeros_like(shifted[-ROWS:])
     part, extent, lanes = estimate.shape
     slab = extent - 2 * SWEEPS
     flat = (part * extent, lanes)
     joined = lax.rsqrt(lax.rsqrt(kept[...] * received[...]))
     cells = (estimate[...] * joined).reshape(flat)
     for _ in range(SWEEPS):
-        cells = swept(cells, shares, extent, depth_cells)
+        cells = swept(cells, shares, shifted, extent, depth_cells)
     cells = cells.reshape(part, extent, lanes)[:, SWEEPS : SWEEPS + slab]
     cells = cells.reshape(part * slab, lanes)
     cells = jnp.take_along_axis(cells, lane_order(cells.shape, depth_cells), axis=1)
@@ -500,10 +506,10 @@
         call(blocks_kernel, [two], [], *bands, *blocks[2:])[0],
     ]
     opposite = [swap(cells, 2) for cells in made]
-    pieces = part // groups
+    pieces = 2
     products = call(
         functools.partial(pair_kernel, tiles),
-        [((groups,) + view[1:], f32)] * pieces,
+        [((part // pieces,) + view[1:], f32)] * pieces,
         [],
         *made,
         *opposite,
@@ -526,7 +532,7 @@
     estimate, correction = call(
         functools.partial(second_kernel, depth_cells),
         [(view, f32)] * 2,
-        [],
+        [pltpu.VMEM((part * total_rows + 2 * ROWS, LANES), f32)],
         *bands,
         recorded,
         *products,
@@ -548,7 +554,7 @@
     (out,) = call(
         functools.partial(last_kernel, groups, depth_cells),
         [(data.shape, f32)],
-        [pltpu.VMEM(data.shape[1:], f32)],
+        [pltpu.VMEM(data.shape[1:], f32), pltpu.VMEM((part * extent + 2 * ROWS, LANES), f32)],
         near_cells[0],
         kept,
         received,

time: 29.4 us -> 29.2 us (level)
    ppermute x7 -> x6, waiting for transfers between devices: 8.11 us -> 7.78 us  [swap(): return lax.ppermute(cells, 'view', [(i, i ^ bit) for i in range(VIEWS)])]
    ppermute x7 -> x6, starting transfers between devices: 4.38 us -> 4.52 us  [swap(): return lax.ppermute(cells, 'view', [(i, i ^ bit) for i in range(VIEWS)])]
  transfers between devices with their start and end apart: 11 -> 10, of which waited for: 9 -> 8; matrix products, arithmetic and copies ran while one was open for 0% -> 0% of each run, Pallas kernels for 5% -> 5%
where the time goes in v5:
time: 29.2 us; the launch traced here: 29.1 us
  starting transfers between devices  11.8 us (40%)
  waiting for transfers between devices  11.2 us (38%)
  Pallas kernels  3.97 us (14%)
  local copies, waits for them, and re-layouts  2.03 us (7%)
    ppermute x6, waiting for transfers between devices, swap(): return lax.ppermute(cells, 'view', [(i, i ^ bit) for i in range(VIEWS)])  7.78 us
    ppermute x4, starting transfers between devices, across(): return lax.ppermute(cells, 'tile', [(i, i ^ k) for i in range(tiles)])  7.29 us
    ppermute x6, starting transfers between devices, swap(): return lax.ppermute(cells, 'view', [(i, i ^ bit) for i in range(VIEWS)])  4.52 us
    pallas_call x12, Pallas kernels, call(): pl.pallas_call(body, out_shape=shapes, in_specs=[vmem] * len(args), out_s...  3.97 us
    ppermute x4, waiting for transfers between devices, across(): return lax.ppermute(cells, 'tile', [(i, i ^ k) for i in range(tiles)])  3.39 us
    unnamed x9, local copies, waits for them, and re-layouts  1.26 us
    pallas_call x1, local copies, waits for them, and re-layouts, call(): pl.pallas_call(body, out_shape=shapes, in_specs=[vmem] * len(args), out_s...  0.77 us
  transfers between devices with their start and end apart: 10, of which 8 were waited for; matrix products, arithmetic and copies ran while one was open for 0% of the time, Pallas kernels for 5%

profile of v5, /device:TPU:0, one launch (start us, length us, event | category | flops | bytes accessed | tf_op | source)
XLA Modules:
  0.0 29.1 jit_solution(1993968425653512690)
XLA Ops:
  0.0 0.0 copy-start.1
  0.0 1.0 %copy.6.data = f32[1,8,48,32]{3,2,1,0:T(8,128)S(1)} copy(f32[1,8,48,32]{2,3,1,0:T(8,128)} %param.4) | data formatting | bytes 98304 | tf_op args[0]
  1.1 0.0 copy-done.1
  1.1 0.1 copy.7.labels
  1.2 0.0 copy-start.2
  1.2 0.3 shard_map.47
  1.5 5.1 %collective-permute-start.2 = (f32[24,8,128]{2,1,0:T(8,128)S(1)}, f32[24,8,128]{2,1,0:T(8,128)S(1)}, u32[]{:S(2)}, u32[]{:S(2)}) collective-permute-start(f32[24,8,128]{2,1,0:T(8,128)S(1)} %get-tuple-element.33.own_both), channel_id=1, source_target_pairs={{0,3},{1,2},{2,1},{3,0},{4,7},{5,6},{6,5},{7,4},{8,11},{9,10},{10,... | collective-permute-start | bytes 294920 | tf_op jit(solution)/shard_map/ppermute | solution.py:488
  6.6 0.0 copy-start
  6.6 0.0 collective-permute-start
  6.6 0.6 %collective-permute-start.1 = (f32[12,8,128]{2,1,0:T(8,128)S(1)}, f32[12,8,128]{2,1,0:T(8,128)S(1)}, u32[]{:S(2)}, u32[]{:S(2)}) collective-permute-start(f32[12,8,128]{2,1,0:T(8,128)S(1)} %get-tuple-element.32.refs_0_), channel_id=1, source_target_pairs={{0,2},{1,3},{2,0},{3,1},{4,6},{5,7},{6,4},{7,5},{8,10},{9,11},{10,... | collective-permute-start | bytes 147464 | tf_op jit(solution)/shard_map/ppermute | solution.py:488
  7.2 0.0 copy-done.2
  7.2 0.1 copy.5.kernel
  7.3 0.0 copy-done
  7.3 0.5 %shard_map.46 = (bf16[256,256]{1,0:T(8,128)(2,1)S(1)}, bf16[256,256]{1,0:T(8,128)(2,1)S(1)}) custom-call(f32[1,32,9]{2,1,0:T(8,128)S(1)} %copy.5.kernel, s32[1,32]{1,0:T(1,128)S(1)} %copy-done), custom_call_target="tpu_custom_call" | custom-call | tf_op jit(solution)/shard_map/pallas_call | solution.py:478
  7.8 3.2 %collective-permute-done.refs_1_ = f32[12,8,128]{2,1,0:T(8,128)S(1)} collective-permute-done((f32[12,8,128]{2,1,0:T(8,128)S(1)}, f32[12,8,128]{2,1,0:T(8,128)S(1)}, u32[]{:S(2)}, u32[]{:S(2)}) %collective-permute-start) | collective-permute-done | bytes 49184 | tf_op jit(solution)/shard_map/ppermute | solution.py:488
  11.0 0.3 %shard_map.49.refs_0_ = f32[24,8,128]{2,1,0:T(8,128)S(1)} custom-call(bf16[256,256]{1,0:T(8,128)(2,1)S(1)} %get-tuple-element.30.blur_band, bf16[256,256]{1,0:T(8,128)(2,1)S(1)} %get-tuple-element.31.adjoint_band, f32[12,8,128]{2,1,0:T(8,128)S(1)} %get-tuple-element.32.refs_0_, f32[12,8,128]{2,1,0:T(8,128)S(1)} %collective-permute-done.refs_1_), custom_call_target="tpu_custom_call" | custom-call | tf_op jit(solution)/shard_map/pallas_call | solution.py:478
  11.4 1.6 %collective-permute-start.3 = (f32[24,8,128]{2,1,0:T(8,128)S(1)}, f32[24,8,128]{2,1,0:T(8,128)S(1)}, u32[]{:S(2)}, u32[]{:S(2)}) collective-permute-start(f32[24,8,128]{2,1,0:T(8,128)S(1)} %shard_map.49.refs_0_), channel_id=1, source_target_pairs={{0,8},{4,12},{8,0},{12,4},{1,9},{5,13},{9,1},{13,5},{2,10},{6,14},... | collective-permute-start | bytes 294920 | tf_op jit(solution)/shard_map/ppermute | solution.py:491
  13.0 0.0 collective-permute-done.1.refs_2_.refs_0_
  13.0 0.0 collective-permute-done.2.refs_3_.refs_1_.both
  13.0 0.3 %shard_map.50.refs_1_ = f32[24,8,128]{2,1,0:T(8,128)S(1)} custom-call(bf16[256,256]{1,0:T(8,128)(2,1)S(1)} %get-tuple-element.30.blur_band, bf16[256,256]{1,0:T(8,128)(2,1)S(1)} %get-tuple-element.31.adjoint_band, f32[12,8,128]{2,1,0:T(8,128)S(1)} %collective-permute-done.1.refs_2_.refs_0_, f32[24,8,128]{2,1,0:T(8,128)S(1)} %collective-permute-done.2.refs_3_.refs_1_.both), custom_call_target="tpu_custom_call" | custom-call | tf_op jit(solution)/shard_map/pallas_call | solution.py:478
  13.3 0.8 %collective-permute-start.4 = (f32[24,8,128]{2,1,0:T(8,128)S(1)}, f32[24,8,128]{2,1,0:T(8,128)S(1)}, u32[]{:S(2)}, u32[]{:S(2)}) collective-permute-start(f32[24,8,128]{2,1,0:T(8,128)S(1)} %shard_map.50.refs_1_), channel_id=1, source_target_pairs={{0,8},{4,12},{8,0},{12,4},{1,9},{5,13},{9,1},{13,5},{2,10},{6,14},... | collective-permute-start | bytes 294920 | tf_op jit(solution)/shard_map/ppermute | solution.py:491
  14.1 1.5 %collective-permute-start.7 = (f32[24,8,128]{2,1,0:T(8,128)S(1)}, f32[24,8,128]{2,1,0:T(8,128)S(1)}, u32[]{:S(2)}, u32[]{:S(2)}) collective-permute-start(f32[24,8,128]{2,1,0:T(8,128)S(1)} %shard_map.52.near), channel_id=1, source_target_pairs={{0,1},{1,0},{2,3},{3,2},{4,5},{5,4},{6,7},{7,6},{8,9},{9,8},{10,11... | collective-permute-start | bytes 294920 | tf_op jit(solution)/shard_map/ppermute | solution.py:488
  15.6 1.1 %collective-permute-done.3.refs_2_ = f32[24,8,128]{2,1,0:T(8,128)S(1)} collective-permute-done((f32[24,8,128]{2,1,0:T(8,128)S(1)}, f32[24,8,128]{2,1,0:T(8,128)S(1)}, u32[]{:S(2)}, u32[]{:S(2)}) %collective-permute-start.3) | collective-permute-done | bytes 98336 | tf_op jit(solution)/shard_map/ppermute | solution.py:491
  16.8 1.2 %collective-permute-done.4.refs_3_ = f32[24,8,128]{2,1,0:T(8,128)S(1)} collective-permute-done((f32[24,8,128]{2,1,0:T(8,128)S(1)}, f32[24,8,128]{2,1,0:T(8,128)S(1)}, u32[]{:S(2)}, u32[]{:S(2)}) %collective-permute-start.4) | collective-permute-done | bytes 98336 | tf_op jit(solution)/shard_map/ppermute | solution.py:491
  18.0 0.1 collective-permute-start.5
  18.1 0.5 %collective-permute-start.6 = (f32[6,32,128]{2,1,0:T(8,128)S(1)}, f32[6,32,128]{2,1,0:T(8,128)S(1)}, u32[]{:S(2)}, u32[]{:S(2)}) collective-permute-start(f32[6,32,128]{2,1,0:T(8,128)S(1)} %get-tuple-element.35.refs_1_), channel_id=1, source_target_pairs={{0,4},{4,0},{8,12},{12,8},{1,5},{5,1},{9,13},{13,9},{2,6},{6,2},{1... | collective-permute-start | bytes 294920 | tf_op jit(solution)/shard_map/ppermute | solution.py:491
  18.6 0.2 collective-permute-done.7.far
  18.8 0.2 shard_map.53
  19.0 0.4 %collective-permute-done.5.refs_2_ = f32[6,32,128]{2,1,0:T(8,128)S(1)} collective-permute-done((f32[6,32,128]{2,1,0:T(8,128)S(1)}, f32[6,32,128]{2,1,0:T(8,128)S(1)}, u32[]{:S(2)}, u32[]{:S(2)}) %collective-permute-start.5) | collective-permute-done | bytes 98336 | tf_op jit(solution)/shard_map/ppermute | solution.py:491
  19.4 0.2 collective-permute-done.6.refs_3_
  19.5 1.1 %shard_map.54 = (f32[12,32,128]{2,1,0:T(8,128)S(1)}, f32[12,32,128]{2,1,0:T(8,128)S(1)}) custom-call(bf16[256,256]{1,0:T(8,128)(2,1)S(1)} %get-tuple-element.30.blur_band, bf16[256,256]{1,0:T(8,128)(2,1)S(1)} %get-tuple-element.31.adjoint_band, f32[12,32,128]{2,1,0:T(8,128)S(1)} %shard_map.48.recorded, f32[6,32,128]{2,1,0:T(8,128)S(1)} %get-tuple-element.34.refs_0_, ...), custom_call_target="tpu_custom_call" | custom-call | tf_op jit(solution)/shard_map/pallas_call | solution.py:478
  20.6 0.4 %collective-permute-start.8 = (f32[12,32,128]{2,1,0:T(8,128)S(1)}, f32[12,32,128]{2,1,0:T(8,128)S(1)}, u32[]{:S(2)}, u32[]{:S(2)}) collective-permute-start(f32[12,32,128]{2,1,0:T(8,128)S(1)} %get-tuple-element.45.own), channel_id=1, source_target_pairs={{0,4},{4,0},{8,12},{12,8},{1,5},{5,1},{9,13},{13,9},{2,6},{6,2},{1... | collective-permute-start | bytes 589832 | tf_op jit(solution)/shard_map/ppermute | solution.py:491
  21.0 1.1 %collective-permute-done.8.other = f32[12,32,128]{2,1,0:T(8,128)S(1)} collective-permute-done((f32[12,32,128]{2,1,0:T(8,128)S(1)}, f32[12,32,128]{2,1,0:T(8,128)S(1)}, u32[]{:S(2)}, u32[]{:S(2)}) %collective-permute-start.8) | collective-permute-done | bytes 196640 | tf_op jit(solution)/shard_map/ppermute | solution.py:491
  22.1 0.3 %shard_map.56 = (f32[12,16,128]{2,1,0:T(8,128)S(1)}, f32[12,16,128]{2,1,0:T(8,128)S(1)}) custom-call(f32[12,32,128]{2,1,0:T(8,128)S(1)} %get-tuple-element.45.own, f32[12,32,128]{2,1,0:T(8,128)S(1)} %collective-permute-done.8.other), custom_call_target="tpu_custom_call" | custom-call | tf_op jit(solution)/shard_map/pallas_call | solution.py:478
  22.5 1.1 %collective-permute-start.9 = (f32[12,16,128]{2,1,0:T(8,128)S(1)}, f32[12,16,128]{2,1,0:T(8,128)S(1)}, u32[]{:S(2)}, u32[]{:S(2)}) collective-permute-start(f32[12,16,128]{2,1,0:T(8,128)S(1)} %get-tuple-element.47), channel_id=1, source_target_pairs={{0,8},{4,12},{8,0},{12,4},{1,9},{5,13},{9,1},{13,5},{2,10},{6,14},... | collective-permute-start | bytes 294920 | tf_op jit(solution)/shard_map/ppermute | solution.py:491
  23.6 0.2 shard_map.55
  23.8 3.8 %collective-permute-done.9.received = f32[12,16,128]{2,1,0:T(8,128)S(1)} collective-permute-done((f32[12,16,128]{2,1,0:T(8,128)S(1)}, f32[12,16,128]{2,1,0:T(8,128)S(1)}, u32[]{:S(2)}, u32[]{:S(2)}) %collective-permute-start.9) | collective-permute-done | bytes 98336 | tf_op jit(solution)/shard_map/ppermute | solution.py:491
  27.6 0.7 %shard_map.57 = f32[1,8,48,32]{3,2,1,0:T(8,128)S(1)} custom-call(f32[12,16,128]{2,1,0:T(8,128)S(1)} %get-tuple-element.44.estimate, f32[12,16,128]{2,1,0:T(8,128)S(1)} %get-tuple-element.46.kept, f32[12,16,128]{2,1,0:T(8,128)S(1)} %collective-permute-done.9.received, f32[12,16,128]{2,1,0:T(8,128)S(1)} %get-tuple-element.48.refs_0_, ...), custom_call_target="tpu_custom_call" | custom-call | tf_op jit(solution)/shard_map/pallas_call | solution.py:478
  28.3 0.8 %copy.8 = f32[1,8,48,32]{2,3,1,0:T(8,128)} copy(f32[1,8,48,32]{3,2,1,0:T(8,128)S(1)} %shard_map.57) | data formatting | bytes 98304 | tf_op jit(solution)/shard_map/pallas_call | solution.py:478
  (3 shorter events, 0.1 us)
Async XLA Ops:
  0.0 1.1 %copy-start.1 = (s32[1,8,48,32]{2,3,1,0:T(8,128)S(1)}, s32[1,8,48,32]{2,3,1,0:T(8,128)}, u32[]{:S(2)}) copy-start(s32[1,8,48,32]{2,3,1,0:T(8,128)} %param.5) | copy-start | bytes 147460
  1.2 6.0 %copy-start.2 = (f32[1,32,9]{1,0,2:T(1,128)S(1)}, f32[1,32,9]{1,0,2:T(1,128)}, u32[]{:S(2)}) copy-start(f32[1,32,9]{1,0,2:T(1,128)} %param.6) | copy-start | bytes 3460
  1.5 11.5 %collective-permute-start.2 = (f32[24,8,128]{2,1,0:T(8,128)S(1)}, f32[24,8,128]{2,1,0:T(8,128)S(1)}, u32[]{:S(2)}, u32[]{:S(2)}) collective-permute-start(f32[24,8,128]{2,1,0:T(8,128)S(1)} %get-tuple-element.33.own_both), channel_id=1, source_target_pairs={{0,3},{1,2},{2,1},{3,0},{4,7},{5,6},{6,5},{7,4},{8,11},{9,10},{10,... | collective-permute-start | bytes 294920 | tf_op jit(solution)/shard_map/ppermute | solution.py:488
  6.6 0.7 %copy-start = (s32[1,32]{1,0:T(1,128)S(1)}, s32[1,32]{1,0:T(1,128)}, u32[]{:S(2)}) copy-start(s32[1,32]{1,0:T(1,128)} %offsets.1) | copy-start | bytes 388
  6.6 4.5 %collective-permute-start = (f32[12,8,128]{2,1,0:T(8,128)S(1)}, f32[12,8,128]{2,1,0:T(8,128)S(1)}, u32[]{:S(2)}, u32[]{:S(2)}) collective-permute-start(f32[12,8,128]{2,1,0:T(8,128)S(1)} %get-tuple-element.32.refs_0_), channel_id=1, source_target_pairs={{0,1},{1,0},{2,3},{3,2},{4,5},{5,4},{6,7},{7,6},{8,9},{9,8},{10,11... | collective-permute-start | bytes 147464 | tf_op jit(solution)/shard_map/ppermute | solution.py:488
  6.6 6.4 %collective-permute-start.1 = (f32[12,8,128]{2,1,0:T(8,128)S(1)}, f32[12,8,128]{2,1,0:T(8,128)S(1)}, u32[]{:S(2)}, u32[]{:S(2)}) collective-permute-start(f32[12,8,128]{2,1,0:T(8,128)S(1)} %get-tuple-element.32.refs_0_), channel_id=1, source_target_pairs={{0,2},{1,3},{2,0},{3,1},{4,6},{5,7},{6,4},{7,5},{8,10},{9,11},{10,... | collective-permute-start | bytes 147464 | tf_op jit(solution)/shard_map/ppermute | solution.py:488
  11.4 5.4 %collective-permute-start.3 = (f32[24,8,128]{2,1,0:T(8,128)S(1)}, f32[24,8,128]{2,1,0:T(8,128)S(1)}, u32[]{:S(2)}, u32[]{:S(2)}) collective-permute-start(f32[24,8,128]{2,1,0:T(8,128)S(1)} %shard_map.49.refs_0_), channel_id=1, source_target_pairs={{0,8},{4,12},{8,0},{12,4},{1,9},{5,13},{9,1},{13,5},{2,10},{6,14},... | collective-permute-start | bytes 294920 | tf_op jit(solution)/shard_map/ppermute | solution.py:491
  13.3 4.7 %collective-permute-start.4 = (f32[24,8,128]{2,1,0:T(8,128)S(1)}, f32[24,8,128]{2,1,0:T(8,128)S(1)}, u32[]{:S(2)}, u32[]{:S(2)}) collective-permute-start(f32[24,8,128]{2,1,0:T(8,128)S(1)} %shard_map.50.refs_1_), channel_id=1, source_target_pairs={{0,8},{4,12},{8,0},{12,4},{1,9},{5,13},{9,1},{13,5},{2,10},{6,14},... | collective-permute-start | bytes 294920 | tf_op jit(solution)/shard_map/ppermute | solution.py:491
  14.1 4.7 %collective-permute-start.7 = (f32[24,8,128]{2,1,0:T(8,128)S(1)}, f32[24,8,128]{2,1,0:T(8,128)S(1)}, u32[]{:S(2)}, u32[]{:S(2)}) collective-permute-start(f32[24,8,128]{2,1,0:T(8,128)S(1)} %shard_map.52.near), channel_id=1, source_target_pairs={{0,1},{1,0},{2,3},{3,2},{4,5},{5,4},{6,7},{7,6},{8,9},{9,8},{10,11... | collective-permute-start | bytes 294920 | tf_op jit(solution)/shard_map/ppermute | solution.py:488
  18.0 1.4 %collective-permute-start.5 = (f32[6,32,128]{2,1,0:T(8,128)S(1)}, f32[6,32,128]{2,1,0:T(8,128)S(1)}, u32[]{:S(2)}, u32[]{:S(2)}) collective-permute-start(f32[6,32,128]{2,1,0:T(8,128)S(1)} %get-tuple-element.34.refs_0_), channel_id=1, source_target_pairs={{0,4},{4,0},{8,12},{12,8},{1,5},{5,1},{9,13},{13,9},{2,6},{6,2},{1... | collective-permute-start | bytes 294920 | tf_op jit(solution)/shard_map/ppermute | solution.py:491
  18.1 1.4 %collective-permute-start.6 = (f32[6,32,128]{2,1,0:T(8,128)S(1)}, f32[6,32,128]{2,1,0:T(8,128)S(1)}, u32[]{:S(2)}, u32[]{:S(2)}) collective-permute-start(f32[6,32,128]{2,1,0:T(8,128)S(1)} %get-tuple-element.35.refs_1_), channel_id=1, source_target_pairs={{0,4},{4,0},{8,12},{12,8},{1,5},{5,1},{9,13},{13,9},{2,6},{6,2},{1... | collective-permute-start | bytes 294920 | tf_op jit(solution)/shard_map/ppermute | solution.py:491
  20.6 1.5 %collective-permute-start.8 = (f32[12,32,128]{2,1,0:T(8,128)S(1)}, f32[12,32,128]{2,1,0:T(8,128)S(1)}, u32[]{:S(2)}, u32[]{:S(2)}) collective-permute-start(f32[12,32,128]{2,1,0:T(8,128)S(1)} %get-tuple-element.45.own), channel_id=1, source_target_pairs={{0,4},{4,0},{8,12},{12,8},{1,5},{5,1},{9,13},{13,9},{2,6},{6,2},{1... | collective-permute-start | bytes 589832 | tf_op jit(solution)/shard_map/ppermute | solution.py:491
  22.5 5.1 %collective-permute-start.9 = (f32[12,16,128]{2,1,0:T(8,128)S(1)}, f32[12,16,128]{2,1,0:T(8,128)S(1)}, u32[]{:S(2)}, u32[]{:S(2)}) collective-permute-start(f32[12,16,128]{2,1,0:T(8,128)S(1)} %get-tuple-element.47), channel_id=1, source_target_pairs={{0,8},{4,12},{8,0},{12,4},{1,9},{5,13},{9,1},{13,5},{2,10},{6,14},... | collective-permute-start | bytes 294920 | tf_op jit(solution)/shard_map/ppermute | solution.py:491

commit v6 on v5

--- a/solution.py
+++ b/solution.py
@@ -190,7 +190,7 @@
     return high, (cells - high.astype(jnp.float32)).astype(jnp.bfloat16)
 
 
-def band_kernel(kernel, offsets, blur_out, adjoint_out):
+def band_kernel(kernel, offsets, blur_out, adjoint_out, turned_out):
     depth_cells, taps = kernel.shape[1:]
     span = blur_out.shape[0] // 2
     turn = depth_reversed()
@@ -224,6 +224,9 @@
         for half in range(2):
             out[half * span : (half + 1) * span, :span] = high
             out[half * span : (half + 1) * span, span:] = low
+    for half, cells in enumerate(split(matrix.T)):
+        turned_out[half * span : (half + 1) * span, :span] = cells
+        turned_out[half * span : (half + 1) * span, span:] = cells
 
 
 def banded(cells, band):
@@ -368,14 +371,23 @@
 def exchanged(cells, depth_cells):
     part, rows, lanes = cells.shape
     groups = lanes // depth_cells
+    turned = [
+        cells[first : first + groups].reshape(groups * rows, lanes).T
+        for first in range(0, part, groups)
+    ]
+    return regrouped(turned, rows, depth_cells)
+
+
+def regrouped(turned, rows, depth_cells):
+    lanes = turned[0].shape[1]
+    groups = lanes // depth_cells
     lane_group = lax.broadcasted_iota(jnp.int32, (rows, lanes), 1) // depth_cells
     out = []
-    for first in range(0, part, groups):
-        turned = cells[first : first + groups].reshape(groups * rows, lanes).T
+    for cells in turned:
         for a in range(groups):
             plane = None
             for b in range(groups):
-                piece = turned[b * rows : (b + 1) * rows]
+                piece = cells[b * rows : (b + 1) * rows]
                 moved = (b - a) % groups * depth_cells
                 if moved:
                     piece = pltpu.roll(piece, moved, 1)
@@ -396,10 +408,11 @@
     depth_cells,
     blur_band,
     adjoint_band,
+    turned_band,
     recorded,
     *refs,
 ):
-    refs, (estimate, correction, shifted) = refs[:-3], refs[-3:]
+    refs, (estimate, correction, turned, shifted) = refs[:-4], refs[-4:]
     shifted[:ROWS] = jnp.zeros_like(shifted[:ROWS])
     shifted[-ROWS:] = jnp.zeros_like(shifted[-ROWS:])
     pieces, shares = refs[:-SHARES], refs[-SHARES:]
@@ -415,17 +428,23 @@
     for _ in range(SWEEPS):
         cells = swept(cells, shares, shifted, total_rows, depth_cells)
     estimate[...] = cells.reshape(estimate.shape)
-    correction[...] = corrected(
-        recorded[...].reshape(flat), cells, blur_band, adjoint_band
-    ).reshape(correction.shape)
-
-
-def windows_kernel(tiles, depth_cells, own, other, kept, sent, product):
-    product[...] = own[...] * exchanged(other[...], depth_cells)
+    ratio = recorded[...].reshape(flat) / banded(cells, blur_band)
+    both = lax.dot_general(
+        turned_band[...],
+        jnp.concatenate(split(ratio), axis=1),
+        (((1,), (1,)), ((), ())),
+        preferred_element_type=jnp.float32,
+    )
+    both = both[:lanes] + both[lanes:]
+    both = [both[:, first : first + lanes] for first in range(0, both.shape[1], lanes)]
+    turned[...] = regrouped(both, total_rows, depth_cells)
+    correction[...] = banded(ratio, adjoint_band).reshape(correction.shape)
+
+
+def windows_kernel(tiles, own, other, sent, product):
+    product[...] = own[...] * other[...]
     slab = product.shape[1] // tiles
-    slot = own_slot(tiles)
-    kept[...] = window(product, slot, tiles, slab, SWEEPS)
-    sent[...] = window(product, tiles - 1 - slot, tiles, slab, SWEEPS)
+    sent[...] = window(product, tiles - 1 - own_slot(tiles), tiles, slab, SWEEPS)
 
 
 def near_kernel(tiles, *refs):
@@ -497,7 +516,9 @@
         data,
         labels,
     )
-    bands = call(band_kernel, [((2 * LANES, 2 * LANES), jnp.bfloat16)] * 2, [], kernel, offsets)
+    *bands, turned_band = call(
+        band_kernel, [((2 * LANES, 2 * LANES), jnp.bfloat16)] * 3, [], kernel, offsets
+    )
     blocks = [packed] + [across(both if k == LABELS_WITH else packed, k) for k in range(1, tiles)]
     two = ((2 * part,) + block[1:], f32)
     (near_labels,) = call(relay_kernel, [two], [], both, blocks[LABELS_WITH])
@@ -529,26 +550,32 @@
         near_labels,
         far_labels,
     )
-    estimate, correction = call(
+    estimate, correction, turned = call(
         functools.partial(second_kernel, depth_cells),
-        [(view, f32)] * 2,
+        [(view, f32)] * 3,
         [pltpu.VMEM((part * total_rows + 2 * ROWS, LANES), f32)],
         *bands,
+        turned_band,
         recorded,
         *products,
         *others,
         *shares,
     )
-    other = swap(correction, 1)
-    near_cells = call(
-        functools.partial(near_kernel, tiles), [(near, f32)] * (1 + SHARES), [], estimate, *shares
-    )
-    kept, sent = call(
-        functools.partial(windows_kernel, tiles, depth_cells),
-        [(near, f32)] * 2,
-        [pltpu.VMEM(view, f32)],
+    other = swap(turned, 1)
+    sent, product = call(
+        functools.partial(windows_kernel, tiles),
+        [(near, f32), (view, f32)],
+        [],
         correction,
         other,
+    )
+    kept, *near_cells = call(
+        functools.partial(near_kernel, tiles),
+        [(near, f32)] * (2 + SHARES),
+        [],
+        product,
+        estimate,
+        *shares,
     )
     received = swap(sent, 2)
     (out,) = call(

time: 29.2 us -> 29.1 us (level)
  transfers between devices with their start and end apart: 10 -> 10, of which waited for: 8 -> 8; matrix products, arithmetic and copies ran while one was open for 0% -> 0% of each run, Pallas kernels for 5% -> 6%
where the time goes in v6:
time: 29.1 us; the launch traced here: 29 us
  starting transfers between devices  11.8 us (41%)
  waiting for transfers between devices  11.1 us (38%)
  Pallas kernels  3.89 us (13%)
  local copies, waits for them, and re-layouts  2.03 us (7%)
    ppermute x6, waiting for transfers between devices, swap(): return lax.ppermute(cells, 'view', [(i, i ^ bit) for i in range(VIEWS)])  7.76 us
    ppermute x4, starting transfers between devices, across(): return lax.ppermute(cells, 'tile', [(i, i ^ k) for i in range(tiles)])  7.29 us
    ppermute x6, starting transfers between devices, swap(): return lax.ppermute(cells, 'view', [(i, i ^ bit) for i in range(VIEWS)])  4.52 us
    pallas_call x12, Pallas kernels, call(): pl.pallas_call(body, out_shape=shapes, in_specs=[vmem] * len(args), out_s...  3.89 us
    ppermute x4, waiting for transfers between devices, across(): return lax.ppermute(cells, 'tile', [(i, i ^ k) for i in range(tiles)])  3.38 us
    unnamed x9, local copies, waits for them, and re-layouts  1.26 us
    pallas_call x1, local copies, waits for them, and re-layouts, call(): pl.pallas_call(body, out_shape=shapes, in_specs=[vmem] * len(args), out_s...  0.77 us
  transfers between devices with their start and end apart: 10, of which 8 were waited for; matrix products, arithmetic and copies ran while one was open for 0% of the time, Pallas kernels for 6%

profile of v6, /device:TPU:0, one launch (start us, length us, event | category | flops | bytes accessed | tf_op | source)
XLA Modules:
  0.0 29.0 jit_solution(8641897854723359857)
XLA Ops:
  0.0 0.0 copy-start.1
  0.0 1.0 %copy.6.data = f32[1,8,48,32]{3,2,1,0:T(8,128)S(1)} copy(f32[1,8,48,32]{2,3,1,0:T(8,128)} %param.4) | data formatting | bytes 98304 | tf_op args[0]
  1.1 0.0 copy-done.1
  1.1 0.1 copy.7.labels
  1.2 0.0 copy-start.2
  1.2 0.3 shard_map.47
  1.5 5.1 %collective-permute-start.2 = (f32[24,8,128]{2,1,0:T(8,128)S(1)}, f32[24,8,128]{2,1,0:T(8,128)S(1)}, u32[]{:S(2)}, u32[]{:S(2)}) collective-permute-start(f32[24,8,128]{2,1,0:T(8,128)S(1)} %get-tuple-element.37.own_both), channel_id=1, source_target_pairs={{0,3},{1,2},{2,1},{3,0},{4,7},{5,6},{6,5},{7,4},{8,11},{9,10},{10,... | collective-permute-start | bytes 294920 | tf_op jit(solution)/shard_map/ppermute | solution.py:507
  6.6 0.0 copy-start
  6.6 0.0 collective-permute-start
  6.6 0.6 %collective-permute-start.1 = (f32[12,8,128]{2,1,0:T(8,128)S(1)}, f32[12,8,128]{2,1,0:T(8,128)S(1)}, u32[]{:S(2)}, u32[]{:S(2)}) collective-permute-start(f32[12,8,128]{2,1,0:T(8,128)S(1)} %get-tuple-element.36.refs_0_), channel_id=1, source_target_pairs={{0,2},{1,3},{2,0},{3,1},{4,6},{5,7},{6,4},{7,5},{8,10},{9,11},{10,... | collective-permute-start | bytes 147464 | tf_op jit(solution)/shard_map/ppermute | solution.py:507
  7.2 0.0 copy-done.2
  7.2 0.1 copy.5.kernel
  7.3 0.0 copy-done
  7.3 0.5 %shard_map.46 = (bf16[256,256]{1,0:T(8,128)(2,1)S(1)}, bf16[256,256]{1,0:T(8,128)(2,1)S(1)}, bf16[256,256]{1,0:T(8,128)(2,1)S(1)}) custom-call(f32[1,32,9]{2,1,0:T(8,128)S(1)} %copy.5.kernel, s32[1,32]{1,0:T(1,128)S(1)} %copy-done), custom_call_target="tpu_custom_call" | custom-call | tf_op jit(solution)/shard_map/pallas_call | solution.py:497
  7.8 3.2 %collective-permute-done.refs_1_ = f32[12,8,128]{2,1,0:T(8,128)S(1)} collective-permute-done((f32[12,8,128]{2,1,0:T(8,128)S(1)}, f32[12,8,128]{2,1,0:T(8,128)S(1)}, u32[]{:S(2)}, u32[]{:S(2)}) %collective-permute-start) | collective-permute-done | bytes 49184 | tf_op jit(solution)/shard_map/ppermute | solution.py:507
  11.0 0.3 %shard_map.49.refs_0_ = f32[24,8,128]{2,1,0:T(8,128)S(1)} custom-call(bf16[256,256]{1,0:T(8,128)(2,1)S(1)} %get-tuple-element.33.blur_band, bf16[256,256]{1,0:T(8,128)(2,1)S(1)} %get-tuple-element.34.adjoint_band, f32[12,8,128]{2,1,0:T(8,128)S(1)} %get-tuple-element.36.refs_0_, f32[12,8,128]{2,1,0:T(8,128)S(1)} %collective-permute-done.refs_1_), custom_call_target="tpu_custom_call" | custom-call | tf_op jit(solution)/shard_map/pallas_call | solution.py:497
  11.4 1.6 %collective-permute-start.3 = (f32[24,8,128]{2,1,0:T(8,128)S(1)}, f32[24,8,128]{2,1,0:T(8,128)S(1)}, u32[]{:S(2)}, u32[]{:S(2)}) collective-permute-start(f32[24,8,128]{2,1,0:T(8,128)S(1)} %shard_map.49.refs_0_), channel_id=1, source_target_pairs={{0,8},{4,12},{8,0},{12,4},{1,9},{5,13},{9,1},{13,5},{2,10},{6,14},... | collective-permute-start | bytes 294920 | tf_op jit(solution)/shard_map/ppermute | solution.py:510
  13.0 0.0 collective-permute-done.1.refs_2_.refs_0_
  13.0 0.0 collective-permute-done.2.refs_3_.refs_1_.both
  13.0 0.3 %shard_map.50.refs_1_ = f32[24,8,128]{2,1,0:T(8,128)S(1)} custom-call(bf16[256,256]{1,0:T(8,128)(2,1)S(1)} %get-tuple-element.33.blur_band, bf16[256,256]{1,0:T(8,128)(2,1)S(1)} %get-tuple-element.34.adjoint_band, f32[12,8,128]{2,1,0:T(8,128)S(1)} %collective-permute-done.1.refs_2_.refs_0_, f32[24,8,128]{2,1,0:T(8,128)S(1)} %collective-permute-done.2.refs_3_.refs_1_.both), custom_call_target="tpu_custom_call" | custom-call | tf_op jit(solution)/shard_map/pallas_call | solution.py:497
  13.3 0.8 %collective-permute-start.4 = (f32[24,8,128]{2,1,0:T(8,128)S(1)}, f32[24,8,128]{2,1,0:T(8,128)S(1)}, u32[]{:S(2)}, u32[]{:S(2)}) collective-permute-start(f32[24,8,128]{2,1,0:T(8,128)S(1)} %shard_map.50.refs_1_), channel_id=1, source_target_pairs={{0,8},{4,12},{8,0},{12,4},{1,9},{5,13},{9,1},{13,5},{2,10},{6,14},... | collective-permute-start | bytes 294920 | tf_op jit(solution)/shard_map/ppermute | solution.py:510
  14.1 1.5 %collective-permute-start.7 = (f32[24,8,128]{2,1,0:T(8,128)S(1)}, f32[24,8,128]{2,1,0:T(8,128)S(1)}, u32[]{:S(2)}, u32[]{:S(2)}) collective-permute-start(f32[24,8,128]{2,1,0:T(8,128)S(1)} %shard_map.52.near), channel_id=1, source_target_pairs={{0,1},{1,0},{2,3},{3,2},{4,5},{5,4},{6,7},{7,6},{8,9},{9,8},{10,11... | collective-permute-start | bytes 294920 | tf_op jit(solution)/shard_map/ppermute | solution.py:507
  15.6 1.1 %collective-permute-done.3.refs_2_ = f32[24,8,128]{2,1,0:T(8,128)S(1)} collective-permute-done((f32[24,8,128]{2,1,0:T(8,128)S(1)}, f32[24,8,128]{2,1,0:T(8,128)S(1)}, u32[]{:S(2)}, u32[]{:S(2)}) %collective-permute-start.3) | collective-permute-done | bytes 98336 | tf_op jit(solution)/shard_map/ppermute | solution.py:510
  16.8 1.2 %collective-permute-done.4.refs_3_ = f32[24,8,128]{2,1,0:T(8,128)S(1)} collective-permute-done((f32[24,8,128]{2,1,0:T(8,128)S(1)}, f32[24,8,128]{2,1,0:T(8,128)S(1)}, u32[]{:S(2)}, u32[]{:S(2)}) %collective-permute-start.4) | collective-permute-done | bytes 98336 | tf_op jit(solution)/shard_map/ppermute | solution.py:510
  18.0 0.1 collective-permute-start.5
  18.1 0.5 %collective-permute-start.6 = (f32[6,32,128]{2,1,0:T(8,128)S(1)}, f32[6,32,128]{2,1,0:T(8,128)S(1)}, u32[]{:S(2)}, u32[]{:S(2)}) collective-permute-start(f32[6,32,128]{2,1,0:T(8,128)S(1)} %get-tuple-element.39.refs_1_), channel_id=1, source_target_pairs={{0,4},{4,0},{8,12},{12,8},{1,5},{5,1},{9,13},{13,9},{2,6},{6,2},{1... | collective-permute-start | bytes 294920 | tf_op jit(solution)/shard_map/ppermute | solution.py:510
  18.6 0.2 collective-permute-done.7.far
  18.8 0.2 shard_map.53
  19.0 0.4 %collective-permute-done.5.refs_2_ = f32[6,32,128]{2,1,0:T(8,128)S(1)} collective-permute-done((f32[6,32,128]{2,1,0:T(8,128)S(1)}, f32[6,32,128]{2,1,0:T(8,128)S(1)}, u32[]{:S(2)}, u32[]{:S(2)}) %collective-permute-start.5) | collective-permute-done | bytes 98336 | tf_op jit(solution)/shard_map/ppermute | solution.py:510
  19.4 0.2 collective-permute-done.6.refs_3_
  19.5 1.3 %shard_map.54 = (f32[12,32,128]{2,1,0:T(8,128)S(1)}, f32[12,32,128]{2,1,0:T(8,128)S(1)}, f32[12,32,128]{2,1,0:T(8,128)S(1)}) custom-call(bf16[256,256]{1,0:T(8,128)(2,1)S(1)} %get-tuple-element.33.blur_band, bf16[256,256]{1,0:T(8,128)(2,1)S(1)} %get-tuple-element.34.adjoint_band, bf16[256,256]{1,0:T(8,128)(2,1)S(1)} %get-tuple-element.35.turned_band, ...), custom_call_target="tpu_custom_call" | custom-call | tf_op jit(solution)/shard_map/pallas_call | solution.py:497
  20.8 0.4 %collective-permute-start.8 = (f32[12,32,128]{2,1,0:T(8,128)S(1)}, f32[12,32,128]{2,1,0:T(8,128)S(1)}, u32[]{:S(2)}, u32[]{:S(2)}) collective-permute-start(f32[12,32,128]{2,1,0:T(8,128)S(1)} %get-tuple-element.48), channel_id=1, source_target_pairs={{0,4},{4,0},{8,12},{12,8},{1,5},{5,1},{9,13},{13,9},{2,6},{6,2},{1... | collective-permute-start | bytes 589832 | tf_op jit(solution)/shard_map/ppermute | solution.py:510
  21.2 1.1 %collective-permute-done.8.other = f32[12,32,128]{2,1,0:T(8,128)S(1)} collective-permute-done((f32[12,32,128]{2,1,0:T(8,128)S(1)}, f32[12,32,128]{2,1,0:T(8,128)S(1)}, u32[]{:S(2)}, u32[]{:S(2)}) %collective-permute-start.8) | collective-permute-done | bytes 196640 | tf_op jit(solution)/shard_map/ppermute | solution.py:510
  22.4 1.2 %collective-permute-start.9 = (f32[12,16,128]{2,1,0:T(8,128)S(1)}, f32[12,16,128]{2,1,0:T(8,128)S(1)}, u32[]{:S(2)}, u32[]{:S(2)}) collective-permute-start(f32[12,16,128]{2,1,0:T(8,128)S(1)} %get-tuple-element.53), channel_id=1, source_target_pairs={{0,8},{4,12},{8,0},{12,4},{1,9},{5,13},{9,1},{13,5},{2,10},{6,14},... | collective-permute-start | bytes 294920 | tf_op jit(solution)/shard_map/ppermute | solution.py:510
  23.5 0.2 shard_map.56
  23.7 3.8 %collective-permute-done.9.received = f32[12,16,128]{2,1,0:T(8,128)S(1)} collective-permute-done((f32[12,16,128]{2,1,0:T(8,128)S(1)}, f32[12,16,128]{2,1,0:T(8,128)S(1)}, u32[]{:S(2)}, u32[]{:S(2)}) %collective-permute-start.9) | collective-permute-done | bytes 98336 | tf_op jit(solution)/shard_map/ppermute | solution.py:510
  27.5 0.7 %shard_map.57 = f32[1,8,48,32]{3,2,1,0:T(8,128)S(1)} custom-call(f32[12,16,128]{2,1,0:T(8,128)S(1)} %get-tuple-element.51.estimate, f32[12,16,128]{2,1,0:T(8,128)S(1)} %get-tuple-element.52.kept, f32[12,16,128]{2,1,0:T(8,128)S(1)} %collective-permute-done.9.received, f32[12,16,128]{2,1,0:T(8,128)S(1)} %get-tuple-element.54.refs_0_, ...), custom_call_target="tpu_custom_call" | custom-call | tf_op jit(solution)/shard_map/pallas_call | solution.py:497
  28.2 0.8 %copy.8 = f32[1,8,48,32]{2,3,1,0:T(8,128)} copy(f32[1,8,48,32]{3,2,1,0:T(8,128)S(1)} %shard_map.57) | data formatting | bytes 98304 | tf_op jit(solution)/shard_map/pallas_call | solution.py:497
  (4 shorter events, 0.1 us)
Async XLA Ops:
  0.0 1.1 %copy-start.1 = (s32[1,8,48,32]{2,3,1,0:T(8,128)S(1)}, s32[1,8,48,32]{2,3,1,0:T(8,128)}, u32[]{:S(2)}) copy-start(s32[1,8,48,32]{2,3,1,0:T(8,128)} %param.5) | copy-start | bytes 147460
  1.2 6.0 %copy-start.2 = (f32[1,32,9]{1,0,2:T(1,128)S(1)}, f32[1,32,9]{1,0,2:T(1,128)}, u32[]{:S(2)}) copy-start(f32[1,32,9]{1,0,2:T(1,128)} %param.6) | copy-start | bytes 3460
  1.5 11.5 %collective-permute-start.2 = (f32[24,8,128]{2,1,0:T(8,128)S(1)}, f32[24,8,128]{2,1,0:T(8,128)S(1)}, u32[]{:S(2)}, u32[]{:S(2)}) collective-permute-start(f32[24,8,128]{2,1,0:T(8,128)S(1)} %get-tuple-element.37.own_both), channel_id=1, source_target_pairs={{0,3},{1,2},{2,1},{3,0},{4,7},{5,6},{6,5},{7,4},{8,11},{9,10},{10,... | collective-permute-start | bytes 294920 | tf_op jit(solution)/shard_map/ppermute | solution.py:507
  6.6 0.7 %copy-start = (s32[1,32]{1,0:T(1,128)S(1)}, s32[1,32]{1,0:T(1,128)}, u32[]{:S(2)}) copy-start(s32[1,32]{1,0:T(1,128)} %offsets.1) | copy-start | bytes 388
  6.6 4.5 %collective-permute-start = (f32[12,8,128]{2,1,0:T(8,128)S(1)}, f32[12,8,128]{2,1,0:T(8,128)S(1)}, u32[]{:S(2)}, u32[]{:S(2)}) collective-permute-start(f32[12,8,128]{2,1,0:T(8,128)S(1)} %get-tuple-element.36.refs_0_), channel_id=1, source_target_pairs={{0,1},{1,0},{2,3},{3,2},{4,5},{5,4},{6,7},{7,6},{8,9},{9,8},{10,11... | collective-permute-start | bytes 147464 | tf_op jit(solution)/shard_map/ppermute | solution.py:507
  6.6 6.4 %collective-permute-start.1 = (f32[12,8,128]{2,1,0:T(8,128)S(1)}, f32[12,8,128]{2,1,0:T(8,128)S(1)}, u32[]{:S(2)}, u32[]{:S(2)}) collective-permute-start(f32[12,8,128]{2,1,0:T(8,128)S(1)} %get-tuple-element.36.refs_0_), channel_id=1, source_target_pairs={{0,2},{1,3},{2,0},{3,1},{4,6},{5,7},{6,4},{7,5},{8,10},{9,11},{10,... | collective-permute-start | bytes 147464 | tf_op jit(solution)/shard_map/ppermute | solution.py:507
  11.4 5.4 %collective-permute-start.3 = (f32[24,8,128]{2,1,0:T(8,128)S(1)}, f32[24,8,128]{2,1,0:T(8,128)S(1)}, u32[]{:S(2)}, u32[]{:S(2)}) collective-permute-start(f32[24,8,128]{2,1,0:T(8,128)S(1)} %shard_map.49.refs_0_), channel_id=1, source_target_pairs={{0,8},{4,12},{8,0},{12,4},{1,9},{5,13},{9,1},{13,5},{2,10},{6,14},... | collective-permute-start | bytes 294920 | tf_op jit(solution)/shard_map/ppermute | solution.py:510
  13.3 4.7 %collective-permute-start.4 = (f32[24,8,128]{2,1,0:T(8,128)S(1)}, f32[24,8,128]{2,1,0:T(8,128)S(1)}, u32[]{:S(2)}, u32[]{:S(2)}) collective-permute-start(f32[24,8,128]{2,1,0:T(8,128)S(1)} %shard_map.50.refs_1_), channel_id=1, source_target_pairs={{0,8},{4,12},{8,0},{12,4},{1,9},{5,13},{9,1},{13,5},{2,10},{6,14},... | collective-permute-start | bytes 294920 | tf_op jit(solution)/shard_map/ppermute | solution.py:510
  14.1 4.7 %collective-permute-start.7 = (f32[24,8,128]{2,1,0:T(8,128)S(1)}, f32[24,8,128]{2,1,0:T(8,128)S(1)}, u32[]{:S(2)}, u32[]{:S(2)}) collective-permute-start(f32[24,8,128]{2,1,0:T(8,128)S(1)} %shard_map.52.near), channel_id=1, source_target_pairs={{0,1},{1,0},{2,3},{3,2},{4,5},{5,4},{6,7},{7,6},{8,9},{9,8},{10,11... | collective-permute-start | bytes 294920 | tf_op jit(solution)/shard_map/ppermute | solution.py:507
  18.0 1.4 %collective-permute-start.5 = (f32[6,32,128]{2,1,0:T(8,128)S(1)}, f32[6,32,128]{2,1,0:T(8,128)S(1)}, u32[]{:S(2)}, u32[]{:S(2)}) collective-permute-start(f32[6,32,128]{2,1,0:T(8,128)S(1)} %get-tuple-element.38.refs_0_), channel_id=1, source_target_pairs={{0,4},{4,0},{8,12},{12,8},{1,5},{5,1},{9,13},{13,9},{2,6},{6,2},{1... | collective-permute-start | bytes 294920 | tf_op jit(solution)/shard_map/ppermute | solution.py:510
  18.1 1.4 %collective-permute-start.6 = (f32[6,32,128]{2,1,0:T(8,128)S(1)}, f32[6,32,128]{2,1,0:T(8,128)S(1)}, u32[]{:S(2)}, u32[]{:S(2)}) collective-permute-start(f32[6,32,128]{2,1,0:T(8,128)S(1)} %get-tuple-element.39.refs_1_), channel_id=1, source_target_pairs={{0,4},{4,0},{8,12},{12,8},{1,5},{5,1},{9,13},{13,9},{2,6},{6,2},{1... | collective-permute-start | bytes 294920 | tf_op jit(solution)/shard_map/ppermute | solution.py:510
  20.8 1.5 %collective-permute-start.8 = (f32[12,32,128]{2,1,0:T(8,128)S(1)}, f32[12,32,128]{2,1,0:T(8,128)S(1)}, u32[]{:S(2)}, u32[]{:S(2)}) collective-permute-start(f32[12,32,128]{2,1,0:T(8,128)S(1)} %get-tuple-element.48), channel_id=1, source_target_pairs={{0,4},{4,0},{8,12},{12,8},{1,5},{5,1},{9,13},{13,9},{2,6},{6,2},{1... | collective-permute-start | bytes 589832 | tf_op jit(solution)/shard_map/ppermute | solution.py:510
  22.4 5.1 %collective-permute-start.9 = (f32[12,16,128]{2,1,0:T(8,128)S(1)}, f32[12,16,128]{2,1,0:T(8,128)S(1)}, u32[]{:S(2)}, u32[]{:S(2)}) collective-permute-start(f32[12,16,128]{2,1,0:T(8,128)S(1)} %get-tuple-element.53), channel_id=1, source_target_pairs={{0,8},{4,12},{8,0},{12,4},{1,9},{5,13},{9,1},{13,5},{2,10},{6,14},... | collective-permute-start | bytes 294920 | tf_op jit(solution)/shard_map/ppermute | solution.py:510

commit v7 on v6

--- a/solution.py
+++ b/solution.py
@@ -239,7 +239,7 @@
 
 
 def corrected(recorded, estimate, blur_band, adjoint_band):
-    return banded(recorded / banded(estimate, blur_band), adjoint_band)
+    return banded(recorded * pl.reciprocal(banded(estimate, blur_band)), adjoint_band)
 
 
 def first_correction(block, blur_band, adjoint_band):
@@ -428,7 +428,7 @@
     for _ in range(SWEEPS):
         cells = swept(cells, shares, shifted, total_rows, depth_cells)
     estimate[...] = cells.reshape(estimate.shape)
-    ratio = recorded[...].reshape(flat) / banded(cells, blur_band)
+    ratio = recorded[...].reshape(flat) * pl.reciprocal(banded(cells, blur_band))
     both = lax.dot_general(
         turned_band[...],
         jnp.concatenate(split(ratio), axis=1),

time: 29.1 us -> 29.1 us (level)
  no operation moved by 1% of the time
where the time goes in v7:
time: 29.1 us; the launch traced here: 29 us
  starting transfers between devices  11.8 us (41%)
  waiting for transfers between devices  11.1 us (38%)
  Pallas kernels  3.89 us (13%)
  local copies, waits for them, and re-layouts  2.03 us (7%)
    ppermute x6, waiting for transfers between devices, swap(): return lax.ppermute(cells, 'view', [(i, i ^ bit) for i in range(VIEWS)])  7.76 us
    ppermute x4, starting transfers between devices, across(): return lax.ppermute(cells, 'tile', [(i, i ^ k) for i in range(tiles)])  7.29 us
    ppermute x6, starting transfers between devices, swap(): return lax.ppermute(cells, 'view', [(i, i ^ bit) for i in range(VIEWS)])  4.52 us
    pallas_call x12, Pallas kernels, call(): pl.pallas_call(body, out_shape=shapes, in_specs=[vmem] * len(args), out_s...  3.89 us
    ppermute x4, waiting for transfers between devices, across(): return lax.ppermute(cells, 'tile', [(i, i ^ k) for i in range(tiles)])  3.38 us
    unnamed x9, local copies, waits for them, and re-layouts  1.26 us
    pallas_call x1, local copies, waits for them, and re-layouts, call(): pl.pallas_call(body, out_shape=shapes, in_specs=[vmem] * len(args), out_s...  0.77 us
  transfers between devices with their start and end apart: 10, of which 8 were waited for; matrix products, arithmetic and copies ran while one was open for 0% of the time, Pallas kernels for 6%

profile of v7, /device:TPU:0, one launch (start us, length us, event | category | flops | bytes accessed | tf_op | source)
XLA Modules:
  0.0 29.0 jit_solution(8641897854723359857)
XLA Ops:
  0.0 0.0 copy-start.1
  0.0 1.0 %copy.6.data = f32[1,8,48,32]{3,2,1,0:T(8,128)S(1)} copy(f32[1,8,48,32]{2,3,1,0:T(8,128)} %param.4) | data formatting | bytes 98304 | tf_op args[0]
  1.1 0.0 copy-done.1
  1.1 0.1 copy.7.labels
  1.2 0.0 copy-start.2
  1.2 0.3 shard_map.47
  1.5 5.1 %collective-permute-start.2 = (f32[24,8,128]{2,1,0:T(8,128)S(1)}, f32[24,8,128]{2,1,0:T(8,128)S(1)}, u32[]{:S(2)}, u32[]{:S(2)}) collective-permute-start(f32[24,8,128]{2,1,0:T(8,128)S(1)} %get-tuple-element.37.own_both), channel_id=1, source_target_pairs={{0,3},{1,2},{2,1},{3,0},{4,7},{5,6},{6,5},{7,4},{8,11},{9,10},{10,... | collective-permute-start | bytes 294920 | tf_op jit(solution)/shard_map/ppermute | solution.py:507
  6.6 0.0 copy-start
  6.6 0.0 collective-permute-start
  6.6 0.6 %collective-permute-start.1 = (f32[12,8,128]{2,1,0:T(8,128)S(1)}, f32[12,8,128]{2,1,0:T(8,128)S(1)}, u32[]{:S(2)}, u32[]{:S(2)}) collective-permute-start(f32[12,8,128]{2,1,0:T(8,128)S(1)} %get-tuple-element.36.refs_0_), channel_id=1, source_target_pairs={{0,2},{1,3},{2,0},{3,1},{4,6},{5,7},{6,4},{7,5},{8,10},{9,11},{10,... | collective-permute-start | bytes 147464 | tf_op jit(solution)/shard_map/ppermute | solution.py:507
  7.2 0.0 copy-done.2
  7.2 0.1 copy.5.kernel
  7.3 0.0 copy-done
  7.3 0.5 %shard_map.46 = (bf16[256,256]{1,0:T(8,128)(2,1)S(1)}, bf16[256,256]{1,0:T(8,128)(2,1)S(1)}, bf16[256,256]{1,0:T(8,128)(2,1)S(1)}) custom-call(f32[1,32,9]{2,1,0:T(8,128)S(1)} %copy.5.kernel, s32[1,32]{1,0:T(1,128)S(1)} %copy-done), custom_call_target="tpu_custom_call" | custom-call | tf_op jit(solution)/shard_map/pallas_call | solution.py:497
  7.8 3.2 %collective-permute-done.refs_1_ = f32[12,8,128]{2,1,0:T(8,128)S(1)} collective-permute-done((f32[12,8,128]{2,1,0:T(8,128)S(1)}, f32[12,8,128]{2,1,0:T(8,128)S(1)}, u32[]{:S(2)}, u32[]{:S(2)}) %collective-permute-start) | collective-permute-done | bytes 49184 | tf_op jit(solution)/shard_map/ppermute | solution.py:507
  11.0 0.3 %shard_map.49.refs_0_ = f32[24,8,128]{2,1,0:T(8,128)S(1)} custom-call(bf16[256,256]{1,0:T(8,128)(2,1)S(1)} %get-tuple-element.33.blur_band, bf16[256,256]{1,0:T(8,128)(2,1)S(1)} %get-tuple-element.34.adjoint_band, f32[12,8,128]{2,1,0:T(8,128)S(1)} %get-tuple-element.36.refs_0_, f32[12,8,128]{2,1,0:T(8,128)S(1)} %collective-permute-done.refs_1_), custom_call_target="tpu_custom_call" | custom-call | tf_op jit(solution)/shard_map/pallas_call | solution.py:497
  11.4 1.6 %collective-permute-start.3 = (f32[24,8,128]{2,1,0:T(8,128)S(1)}, f32[24,8,128]{2,1,0:T(8,128)S(1)}, u32[]{:S(2)}, u32[]{:S(2)}) collective-permute-start(f32[24,8,128]{2,1,0:T(8,128)S(1)} %shard_map.49.refs_0_), channel_id=1, source_target_pairs={{0,8},{4,12},{8,0},{12,4},{1,9},{5,13},{9,1},{13,5},{2,10},{6,14},... | collective-permute-start | bytes 294920 | tf_op jit(solution)/shard_map/ppermute | solution.py:510
  13.0 0.0 collective-permute-done.1.refs_2_.refs_0_
  13.0 0.0 collective-permute-done.2.refs_3_.refs_1_.both
  13.0 0.3 %shard_map.50.refs_1_ = f32[24,8,128]{2,1,0:T(8,128)S(1)} custom-call(bf16[256,256]{1,0:T(8,128)(2,1)S(1)} %get-tuple-element.33.blur_band, bf16[256,256]{1,0:T(8,128)(2,1)S(1)} %get-tuple-element.34.adjoint_band, f32[12,8,128]{2,1,0:T(8,128)S(1)} %collective-permute-done.1.refs_2_.refs_0_, f32[24,8,128]{2,1,0:T(8,128)S(1)} %collective-permute-done.2.refs_3_.refs_1_.both), custom_call_target="tpu_custom_call" | custom-call | tf_op jit(solution)/shard_map/pallas_call | solution.py:497
  13.3 0.8 %collective-permute-start.4 = (f32[24,8,128]{2,1,0:T(8,128)S(1)}, f32[24,8,128]{2,1,0:T(8,128)S(1)}, u32[]{:S(2)}, u32[]{:S(2)}) collective-permute-start(f32[24,8,128]{2,1,0:T(8,128)S(1)} %shard_map.50.refs_1_), channel_id=1, source_target_pairs={{0,8},{4,12},{8,0},{12,4},{1,9},{5,13},{9,1},{13,5},{2,10},{6,14},... | collective-permute-start | bytes 294920 | tf_op jit(solution)/shard_map/ppermute | solution.py:510
  14.1 1.5 %collective-permute-start.7 = (f32[24,8,128]{2,1,0:T(8,128)S(1)}, f32[24,8,128]{2,1,0:T(8,128)S(1)}, u32[]{:S(2)}, u32[]{:S(2)}) collective-permute-start(f32[24,8,128]{2,1,0:T(8,128)S(1)} %shard_map.52.near), channel_id=1, source_target_pairs={{0,1},{1,0},{2,3},{3,2},{4,5},{5,4},{6,7},{7,6},{8,9},{9,8},{10,11... | collective-permute-start | bytes 294920 | tf_op jit(solution)/shard_map/ppermute | solution.py:507
  15.6 1.1 %collective-permute-done.3.refs_2_ = f32[24,8,128]{2,1,0:T(8,128)S(1)} collective-permute-done((f32[24,8,128]{2,1,0:T(8,128)S(1)}, f32[24,8,128]{2,1,0:T(8,128)S(1)}, u32[]{:S(2)}, u32[]{:S(2)}) %collective-permute-start.3) | collective-permute-done | bytes 98336 | tf_op jit(solution)/shard_map/ppermute | solution.py:510
  16.8 1.2 %collective-permute-done.4.refs_3_ = f32[24,8,128]{2,1,0:T(8,128)S(1)} collective-permute-done((f32[24,8,128]{2,1,0:T(8,128)S(1)}, f32[24,8,128]{2,1,0:T(8,128)S(1)}, u32[]{:S(2)}, u32[]{:S(2)}) %collective-permute-start.4) | collective-permute-done | bytes 98336 | tf_op jit(solution)/shard_map/ppermute | solution.py:510
  18.0 0.1 collective-permute-start.5
  18.1 0.5 %collective-permute-start.6 = (f32[6,32,128]{2,1,0:T(8,128)S(1)}, f32[6,32,128]{2,1,0:T(8,128)S(1)}, u32[]{:S(2)}, u32[]{:S(2)}) collective-permute-start(f32[6,32,128]{2,1,0:T(8,128)S(1)} %get-tuple-element.39.refs_1_), channel_id=1, source_target_pairs={{0,4},{4,0},{8,12},{12,8},{1,5},{5,1},{9,13},{13,9},{2,6},{6,2},{1... | collective-permute-start | bytes 294920 | tf_op jit(solution)/shard_map/ppermute | solution.py:510
  18.6 0.2 collective-permute-done.7.far
  18.8 0.2 shard_map.53
  19.0 0.4 %collective-permute-done.5.refs_2_ = f32[6,32,128]{2,1,0:T(8,128)S(1)} collective-permute-done((f32[6,32,128]{2,1,0:T(8,128)S(1)}, f32[6,32,128]{2,1,0:T(8,128)S(1)}, u32[]{:S(2)}, u32[]{:S(2)}) %collective-permute-start.5) | collective-permute-done | bytes 98336 | tf_op jit(solution)/shard_map/ppermute | solution.py:510
  19.4 0.2 collective-permute-done.6.refs_3_
  19.5 1.3 %shard_map.54 = (f32[12,32,128]{2,1,0:T(8,128)S(1)}, f32[12,32,128]{2,1,0:T(8,128)S(1)}, f32[12,32,128]{2,1,0:T(8,128)S(1)}) custom-call(bf16[256,256]{1,0:T(8,128)(2,1)S(1)} %get-tuple-element.33.blur_band, bf16[256,256]{1,0:T(8,128)(2,1)S(1)} %get-tuple-element.34.adjoint_band, bf16[256,256]{1,0:T(8,128)(2,1)S(1)} %get-tuple-element.35.turned_band, ...), custom_call_target="tpu_custom_call" | custom-call | tf_op jit(solution)/shard_map/pallas_call | solution.py:497
  20.8 0.4 %collective-permute-start.8 = (f32[12,32,128]{2,1,0:T(8,128)S(1)}, f32[12,32,128]{2,1,0:T(8,128)S(1)}, u32[]{:S(2)}, u32[]{:S(2)}) collective-permute-start(f32[12,32,128]{2,1,0:T(8,128)S(1)} %get-tuple-element.48), channel_id=1, source_target_pairs={{0,4},{4,0},{8,12},{12,8},{1,5},{5,1},{9,13},{13,9},{2,6},{6,2},{1... | collective-permute-start | bytes 589832 | tf_op jit(solution)/shard_map/ppermute | solution.py:510
  21.2 1.1 %collective-permute-done.8.other = f32[12,32,128]{2,1,0:T(8,128)S(1)} collective-permute-done((f32[12,32,128]{2,1,0:T(8,128)S(1)}, f32[12,32,128]{2,1,0:T(8,128)S(1)}, u32[]{:S(2)}, u32[]{:S(2)}) %collective-permute-start.8) | collective-permute-done | bytes 196640 | tf_op jit(solution)/shard_map/ppermute | solution.py:510
  22.4 1.2 %collective-permute-start.9 = (f32[12,16,128]{2,1,0:T(8,128)S(1)}, f32[12,16,128]{2,1,0:T(8,128)S(1)}, u32[]{:S(2)}, u32[]{:S(2)}) collective-permute-start(f32[12,16,128]{2,1,0:T(8,128)S(1)} %get-tuple-element.53), channel_id=1, source_target_pairs={{0,8},{4,12},{8,0},{12,4},{1,9},{5,13},{9,1},{13,5},{2,10},{6,14},... | collective-permute-start | bytes 294920 | tf_op jit(solution)/shard_map/ppermute | solution.py:510
  23.5 0.2 shard_map.56
  23.7 3.8 %collective-permute-done.9.received = f32[12,16,128]{2,1,0:T(8,128)S(1)} collective-permute-done((f32[12,16,128]{2,1,0:T(8,128)S(1)}, f32[12,16,128]{2,1,0:T(8,128)S(1)}, u32[]{:S(2)}, u32[]{:S(2)}) %collective-permute-start.9) | collective-permute-done | bytes 98336 | tf_op jit(solution)/shard_map/ppermute | solution.py:510
  27.5 0.7 %shard_map.57 = f32[1,8,48,32]{3,2,1,0:T(8,128)S(1)} custom-call(f32[12,16,128]{2,1,0:T(8,128)S(1)} %get-tuple-element.51.estimate, f32[12,16,128]{2,1,0:T(8,128)S(1)} %get-tuple-element.52.kept, f32[12,16,128]{2,1,0:T(8,128)S(1)} %collective-permute-done.9.received, f32[12,16,128]{2,1,0:T(8,128)S(1)} %get-tuple-element.54.refs_0_, ...), custom_call_target="tpu_custom_call" | custom-call | tf_op jit(solution)/shard_map/pallas_call | solution.py:497
  28.2 0.8 %copy.8 = f32[1,8,48,32]{2,3,1,0:T(8,128)} copy(f32[1,8,48,32]{3,2,1,0:T(8,128)S(1)} %shard_map.57) | data formatting | bytes 98304 | tf_op jit(solution)/shard_map/pallas_call | solution.py:497
  (4 shorter events, 0.1 us)
Async XLA Ops:
  0.0 1.1 %copy-start.1 = (s32[1,8,48,32]{2,3,1,0:T(8,128)S(1)}, s32[1,8,48,32]{2,3,1,0:T(8,128)}, u32[]{:S(2)}) copy-start(s32[1,8,48,32]{2,3,1,0:T(8,128)} %param.5) | copy-start | bytes 147460
  1.2 6.0 %copy-start.2 = (f32[1,32,9]{1,0,2:T(1,128)S(1)}, f32[1,32,9]{1,0,2:T(1,128)}, u32[]{:S(2)}) copy-start(f32[1,32,9]{1,0,2:T(1,128)} %param.6) | copy-start | bytes 3460
  1.5 11.5 %collective-permute-start.2 = (f32[24,8,128]{2,1,0:T(8,128)S(1)}, f32[24,8,128]{2,1,0:T(8,128)S(1)}, u32[]{:S(2)}, u32[]{:S(2)}) collective-permute-start(f32[24,8,128]{2,1,0:T(8,128)S(1)} %get-tuple-element.37.own_both), channel_id=1, source_target_pairs={{0,3},{1,2},{2,1},{3,0},{4,7},{5,6},{6,5},{7,4},{8,11},{9,10},{10,... | collective-permute-start | bytes 294920 | tf_op jit(solution)/shard_map/ppermute | solution.py:507
  6.6 0.7 %copy-start = (s32[1,32]{1,0:T(1,128)S(1)}, s32[1,32]{1,0:T(1,128)}, u32[]{:S(2)}) copy-start(s32[1,32]{1,0:T(1,128)} %offsets.1) | copy-start | bytes 388
  6.6 4.5 %collective-permute-start = (f32[12,8,128]{2,1,0:T(8,128)S(1)}, f32[12,8,128]{2,1,0:T(8,128)S(1)}, u32[]{:S(2)}, u32[]{:S(2)}) collective-permute-start(f32[12,8,128]{2,1,0:T(8,128)S(1)} %get-tuple-element.36.refs_0_), channel_id=1, source_target_pairs={{0,1},{1,0},{2,3},{3,2},{4,5},{5,4},{6,7},{7,6},{8,9},{9,8},{10,11... | collective-permute-start | bytes 147464 | tf_op jit(solution)/shard_map/ppermute | solution.py:507
  6.6 6.4 %collective-permute-start.1 = (f32[12,8,128]{2,1,0:T(8,128)S(1)}, f32[12,8,128]{2,1,0:T(8,128)S(1)}, u32[]{:S(2)}, u32[]{:S(2)}) collective-permute-start(f32[12,8,128]{2,1,0:T(8,128)S(1)} %get-tuple-element.36.refs_0_), channel_id=1, source_target_pairs={{0,2},{1,3},{2,0},{3,1},{4,6},{5,7},{6,4},{7,5},{8,10},{9,11},{10,... | collective-permute-start | bytes 147464 | tf_op jit(solution)/shard_map/ppermute | solution.py:507
  11.4 5.4 %collective-permute-start.3 = (f32[24,8,128]{2,1,0:T(8,128)S(1)}, f32[24,8,128]{2,1,0:T(8,128)S(1)}, u32[]{:S(2)}, u32[]{:S(2)}) collective-permute-start(f32[24,8,128]{2,1,0:T(8,128)S(1)} %shard_map.49.refs_0_), channel_id=1, source_target_pairs={{0,8},{4,12},{8,0},{12,4},{1,9},{5,13},{9,1},{13,5},{2,10},{6,14},... | collective-permute-start | bytes 294920 | tf_op jit(solution)/shard_map/ppermute | solution.py:510
  13.3 4.7 %collective-permute-start.4 = (f32[24,8,128]{2,1,0:T(8,128)S(1)}, f32[24,8,128]{2,1,0:T(8,128)S(1)}, u32[]{:S(2)}, u32[]{:S(2)}) collective-permute-start(f32[24,8,128]{2,1,0:T(8,128)S(1)} %shard_map.50.refs_1_), channel_id=1, source_target_pairs={{0,8},{4,12},{8,0},{12,4},{1,9},{5,13},{9,1},{13,5},{2,10},{6,14},... | collective-permute-start | bytes 294920 | tf_op jit(solution)/shard_map/ppermute | solution.py:510
  14.1 4.7 %collective-permute-start.7 = (f32[24,8,128]{2,1,0:T(8,128)S(1)}, f32[24,8,128]{2,1,0:T(8,128)S(1)}, u32[]{:S(2)}, u32[]{:S(2)}) collective-permute-start(f32[24,8,128]{2,1,0:T(8,128)S(1)} %shard_map.52.near), channel_id=1, source_target_pairs={{0,1},{1,0},{2,3},{3,2},{4,5},{5,4},{6,7},{7,6},{8,9},{9,8},{10,11... | collective-permute-start | bytes 294920 | tf_op jit(solution)/shard_map/ppermute | solution.py:507
  18.0 1.4 %collective-permute-start.5 = (f32[6,32,128]{2,1,0:T(8,128)S(1)}, f32[6,32,128]{2,1,0:T(8,128)S(1)}, u32[]{:S(2)}, u32[]{:S(2)}) collective-permute-start(f32[6,32,128]{2,1,0:T(8,128)S(1)} %get-tuple-element.38.refs_0_), channel_id=1, source_target_pairs={{0,4},{4,0},{8,12},{12,8},{1,5},{5,1},{9,13},{13,9},{2,6},{6,2},{1... | collective-permute-start | bytes 294920 | tf_op jit(solution)/shard_map/ppermute | solution.py:510
  18.1 1.4 %collective-permute-start.6 = (f32[6,32,128]{2,1,0:T(8,128)S(1)}, f32[6,32,128]{2,1,0:T(8,128)S(1)}, u32[]{:S(2)}, u32[]{:S(2)}) collective-permute-start(f32[6,32,128]{2,1,0:T(8,128)S(1)} %get-tuple-element.39.refs_1_), channel_id=1, source_target_pairs={{0,4},{4,0},{8,12},{12,8},{1,5},{5,1},{9,13},{13,9},{2,6},{6,2},{1... | collective-permute-start | bytes 294920 | tf_op jit(solution)/shard_map/ppermute | solution.py:510
  20.8 1.5 %collective-permute-start.8 = (f32[12,32,128]{2,1,0:T(8,128)S(1)}, f32[12,32,128]{2,1,0:T(8,128)S(1)}, u32[]{:S(2)}, u32[]{:S(2)}) collective-permute-start(f32[12,32,128]{2,1,0:T(8,128)S(1)} %get-tuple-element.48), channel_id=1, source_target_pairs={{0,4},{4,0},{8,12},{12,8},{1,5},{5,1},{9,13},{13,9},{2,6},{6,2},{1... | collective-permute-start | bytes 589832 | tf_op jit(solution)/shard_map/ppermute | solution.py:510
  22.4 5.1 %collective-permute-start.9 = (f32[12,16,128]{2,1,0:T(8,128)S(1)}, f32[12,16,128]{2,1,0:T(8,128)S(1)}, u32[]{:S(2)}, u32[]{:S(2)}) collective-permute-start(f32[12,16,128]{2,1,0:T(8,128)S(1)} %get-tuple-element.53), channel_id=1, source_target_pairs={{0,8},{4,12},{8,0},{12,4},{1,9},{5,13},{9,1},{13,5},{2,10},{6,14},... | collective-permute-start | bytes 294920 | tf_op jit(solution)/shard_map/ppermute | solution.py:510
